TPU v7x, 32 devices: a whole 2x2x4 slice. The times are simulated.
32 devices in a mesh: grp: 4 (over y, core), dev: 8 (over z, x).
Axes of the slice: x: 2, y: 2, z: 4, core: 2. Of those that a mesh axis runs over, the one named last changes fastest.
Arguments:
- video_in: bfloat16 [4, 32, 256, 1024], P(None, ('grp', 'dev')), may hold values from -24 to 24
- space_gain: float32 [1024], replicated, may hold values from 0.25 to 1.75
- space_project: bfloat16 [1024, 1536], replicated, may hold values from -6 to 6
- space_output: bfloat16 [512, 1024], replicated, may hold values from -0.25 to 0.25
- time_gain: float32 [1024], replicated, may hold values from 0.25 to 1.75
- time_project: bfloat16 [1024, 1536], replicated, may hold values from -6 to 6
- time_output: bfloat16 [512, 1024], replicated, may hold values from -0.25 to 0.25
Outputs:
- video_out: bfloat16 [4, 32, 256, 1024], P(None, ('grp', 'dev'))
All inputs are finite; a program needn't handle non-finite values.
Results may differ from a plain program's by a relative error of at most 0.007.
Values may be sent and summed in bfloat16 or wider, within the bound.
No kernel may reach another device: no remote copies, remote signals or barrier semaphores. Data moves between devices by JAX's collectives and lax.ppermute only.
A program may use at most 128 MiB of HBM per device.

v0:
```python
import jax
import jax.numpy as jnp
from jax import lax
from jax.sharding import PartitionSpec as P

HEADS = 8
HEAD_DIM = 64


norm_epsilon = 1e-06
masked_score = -1e30


def layer_norm(activations, gain_vec):
    floats = activations.astype(jnp.float32)
    centre = jnp.mean(floats, axis=-1, keepdims=True)
    spread = jnp.mean(jnp.square(floats - centre), axis=-1, keepdims=True)
    return ((floats - centre) * lax.rsqrt(spread + norm_epsilon) * gain_vec).astype(jnp.bfloat16)


def soft_weights(scores, allowed):
    scores = jnp.where(allowed, scores, masked_score)
    top_score = jnp.max(scores, axis=-1, keepdims=True)
    exponent = jnp.where(allowed, jnp.exp(scores - top_score), 0.0)
    row_total = jnp.sum(exponent, axis=-1, keepdims=True)
    return (exponent / row_total).astype(jnp.bfloat16)


def spatial_layer(frame_view, space_gain, space_project, space_output):
    clip_count, patch_count, model_width = frame_view.shape
    attn_width = HEADS * HEAD_DIM
    normed = layer_norm(frame_view, space_gain)
    projected = jnp.dot(
        normed.reshape(-1, model_width), space_project, preferred_element_type=jnp.float32
    )
    projected = projected.astype(jnp.bfloat16).reshape(clip_count, patch_count, 3, HEADS, HEAD_DIM)
    queries = projected[:, :, 0]
    keys_all = projected[:, :, 1]
    values_all = projected[:, :, 2]
    score_scale = HEAD_DIM ** (-0.5)
    scores = (
        jnp.einsum("cqhe,ckhe->chqk", queries, keys_all, preferred_element_type=jnp.float32)
        * score_scale
    )
    allowed = jnp.ones((patch_count, patch_count), jnp.bool_)
    weights = soft_weights(scores, allowed)
    context = jnp.einsum(
        "chqk,ckhe->cqhe", weights, values_all, preferred_element_type=jnp.float32
    ).astype(jnp.bfloat16)
    update = jnp.dot(
        context.reshape(-1, attn_width), space_output, preferred_element_type=jnp.float32
    )
    return (
        frame_view.astype(jnp.float32) + update.reshape(clip_count, patch_count, model_width)
    ).astype(jnp.bfloat16)


def to_frames(sending, group_count, member_count, patch_count):
    clip_count = sending.shape[0]
    lane_width = sending.shape[-1]
    patch_here = sending.shape[2]
    sectioned = sending.reshape(clip_count, group_count, member_count, 1, 1, patch_here, lane_width)
    arrived = lax.all_to_all(
        lax.all_to_all(sectioned, "grp", split_axis=1, concat_axis=3, tiled=True),
        "dev",
        split_axis=2,
        concat_axis=4,
        tiled=True,
    )
    return arrived.reshape(clip_count, patch_count, lane_width)


def per_device(
    video_in, space_gain, space_project, space_output, time_gain, time_project, time_output
):
    clip_count, frame_local, patch_count, model_width = video_in.shape
    attn_width = HEADS * HEAD_DIM
    group_count = lax.axis_size("grp")
    member_count = lax.axis_size("dev")
    frame_view = video_in.reshape(clip_count, patch_count, model_width)
    mixed_rows = spatial_layer(frame_view, space_gain, space_project, space_output)
    sectioned = mixed_rows.reshape(clip_count, 1, 1, patch_count, model_width)
    arrived = lax.all_to_all(
        lax.all_to_all(sectioned, "grp", split_axis=3, concat_axis=1, tiled=True),
        "dev",
        split_axis=3,
        concat_axis=2,
        tiled=True,
    )
    local_rows = arrived.reshape(
        clip_count,
        group_count * member_count,
        patch_count // (group_count * member_count),
        model_width,
    )
    frame_here = local_rows.shape[1]
    patch_here = local_rows.shape[2]
    normed = layer_norm(local_rows, time_gain)
    projected = jnp.dot(
        normed.reshape(-1, model_width), time_project, preferred_element_type=jnp.float32
    )
    projected = projected.astype(jnp.bfloat16).reshape(
        clip_count, frame_here, patch_here, 3, HEADS, HEAD_DIM
    )
    queries = projected[:, :, :, 0]
    keys_here = projected[:, :, :, 1]
    values_here = projected[:, :, :, 2]
    query_frames = jnp.arange(frame_here)
    key_frames = jnp.arange(keys_here.shape[1])
    allowed = key_frames[None, :] <= query_frames[:, None]
    score_scale = HEAD_DIM ** (-0.5)
    scores = (
        jnp.einsum("cqphe,ckphe->cphqk", queries, keys_here, preferred_element_type=jnp.float32)
        * score_scale
    )
    weights = soft_weights(scores, allowed)
    context = jnp.einsum(
        "cphqk,ckphe->cqphe", weights, values_here, preferred_element_type=jnp.float32
    )
    context = context.astype(jnp.bfloat16).reshape(clip_count, frame_here, patch_here, attn_width)
    update = jnp.dot(
        context.reshape(-1, attn_width), time_output, preferred_element_type=jnp.float32
    )
    update_here = update.astype(jnp.bfloat16).reshape(
        clip_count, frame_here, patch_here, model_width
    )
    update_rows = to_frames(update_here, group_count, member_count, patch_count)
    result = (mixed_rows.astype(jnp.float32) + update_rows.astype(jnp.float32)).astype(jnp.bfloat16)
    return result.reshape(clip_count, frame_local, patch_count, model_width)


def solution(mesh):
    in_specs = (P(None, ("grp", "dev"), None, None), P(), P(), P(), P(), P(), P())
    out_specs = P(None, ("grp", "dev"), None, None)
    return jax.shard_map(
        per_device, mesh=mesh, in_specs=in_specs, out_specs=out_specs, check_vma=False
    )
```

profile of v0, /device:TPU:0, one launch (start us, length us, event | category | flops | bytes accessed | tf_op | source)
XLA Modules:
  0.0 249.0 jit_solution(893999209645210632)
XLA Ops:
  0.0 2.1 convert_reduce_fusion
  2.1 2.4 fusion.12
  5.3 4.9 %convolution_convert_fusion.1 = bf16[1024,1536]{1,0:T(8,128)(2,1)} fusion(bf16[1024,1024]{1,0:T(8,128)(2,1)S(1)} %fusion.10, bf16[1024,1536]{1,0:T(8,128)(2,1)S(1)} %copy-done), kind=kOutput, calls=%fused_computation.29 | convolution fusion | flops 3222798336 | bytes 8388608 | tf_op jit(solution)/shard_map/dot_general | solution.py:33
  10.2 8.9 %reshape.130 = bf16[4,256,3,8,64]{4,3,2,1,0:T(8,128)(2,1)} reshape(bf16[1024,1536]{1,0:T(8,128)(2,1)} %convolution_convert_fusion.1) | data formatting | bytes 6291456 | tf_op jit(solution)/shard_map/reshape | solution.py:36
  19.0 5.3 %fusion.36 = (bf16[4,256,1,8,64]{4,3,2,1,0:T(8,128)(2,1)}, bf16[4,256,1,8,64]{4,3,2,1,0:T(8,128)(2,1)}, bf16[4,256,1,8,64]{4,3,2,1,0:T(8,128)(2,1)S(1)}) fusion(bf16[4,256,3,8,64]{4,3,2,1,0:T(8,128)(2,1)} %reshape.130), kind=kLoop, calls=%fused_computation.61 | loop fusion | bytes 6291456 | tf_op jit(solution)/shard_map/slice | solution.py:39
  24.3 3.0 %copy.74 = bf16[4,256,1,8,64]{1,4,3,0,2:T(8,128)(2,1)} copy(bf16[4,256,1,8,64]{4,3,2,1,0:T(8,128)(2,1)} %get-tuple-element.8) | data formatting | bytes 2097152
  27.3 2.2 copy.75
  29.6 1.9 copy.76
  31.5 2.5 %fusion.27 = f32[4,8,256,256]{2,3,1,0:T(8,128)S(1)} fusion(bf16[4,256,1,8,64]{1,4,3,0,2:T(8,128)(2,1)} %copy.76, bf16[4,256,1,8,64]{1,4,3,0,2:T(8,128)(2,1)S(1)} %copy.75), kind=kOutput, calls=%fused_computation.47 | convolution fusion | flops 268435456 | bytes 10485760 | tf_op jit(solution)/shard_map/cqhe,ckhe->chqk/dot_general | solution.py:42
  34.0 6.3 %fusion.37 = (f32[4,8,256]{2,1,0:T(8,128)S(1)}, f32[4,8,256,256]{2,3,1,0:T(8,128)S(1)}) fusion(f32[4,8,256,256]{2,3,1,0:T(8,128)S(1)} %fusion.27), kind=kOutput, calls=%fused_computation.62 | output fusion | flops 8388863 | bytes 16809984 | tf_op jit(solution)/shard_map/sub | solution.py:24
  42.2 1.3 fusion.13
  43.5 1.6 copy.57
  45.1 29.7 %all_to_all.48 = bf16[4,1,1,256,1024]{4,0,2,1,3:T(4,128)(2,1)S(1)} all-to-all(bf16[4,1,1,256,1024]{4,0,2,1,3:T(4,128)(2,1)S(1)} %copy.57), channel_id=1, replica_groups=mesh['grp'=4,'dev'=8] {'grp'}, dimensions={3} | all-to-all | bytes 4194304 | tf_op jit(solution)/shard_map/all_to_all | solution.py:84
  74.9 4.0 %copy.58 = bf16[4,4,1,64,1024]{4,1,0,2,3:T(4,128)(2,1)} copy(bf16[4,4,1,64,1024]{4,0,3,1,2:T(4,128)(2,1)S(1)} %bitcast.92) | data formatting | bytes 4194304 | tf_op jit(solution)/shard_map/all_to_all | solution.py:84
  78.9 5.8 %all-to-all-start.1 = ((bf16[4,4,1,64,1024]{4,1,0,2,3:T(4,128)(2,1)}), bf16[4,4,1,64,1024]{4,1,0,2,3:T(4,128)(2,1)S(1)}, u32[]{:S(2)}, u32[]{:S(2)}) async-start(bf16[4,4,1,64,1024]{4,1,0,2,3:T(4,128)(2,1)} %copy.58), calls=%async_computation.1 | async-start | bytes 4194304 | tf_op jit(solution)/shard_map/all_to_all | solution.py:83
  84.7 47.9 %all-to-all-done.1 = bf16[4,4,1,64,1024]{4,1,0,2,3:T(4,128)(2,1)S(1)} async-done(((bf16[4,4,1,64,1024]{4,1,0,2,3:T(4,128)(2,1)}), bf16[4,4,1,64,1024]{4,1,0,2,3:T(4,128)(2,1)S(1)}, u32[]{:S(2)}, u32[]{:S(2)}) %all-to-all-start.1) | async-done | bytes 2097184 | tf_op jit(solution)/shard_map/all_to_all | solution.py:83
  132.6 1.9 fusion.24
  134.6 2.3 multiply_reduce_fusion.1
  136.9 1.2 copy_convert_fusion
  138.7 1.3 copy-done.9
  140.0 3.6 %convolution_convert_fusion = bf16[1024,1536]{1,0:T(8,128)(2,1)S(1)} fusion(bf16[1024,1024]{1,0:T(8,128)(2,1)S(1)} %fusion.7, bf16[1024,1536]{1,0:T(8,128)(2,1)S(1)} %copy-done.9), kind=kOutput, calls=%fused_computation.28 | convolution fusion | flops 3222798336 | bytes 8388608 | tf_op jit(solution)/shard_map/dot_general | solution.py:99
  143.7 5.9 %reshape.123 = bf16[4,32,8,3,8,64]{5,4,3,2,1,0:T(8,128)(2,1)} reshape(bf16[1024,1536]{1,0:T(8,128)(2,1)S(1)} %convolution_convert_fusion) | data formatting | bytes 6291456 | tf_op jit(solution)/shard_map/reshape | solution.py:102
  149.6 4.4 %fusion.35 = (bf16[4,32,8,1,8,64]{5,4,3,2,1,0:T(8,128)(2,1)S(1)}, bf16[4,32,8,1,8,64]{5,4,3,2,1,0:T(8,128)(2,1)S(1)}, bf16[4,32,8,1,8,64]{5,4,3,2,1,0:T(8,128)(2,1)S(1)}) fusion(bf16[4,32,8,3,8,64]{5,4,3,2,1,0:T(8,128)(2,1)} %reshape.123), kind=kLoop, calls=%fused_computation.60 | loop fusion | bytes 6291456 | tf_op jit(solution)/shard_map/slice | solution.py:107
  153.9 2.7 %fusion.19 = f32[4,8,8,32,32]{3,4,2,1,0:T(8,128)S(1)} fusion(bf16[4,32,8,1,8,64]{5,4,3,2,1,0:T(8,128)(2,1)S(1)} %get-tuple-element.7, bf16[4,32,8,1,8,64]{5,4,3,2,1,0:T(8,128)(2,1)S(1)} %get-tuple-element.6), kind=kOutput, calls=%fused_computation.34 | convolution fusion | flops 33554432 | bytes 3145728 | tf_op jit(solution)/shard_map/cqphe,ckphe->cphqk/dot_general | solution.py:113
  156.7 1.7 fusion.38
  158.3 1.9 convert_bitcast_fusion.1
  161.1 1.3 reshape_reshape.6
  162.4 2.5 convolution_convert_fusion.2
  165.0 28.2 %all_to_all.49 = bf16[4,4,8,1,1,8,1024]{6,5,2,0,4,3,1:T(8,128)(2,1)S(1)} all-to-all(bf16[4,4,8,1,1,8,1024]{6,5,2,0,4,3,1:T(8,128)(2,1)S(1)} %copy.65), channel_id=1, replica_groups=mesh['grp'=4,'dev'=8] {'grp'}, dimensions={1} | all-to-all | bytes 4194304 | tf_op jit(solution)/shard_map/all_to_all | solution.py:64
  193.4 51.4 %all_to_all.50 = bf16[4,1,8,4,1,8,1024]{6,5,3,0,4,1,2:T(8,128)(2,1)S(1)} all-to-all(bf16[4,1,8,4,1,8,1024]{6,5,3,0,4,1,2:T(8,128)(2,1)S(1)} %copy.66), channel_id=1, replica_groups=mesh['grp'=4,'dev'=8] {'dev'}, dimensions={2} | all-to-all | bytes 4194304 | tf_op jit(solution)/shard_map/all_to_all | solution.py:63
  245.6 1.3 copy-done.5
  246.8 2.2 fusion.18
  (37 shorter events, 5.3 us)
Async XLA Ops:
  0.0 5.2 %copy-start = (bf16[1024,1536]{1,0:T(8,128)(2,1)S(1)}, bf16[1024,1536]{1,0:T(8,128)(2,1)}, u32[]{:S(2)}) copy-start(bf16[1024,1536]{1,0:T(8,128)(2,1)} %param.9) | copy-start | bytes 9437188
  0.0 4.5 %copy-start.2 = (bf16[4,1,256,1024]{3,2,1,0:T(8,128)(2,1)S(1)}, bf16[4,1,256,1024]{3,2,1,0:T(8,128)(2,1)}, u32[]{:S(2)}) copy-start(bf16[4,1,256,1024]{3,2,1,0:T(8,128)(2,1)} %param.7) | copy-start | bytes 6291460
  0.0 4.5 %copy-start.7 = (f32[1024]{0:T(1024)S(1)}, f32[1024]{0:T(1024)}, u32[]{:S(2)}) copy-start(f32[1024]{0:T(1024)} %param.8) | copy-start | bytes 12292
  34.0 6.3 %copy-start.6 = (bf16[4,256,1,8,64]{1,4,3,0,2:T(8,128)(2,1)S(1)}, bf16[4,256,1,8,64]{1,4,3,0,2:T(8,128)(2,1)}, u32[]{:S(2)}) copy-start(bf16[4,256,1,8,64]{1,4,3,0,2:T(8,128)(2,1)} %copy.74) | copy-start | bytes 3145732
  40.3 1.6 copy-start.3
  40.4 1.8 copy-start.10
  43.5 31.4 %copy-start.4 = (bf16[4,256,1024]{2,1,0:T(8,128)(2,1)}, bf16[4,256,1024]{2,1,0:T(8,128)(2,1)S(1)}, u32[]{:S(2)}) copy-start(bf16[4,256,1024]{2,1,0:T(8,128)(2,1)S(1)} %fusion.13) | copy-start | bytes 6291460
  78.9 53.7 %all-to-all-start.1 = ((bf16[4,4,1,64,1024]{4,1,0,2,3:T(4,128)(2,1)}), bf16[4,4,1,64,1024]{4,1,0,2,3:T(4,128)(2,1)S(1)}, u32[]{:S(2)}, u32[]{:S(2)}) async-start(bf16[4,4,1,64,1024]{4,1,0,2,3:T(4,128)(2,1)} %copy.58), calls=%async_computation.1 | async-start | bytes 4194304 | tf_op jit(solution)/shard_map/all_to_all | solution.py:83
  134.6 3.6 %copy-start.8 = (f32[1024]{0:T(1024)S(1)}, f32[1024]{0:T(1024)}, u32[]{:S(2)}) copy-start(f32[1024]{0:T(1024)} %param.11) | copy-start | bytes 12292
  138.2 1.9 copy-start.9
  245.2 1.6 copy-start.5
  245.6 3.4 %copy-start.1 = (bf16[1024,1536]{1,0:T(8,128)(2,1)S(1)}, bf16[1024,1536]{1,0:T(8,128)(2,1)}, u32[]{:S(2)}) copy-start(bf16[1024,1536]{1,0:T(8,128)(2,1)} %param.9) | copy-start | bytes 9437188
where the time goes:
time: 250 us; the launch traced here: 249 us
  blocking collectives  109 us (44%)
  waiting for transfers between devices  47.9 us (19%)
  local copies, waits for them, and re-layouts  43.6 us (17%)
  other arithmetic  21.8 us (9%)
  matrix products  20.4 us (8%)
  starting transfers between devices  5.81 us (2%)
    all_to_all x1, blocking collectives, to_frames(): lax.all_to_all(lax.all_to_all(sectioned, 'grp', split_axis=1, concat_axis...  51.4 us
    all_to_all x1, waiting for transfers between devices, per_device(): lax.all_to_all(lax.all_to_all(sectioned, 'grp', split_axis=3, concat_axis...  47.9 us
    all_to_all x1, blocking collectives, per_device(): lax.all_to_all(sectioned, 'grp', split_axis=3, concat_axis=1, tiled=True)  29.7 us
    all_to_all x1, blocking collectives, to_frames(): lax.all_to_all(sectioned, 'grp', split_axis=1, concat_axis=3, tiled=True)  28.2 us
    unnamed x27, local copies, waits for them, and re-layouts  10.7 us
    reshape x1, local copies, waits for them, and re-layouts, spatial_layer(): projected.astype(jnp.bfloat16)  8.86 us
    sub x2, other arithmetic, soft_weights(): exponent = jnp.where(allowed, jnp.exp(scores - top_score), 0.0)  7.97 us
    reshape x1, local copies, waits for them, and re-layouts, per_device(): projected.astype(jnp.bfloat16)  5.89 us
  transfers between devices with their start and end apart: 1, of which 1 were waited for; matrix products, arithmetic and copies ran while one was open for 0% of the time, Pallas kernels for 0%

commit v1 on v0

v1 whole, which is shorter than its diff:
```python
from functools import partial

import jax
import jax.numpy as jnp
from jax import lax
from jax.experimental import pallas as pl
from jax.experimental.pallas import tpu as pltpu
from jax.sharding import PartitionSpec as P

HEADS = 8
HEAD_DIM = 64
WIDTH = HEADS * HEAD_DIM
LANES = 128
EPSILON = 1e-06
MASKED = -1e30
AXES = ("grp", "dev")
CHUNKS = (2, 2)
VMEM_LIMIT = 40 * 1024 * 1024


def normed(floats, gain):
    centred = floats - jnp.mean(floats, axis=-1, keepdims=True)
    spread = jnp.mean(jnp.square(centred), axis=-1, keepdims=True)
    return centred * lax.rsqrt(spread + EPSILON) * gain


def attend(heads, bias):
    rows = heads.shape[0]
    low = lax.broadcasted_iota(jnp.int32, (rows, LANES), 1) < HEAD_DIM
    ones = jnp.ones((rows, LANES), jnp.bfloat16)
    contexts = []
    for pair in range(WIDTH // LANES):
        at = pair * LANES
        queries = heads[:, at : at + LANES] * jnp.bfloat16(HEAD_DIM**-0.5)
        keys = heads[:, WIDTH + at : WIDTH + at + LANES]
        values = heads[:, 2 * WIDTH + at : 2 * WIDTH + at + LANES]
        nothing = jnp.zeros_like(queries)
        stacked = jnp.concatenate([jnp.where(low, queries, nothing), jnp.where(low, nothing, queries)], axis=0)
        scores = lax.dot_general(stacked, keys, (((1,), (1,)), ((), ())), preferred_element_type=jnp.float32)
        if bias is not None:
            scores = scores + jnp.concatenate([bias, bias], axis=0)
        weights = jnp.exp(scores - jnp.max(scores, axis=-1, keepdims=True)).astype(jnp.bfloat16)
        sums = jnp.dot(weights, jnp.concatenate([values, ones], axis=1), preferred_element_type=jnp.float32)
        context = sums[:, :LANES] / sums[:, LANES:]
        contexts.append(jnp.where(low, context[:rows], context[rows:]))
    return jnp.concatenate(contexts, axis=1).astype(jnp.bfloat16)


def space_kernel(video_ref, gain_ref, project_ref, output_ref, time_gain_ref, mixed_ref, sent_ref):
    floats = video_ref[0].astype(jnp.float32)
    heads = jnp.dot(
        normed(floats, gain_ref[...]).astype(jnp.bfloat16), project_ref[...], preferred_element_type=jnp.float32
    ).astype(jnp.bfloat16)
    context = attend(heads, None)
    mixed = (floats + jnp.dot(context, output_ref[...], preferred_element_type=jnp.float32)).astype(jnp.bfloat16)
    mixed_ref[0] = mixed
    sent = normed(mixed.astype(jnp.float32), time_gain_ref[...])
    sent_ref[...] = sent.reshape(sent_ref.shape).astype(jnp.bfloat16)


def time_kernel(patch_here, rows_ref, project_ref, context_ref, bias_ref):
    rows, width = bias_ref.shape[0], rows_ref.shape[-1]

    @pl.when(pl.program_id(0) == 0)
    def _():
        query = lax.broadcasted_iota(jnp.int32, (rows, rows), 0)
        key = lax.broadcasted_iota(jnp.int32, (rows, rows), 1)
        seen = (key <= query) & (lax.rem(query, patch_here) == lax.rem(key, patch_here))
        bias_ref[...] = jnp.where(seen, 0.0, MASKED)

    arrived = rows_ref[...].astype(jnp.float32).reshape(rows, width).astype(jnp.bfloat16)
    heads = jnp.dot(arrived, project_ref[...], preferred_element_type=jnp.float32).astype(jnp.bfloat16)
    context = attend(heads, bias_ref[...])
    context_ref[...] = context.astype(jnp.float32).reshape(context_ref.shape).astype(jnp.bfloat16)


def final_kernel(mixed_ref, context_ref, output_ref, out_ref):
    rows = mixed_ref.shape[1]
    context = context_ref[...].astype(jnp.float32).reshape(rows, WIDTH).astype(jnp.bfloat16)
    update = jnp.dot(context, output_ref[...], preferred_element_type=jnp.float32)
    out_ref[0] = (mixed_ref[0].astype(jnp.float32) + update).astype(jnp.bfloat16)


def whole(shape):
    return pl.BlockSpec(shape, lambda c: (0,) * len(shape))


def exchange_spec(count, patch_here, width):
    if patch_here % 8:
        return pl.BlockSpec((1, count * patch_here, width), lambda c: (c, 0, 0))
    return pl.BlockSpec((count, 1, patch_here, width), lambda c: (0, c, 0, 0))


def exchange_shape(count, clips, patch_here, width):
    if patch_here % 8:
        return jax.ShapeDtypeStruct((clips, count * patch_here, width), jnp.bfloat16)
    return jax.ShapeDtypeStruct((count, clips, patch_here, width), jnp.bfloat16)


def exchange(sent, count, patch_here):
    plain = sent.ndim == 3
    if plain:
        clips, _, width = sent.shape
        sent = sent.reshape(clips, count, patch_here, width).transpose(1, 0, 2, 3)
    arrived = lax.all_to_all(sent, AXES, split_axis=0, concat_axis=0, tiled=True)
    if plain:
        arrived = arrived.transpose(1, 0, 2, 3).reshape(clips, count * patch_here, width)
    return arrived


def cost(macs, bytes_accessed, exps):
    return pl.CostEstimate(flops=2 * macs, bytes_accessed=bytes_accessed, transcendentals=exps)


def space_call(video, first, clips, space_gain, space_project, space_output, time_gain, count):
    rows, width = video.shape[1:]
    patch_here = rows // count
    return pl.pallas_call(
        space_kernel,
        grid=(clips,),
        in_specs=[
            pl.BlockSpec((1, rows, width), lambda c: (first + c, 0, 0)),
            whole((1, width)),
            whole((width, 3 * WIDTH)),
            whole((WIDTH, width)),
            whole((1, width)),
        ],
        out_specs=[
            pl.BlockSpec((1, rows, width), lambda c: (c, 0, 0)),
            exchange_spec(count, patch_here, width),
        ],
        out_shape=[
            jax.ShapeDtypeStruct((clips, rows, width), jnp.bfloat16),
            exchange_shape(count, clips, patch_here, width),
        ],
        cost_estimate=cost(
            clips * rows * (width * 4 * WIDTH + 8 * rows * WIDTH), 2 * (4 * width * WIDTH + 3 * clips * rows * width),
            clips * HEADS * rows * rows,
        ),
        compiler_params=pltpu.CompilerParams(vmem_limit_bytes=VMEM_LIMIT),
        name="space",
    )(video, space_gain, space_project, space_output, time_gain)


def time_call(arrived, clips, rows, time_project, count):
    width = arrived.shape[-1]
    patch_here = rows // count
    return pl.pallas_call(
        partial(time_kernel, patch_here),
        grid=(clips,),
        in_specs=[exchange_spec(count, patch_here, width), whole((width, 3 * WIDTH))],
        out_specs=exchange_spec(count, patch_here, WIDTH),
        out_shape=exchange_shape(count, clips, patch_here, WIDTH),
        scratch_shapes=[pltpu.VMEM((rows, rows), jnp.float32)],
        cost_estimate=cost(
            clips * rows * (width * 3 * WIDTH + 8 * rows * WIDTH), 2 * (3 * width * WIDTH + 2 * clips * rows * width),
            clips * HEADS * rows * rows,
        ),
        compiler_params=pltpu.CompilerParams(vmem_limit_bytes=VMEM_LIMIT),
        name="time",
    )(arrived, time_project)


def final_call(mixed, context, time_output, count):
    clips, rows, width = mixed.shape
    return pl.pallas_call(
        final_kernel,
        grid=(clips,),
        in_specs=[
            pl.BlockSpec((1, rows, width), lambda c: (c, 0, 0)),
            exchange_spec(count, rows // count, WIDTH),
            whole((WIDTH, width)),
        ],
        out_specs=pl.BlockSpec((1, rows, width), lambda c: (c, 0, 0)),
        out_shape=jax.ShapeDtypeStruct((clips, rows, width), jnp.bfloat16),
        cost_estimate=cost(clips * rows * width * WIDTH, 2 * (width * WIDTH + 3 * clips * rows * width), 0),
        compiler_params=pltpu.CompilerParams(vmem_limit_bytes=VMEM_LIMIT),
        name="final",
    )(mixed, context, time_output)


def per_device(video_in, space_gain, space_project, space_output, time_gain, time_project, time_output):
    clip_count, frame_local, patch_count, width = video_in.shape
    count = lax.axis_size("grp") * lax.axis_size("dev")
    patch_here = patch_count // count
    video = video_in.reshape(clip_count, patch_count, width)
    gains = space_gain.reshape(1, width), time_gain.reshape(1, width)
    mixed, arrived, returned = [], [], []
    first = 0
    for clips in CHUNKS:
        here, sent = space_call(video, first, clips, gains[0], space_project, space_output, gains[1], count)
        mixed.append(here)
        arrived.append(exchange(sent, count, patch_here))
        first += clips
    for clips, rows in zip(CHUNKS, arrived):
        context = time_call(rows, clips, patch_count, time_project, count)
        returned.append(exchange(context, count, patch_here))
    done = [final_call(here, context, time_output, count) for here, context in zip(mixed, returned)]
    return jnp.concatenate(done, axis=0).reshape(clip_count, frame_local, patch_count, width)


def solution(mesh):
    in_specs = (P(None, AXES, None, None), P(), P(), P(), P(), P(), P())
    return jax.shard_map(
        per_device, mesh=mesh, in_specs=in_specs, out_specs=P(None, AXES, None, None), check_vma=False
    )
```

time: 250 us -> 120 us (0.48)
  blocking collectives: 109 us -> 0 us
  local copies, waits for them, and re-layouts: 43.6 us -> 17.4 us
  Pallas kernels: 0 us -> 22.3 us
  matrix products: 20.4 us -> 0 us
  other arithmetic: 21.8 us -> 1.5 us
  waiting for transfers between devices: 47.9 us -> 63.2 us
  starting transfers between devices: 5.81 us -> 15.2 us
    all_to_all x3 -> x0, blocking collectives: 109 us -> none  [the longest x1 51.4 us: to_frames(): lax.all_to_all(lax.all_to_all(sectioned, 'grp', split_axis=1, concat_axis...]
    pallas_call x0 -> x6, Pallas kernels: none -> 22.3 us  [the longest x2 11.7 us: space_call(): pl.pallas_call(space_kernel, grid=(clips,), in_specs=[pl.BlockSpec((1, ro...]
    dot_general x8 -> x0, matrix products: 20.4 us -> none  [the longest x1 4.9 us: spatial_layer(): jnp.dot(normed.reshape(-1, model_width), space_project, preferred_element...]
    reshape x3 -> x0, local copies, waits for them, and re-layouts: 16.4 us -> none  [the longest x1 8.86 us: spatial_layer(): projected.astype(jnp.bfloat16)]
    all_to_all x1 -> x4, waiting for transfers between devices: 47.9 us -> 63.2 us  [exchange(): lax.all_to_all(sent, AXES, split_axis=0, concat_axis=0, tiled=True)]
    slice x2 -> x0, local copies, waits for them, and re-layouts: 9.65 us -> none  [the longest x1 5.3 us: spatial_layer(): values_all = projected[:, :, 2]]
    all_to_all x1 -> x4, starting transfers between devices: 5.81 us -> 15.2 us  [exchange(): lax.all_to_all(sent, AXES, split_axis=0, concat_axis=0, tiled=True)]
    reduce_sum x4 -> x0, other arithmetic: 8.64 us -> none  [the longest x2 4.66 us: layer_norm(): spread = jnp.mean(jnp.square(floats - centre), axis=-1, keepdims=True)]
  transfers between devices with their start and end apart: 1 -> 4, of which waited for: 1 -> 4; matrix products, arithmetic and copies ran while one was open for 0% -> 0% of each run, Pallas kernels for 0% -> 13%
where the time goes in v1:
time: 120 us
  waiting for transfers between devices  63.2 us (53%)
  Pallas kernels  22.3 us (19%)
  local copies, waits for them, and re-layouts  17.4 us (14%)
  starting transfers between devices  15.2 us (13%)
  other arithmetic  1.5 us (1%)
    all_to_all x4, waiting for transfers between devices, exchange(): lax.all_to_all(sent, AXES, split_axis=0, concat_axis=0, tiled=True)  63.2 us
    unnamed x34, local copies, waits for them, and re-layouts  17.4 us
    all_to_all x4, starting transfers between devices, exchange(): lax.all_to_all(sent, AXES, split_axis=0, concat_axis=0, tiled=True)  15.2 us
    pallas_call x2, Pallas kernels, space_call(): pl.pallas_call(space_kernel, grid=(clips,), in_specs=[pl.BlockSpec((1, ro...  11.7 us
    pallas_call x2, Pallas kernels, time_call(): pl.pallas_call(partial(time_kernel, patch_here), grid=(clips,), in_specs=...  8.68 us
  transfers between devices with their start and end apart: 4, of which 4 were waited for; matrix products, arithmetic and copies ran while one was open for 0% of the time, Pallas kernels for 13%

profile of v1, /device:TPU:0, one launch (start us, length us, event | category | flops | bytes accessed | tf_op | source)
XLA Modules:
  0.0 119.7 jit_solution(1164382998948701352)
XLA Ops:
  0.0 1.9 %copy-done.5 = bf16[1024,1536]{1,0:T(8,128)(2,1)S(1)} copy-done((bf16[1024,1536]{1,0:T(8,128)(2,1)S(1)}, bf16[1024,1536]{1,0:T(8,128)(2,1)}, u32[]{:S(2)}) %copy-start.5) | copy-done | bytes 3145752
  1.9 1.6 %copy-done.9 = bf16[4,1,256,1024]{3,2,1,0:T(8,128)(2,1)S(1)} copy-done((bf16[4,1,256,1024]{3,2,1,0:T(8,128)(2,1)S(1)}, bf16[4,1,256,1024]{3,2,1,0:T(8,128)(2,1)}, u32[]{:S(2)}) %copy-start.9) | copy-done | bytes 2097176
  3.5 1.2 %copy-done.11 = bf16[512,1024]{1,0:T(8,128)(2,1)S(1)} copy-done((bf16[512,1024]{1,0:T(8,128)(2,1)S(1)}, bf16[512,1024]{1,0:T(8,128)(2,1)}, u32[]{:S(2)}) %copy-start.11) | copy-done | bytes 1048600
  4.7 0.7 copy-done.13
  5.4 0.7 copy-done.15
  6.1 5.8 %space.3 = (bf16[2,256,1024]{2,1,0:T(8,128)(2,1)S(1)}, bf16[32,2,8,1024]{3,2,1,0:T(8,128)(2,1)}) custom-call(bf16[4,256,1024]{2,1,0:T(8,128)(2,1)S(1)} %bitcast.7, f32[1,1024]{1,0:T(1,128)S(1)} %bitcast.9, bf16[1024,1536]{1,0:T(8,128)(2,1)S(1)} %copy-done.5, bf16[512,1024]{1,0:T(8,128)(2,1)S(1)} %copy-done.11, f32[1,1024]{1,0:T(1,128)S(1)} %bitcast.11), custom_call_target="tpu_custom_call" | custom-call | flops 3221225472 | bytes 7340032 | tf_op jit(solution)/shard_map/space/pallas_call | solution.py:118
  11.9 1.0 copy-done.3
  12.9 7.3 %all-to-all-start.2 = ((bf16[32,2,8,1024]{3,2,1,0:T(8,128)(2,1)}), bf16[32,2,8,1024]{3,2,1,0:T(8,128)(2,1)S(1)}, u32[]{:S(2)}, u32[]{:S(2)}) async-start(bf16[32,2,8,1024]{3,2,1,0:T(8,128)(2,1)} %get-tuple-element.12), calls=%async_computation.2 | async-start | bytes 2097152 | tf_op jit(solution)/shard_map/all_to_all | solution.py:105
  20.3 0.0 copy-done.14
  20.3 0.0 copy-start.6
  20.3 1.9 %copy-done.6 = bf16[1024,1536]{1,0:T(8,128)(2,1)S(1)} copy-done((bf16[1024,1536]{1,0:T(8,128)(2,1)S(1)}, bf16[1024,1536]{1,0:T(8,128)(2,1)}, u32[]{:S(2)}) %copy-start.6) | copy-done | bytes 3145752
  22.2 1.2 %copy-done.12 = bf16[512,1024]{1,0:T(8,128)(2,1)S(1)} copy-done((bf16[512,1024]{1,0:T(8,128)(2,1)S(1)}, bf16[512,1024]{1,0:T(8,128)(2,1)}, u32[]{:S(2)}) %copy-start.12) | copy-done | bytes 1048600
  23.4 5.9 %space.2 = (bf16[2,256,1024]{2,1,0:T(8,128)(2,1)S(1)}, bf16[32,2,8,1024]{3,2,1,0:T(8,128)(2,1)}) custom-call(bf16[4,256,1024]{2,1,0:T(8,128)(2,1)S(1)} %bitcast.8, f32[1,1024]{1,0:T(1,128)S(1)} %bitcast.10, bf16[1024,1536]{1,0:T(8,128)(2,1)S(1)} %copy-done.6, bf16[512,1024]{1,0:T(8,128)(2,1)S(1)} %copy-done.12, f32[1,1024]{1,0:T(1,128)S(1)} %bitcast.12), custom_call_target="tpu_custom_call" | custom-call | flops 3221225472 | bytes 7340032 | tf_op jit(solution)/shard_map/space/pallas_call | solution.py:118
  29.3 1.0 copy-done.1
  30.2 17.6 %all-to-all-done.2.rows_ref = bf16[32,2,8,1024]{3,2,1,0:T(8,128)(2,1)S(1)} async-done(((bf16[32,2,8,1024]{3,2,1,0:T(8,128)(2,1)}), bf16[32,2,8,1024]{3,2,1,0:T(8,128)(2,1)S(1)}, u32[]{:S(2)}, u32[]{:S(2)}) %all-to-all-start.2) | async-done | bytes 1048608 | tf_op jit(solution)/shard_map/all_to_all | solution.py:105
  47.8 2.6 %all-to-all-start = ((bf16[32,2,8,1024]{3,2,1,0:T(8,128)(2,1)}), bf16[32,2,8,1024]{3,2,1,0:T(8,128)(2,1)S(1)}, u32[]{:S(2)}, u32[]{:S(2)}) async-start(bf16[32,2,8,1024]{3,2,1,0:T(8,128)(2,1)} %get-tuple-element.10), calls=%async_computation | async-start | bytes 2097152 | tf_op jit(solution)/shard_map/all_to_all | solution.py:105
  50.5 0.0 copy-start.7
  50.5 1.9 %copy-done.7 = bf16[1024,1536]{1,0:T(8,128)(2,1)S(1)} copy-done((bf16[1024,1536]{1,0:T(8,128)(2,1)S(1)}, bf16[1024,1536]{1,0:T(8,128)(2,1)}, u32[]{:S(2)}) %copy-start.7) | copy-done | bytes 3145752
  52.4 4.3 %time.3 = bf16[32,2,8,512]{3,2,1,0:T(8,128)(2,1)} custom-call(bf16[32,2,8,1024]{3,2,1,0:T(8,128)(2,1)S(1)} %all-to-all-done.2.rows_ref, bf16[1024,1536]{1,0:T(8,128)(2,1)S(1)} %copy-done.7), custom_call_target="tpu_custom_call" | custom-call | flops 2684354560 | bytes 5242880 | tf_op jit(solution)/shard_map/time/pallas_call | solution.py:148
  56.7 21.4 %all-to-all-done.rows_ref = bf16[32,2,8,1024]{3,2,1,0:T(8,128)(2,1)S(1)} async-done(((bf16[32,2,8,1024]{3,2,1,0:T(8,128)(2,1)}), bf16[32,2,8,1024]{3,2,1,0:T(8,128)(2,1)S(1)}, u32[]{:S(2)}, u32[]{:S(2)}) %all-to-all-start) | async-done | bytes 1048608 | tf_op jit(solution)/shard_map/all_to_all | solution.py:105
  78.1 2.6 %all-to-all-start.3 = ((bf16[32,2,8,512]{3,2,1,0:T(8,128)(2,1)}), bf16[32,2,8,512]{3,2,1,0:T(8,128)(2,1)S(1)}, u32[]{:S(2)}, u32[]{:S(2)}) async-start(bf16[32,2,8,512]{3,2,1,0:T(8,128)(2,1)} %time.3), calls=%async_computation.3 | async-start | bytes 1048576 | tf_op jit(solution)/shard_map/all_to_all | solution.py:105
  80.7 0.0 copy-start.8
  80.7 1.9 %copy-done.8 = bf16[1024,1536]{1,0:T(8,128)(2,1)S(1)} copy-done((bf16[1024,1536]{1,0:T(8,128)(2,1)S(1)}, bf16[1024,1536]{1,0:T(8,128)(2,1)}, u32[]{:S(2)}) %copy-start.8) | copy-done | bytes 3145752
  82.6 4.4 %time.2 = bf16[32,2,8,512]{3,2,1,0:T(8,128)(2,1)} custom-call(bf16[32,2,8,1024]{3,2,1,0:T(8,128)(2,1)S(1)} %all-to-all-done.rows_ref, bf16[1024,1536]{1,0:T(8,128)(2,1)S(1)} %copy-done.8), custom_call_target="tpu_custom_call" | custom-call | flops 2684354560 | bytes 5242880 | tf_op jit(solution)/shard_map/time/pallas_call | solution.py:148
  86.9 10.1 %all-to-all-done.3.context_ref = bf16[32,2,8,512]{3,2,1,0:T(8,128)(2,1)S(1)} async-done(((bf16[32,2,8,512]{3,2,1,0:T(8,128)(2,1)}), bf16[32,2,8,512]{3,2,1,0:T(8,128)(2,1)S(1)}, u32[]{:S(2)}, u32[]{:S(2)}) %all-to-all-start.3) | async-done | bytes 524320 | tf_op jit(solution)/shard_map/all_to_all | solution.py:105
  97.0 2.6 %all-to-all-start.1 = ((bf16[32,2,8,512]{3,2,1,0:T(8,128)(2,1)}), bf16[32,2,8,512]{3,2,1,0:T(8,128)(2,1)S(1)}, u32[]{:S(2)}, u32[]{:S(2)}) async-start(bf16[32,2,8,512]{3,2,1,0:T(8,128)(2,1)} %time.2), calls=%async_computation.1 | async-start | bytes 1048576 | tf_op jit(solution)/shard_map/all_to_all | solution.py:105
  99.7 1.2 %copy-done.4 = bf16[2,256,1024]{2,1,0:T(8,128)(2,1)S(1)} copy-done((bf16[2,256,1024]{2,1,0:T(8,128)(2,1)S(1)}, bf16[2,256,1024]{2,1,0:T(8,128)(2,1)}, u32[]{:S(2)}) %copy-start.4) | copy-done | bytes 1048600
  100.9 1.0 final.3
  101.9 14.2 %all-to-all-done.1.context_ref = bf16[32,2,8,512]{3,2,1,0:T(8,128)(2,1)S(1)} async-done(((bf16[32,2,8,512]{3,2,1,0:T(8,128)(2,1)}), bf16[32,2,8,512]{3,2,1,0:T(8,128)(2,1)S(1)}, u32[]{:S(2)}, u32[]{:S(2)}) %all-to-all-start.1) | async-done | bytes 524320 | tf_op jit(solution)/shard_map/all_to_all | solution.py:105
  116.0 1.2 %copy-done.2 = bf16[2,256,1024]{2,1,0:T(8,128)(2,1)S(1)} copy-done((bf16[2,256,1024]{2,1,0:T(8,128)(2,1)S(1)}, bf16[2,256,1024]{2,1,0:T(8,128)(2,1)}, u32[]{:S(2)}) %copy-start.2) | copy-done | bytes 1048600
  117.2 1.0 final.2
  118.2 1.5 %maximum_bitcast_fusion = bf16[4,1,256,1024]{3,2,1,0:T(8,128)(2,1)} fusion(bf16[2,256,1024]{2,1,0:T(8,128)(2,1)S(1)} %final.3, bf16[2,256,1024]{2,1,0:T(8,128)(2,1)S(1)} %final.2), kind=kLoop, calls=%fused_computation | loop fusion | flops 1048576 | bytes 4194304 | tf_op jit(solution)/shard_map/reshape | solution.py:199
  (17 shorter events, 0.0 us)
Async XLA Ops:
  0.0 1.9 %copy-start.5 = (bf16[1024,1536]{1,0:T(8,128)(2,1)S(1)}, bf16[1024,1536]{1,0:T(8,128)(2,1)}, u32[]{:S(2)}) copy-start(bf16[1024,1536]{1,0:T(8,128)(2,1)} %project_ref.6) | copy-start | bytes 9437188
  1.9 1.6 %copy-start.9 = (bf16[4,1,256,1024]{3,2,1,0:T(8,128)(2,1)S(1)}, bf16[4,1,256,1024]{3,2,1,0:T(8,128)(2,1)}, u32[]{:S(2)}) copy-start(bf16[4,1,256,1024]{3,2,1,0:T(8,128)(2,1)} %param.7) | copy-start | bytes 6291460
  3.5 1.2 %copy-start.11 = (bf16[512,1024]{1,0:T(8,128)(2,1)S(1)}, bf16[512,1024]{1,0:T(8,128)(2,1)}, u32[]{:S(2)}) copy-start(bf16[512,1024]{1,0:T(8,128)(2,1)} %output_ref.6) | copy-start | bytes 3145732
  4.7 0.7 copy-start.13
  5.4 0.7 copy-start.15
  6.1 14.2 %copy-start.14 = (f32[1024]{0:T(1024)S(1)}, f32[1024]{0:T(1024)}, u32[]{:S(2)}) copy-start(f32[1024]{0:T(1024)} %param.8) | copy-start | bytes 12292
  6.1 14.2 %copy-start.16 = (f32[1024]{0:T(1024)S(1)}, f32[1024]{0:T(1024)}, u32[]{:S(2)}) copy-start(f32[1024]{0:T(1024)} %param.11) | copy-start | bytes 12292
  11.9 1.0 copy-start.3
  12.9 7.3 %copy-start.10 = (bf16[4,1,256,1024]{3,2,1,0:T(8,128)(2,1)S(1)}, bf16[4,1,256,1024]{3,2,1,0:T(8,128)(2,1)}, u32[]{:S(2)}) copy-start(bf16[4,1,256,1024]{3,2,1,0:T(8,128)(2,1)} %param.7) | copy-start | bytes 6291460
  12.9 34.9 %all-to-all-start.2 = ((bf16[32,2,8,1024]{3,2,1,0:T(8,128)(2,1)}), bf16[32,2,8,1024]{3,2,1,0:T(8,128)(2,1)S(1)}, u32[]{:S(2)}, u32[]{:S(2)}) async-start(bf16[32,2,8,1024]{3,2,1,0:T(8,128)(2,1)} %get-tuple-element.12), calls=%async_computation.2 | async-start | bytes 2097152 | tf_op jit(solution)/shard_map/all_to_all | solution.py:105
  20.3 1.9 %copy-start.6 = (bf16[1024,1536]{1,0:T(8,128)(2,1)S(1)}, bf16[1024,1536]{1,0:T(8,128)(2,1)}, u32[]{:S(2)}) copy-start(bf16[1024,1536]{1,0:T(8,128)(2,1)} %project_ref.6) | copy-start | bytes 9437188
  22.2 1.2 %copy-start.12 = (bf16[512,1024]{1,0:T(8,128)(2,1)S(1)}, bf16[512,1024]{1,0:T(8,128)(2,1)}, u32[]{:S(2)}) copy-start(bf16[512,1024]{1,0:T(8,128)(2,1)} %output_ref.6) | copy-start | bytes 3145732
  29.3 1.0 copy-start.1
  47.8 30.2 %all-to-all-start = ((bf16[32,2,8,1024]{3,2,1,0:T(8,128)(2,1)}), bf16[32,2,8,1024]{3,2,1,0:T(8,128)(2,1)S(1)}, u32[]{:S(2)}, u32[]{:S(2)}) async-start(bf16[32,2,8,1024]{3,2,1,0:T(8,128)(2,1)} %get-tuple-element.10), calls=%async_computation | async-start | bytes 2097152 | tf_op jit(solution)/shard_map/all_to_all | solution.py:105
  50.5 1.9 %copy-start.7 = (bf16[1024,1536]{1,0:T(8,128)(2,1)S(1)}, bf16[1024,1536]{1,0:T(8,128)(2,1)}, u32[]{:S(2)}) copy-start(bf16[1024,1536]{1,0:T(8,128)(2,1)} %project_ref.7) | copy-start | bytes 9437188
  78.1 19.0 %all-to-all-start.3 = ((bf16[32,2,8,512]{3,2,1,0:T(8,128)(2,1)}), bf16[32,2,8,512]{3,2,1,0:T(8,128)(2,1)S(1)}, u32[]{:S(2)}, u32[]{:S(2)}) async-start(bf16[32,2,8,512]{3,2,1,0:T(8,128)(2,1)} %time.3), calls=%async_computation.3 | async-start | bytes 1048576 | tf_op jit(solution)/shard_map/all_to_all | solution.py:105
  80.7 1.9 %copy-start.8 = (bf16[1024,1536]{1,0:T(8,128)(2,1)S(1)}, bf16[1024,1536]{1,0:T(8,128)(2,1)}, u32[]{:S(2)}) copy-start(bf16[1024,1536]{1,0:T(8,128)(2,1)} %project_ref.7) | copy-start | bytes 9437188
  82.6 17.1 %copy-start = (bf16[512,1024]{1,0:T(8,128)(2,1)S(1)}, bf16[512,1024]{1,0:T(8,128)(2,1)}, u32[]{:S(2)}) copy-start(bf16[512,1024]{1,0:T(8,128)(2,1)} %output_ref.7) | copy-start | bytes 3145732
  97.0 19.0 %all-to-all-start.1 = ((bf16[32,2,8,512]{3,2,1,0:T(8,128)(2,1)}), bf16[32,2,8,512]{3,2,1,0:T(8,128)(2,1)S(1)}, u32[]{:S(2)}, u32[]{:S(2)}) async-start(bf16[32,2,8,512]{3,2,1,0:T(8,128)(2,1)} %time.2), calls=%async_computation.1 | async-start | bytes 1048576 | tf_op jit(solution)/shard_map/all_to_all | solution.py:105
  99.7 1.2 %copy-start.4 = (bf16[2,256,1024]{2,1,0:T(8,128)(2,1)S(1)}, bf16[2,256,1024]{2,1,0:T(8,128)(2,1)}, u32[]{:S(2)}) copy-start(bf16[2,256,1024]{2,1,0:T(8,128)(2,1)} %copy-done.3) | copy-start | bytes 3145732
  116.0 1.2 %copy-start.2 = (bf16[2,256,1024]{2,1,0:T(8,128)(2,1)S(1)}, bf16[2,256,1024]{2,1,0:T(8,128)(2,1)}, u32[]{:S(2)}) copy-start(bf16[2,256,1024]{2,1,0:T(8,128)(2,1)} %copy-done.1) | copy-start | bytes 3145732

commit v2 on v1

v2 whole, which is shorter than its diff:
```python
from functools import partial

import jax
import jax.numpy as jnp
from jax import lax
from jax.experimental import pallas as pl
from jax.experimental.pallas import tpu as pltpu
from jax.sharding import PartitionSpec as P

HEADS = 8
HEAD_DIM = 64
WIDTH = HEADS * HEAD_DIM
LANES = 128
EPSILON = 1e-06
MASKED = -1e30
ANYWHERE = pl.BlockSpec(memory_space=pl.ANY)
AXES = ("grp", "dev")
VMEM_LIMIT = 60 * 1024 * 1024
TIME_VMEM_LIMIT = 40 * 1024 * 1024
FINAL_VMEM_LIMIT = 40 * 1024 * 1024


def normed(floats, gain):
    centred = floats - jnp.mean(floats, axis=-1, keepdims=True)
    spread = jnp.mean(jnp.square(centred), axis=-1, keepdims=True)
    return centred * lax.rsqrt(spread + EPSILON) * gain


def attend(heads, bias):
    rows = heads.shape[0]
    low = lax.broadcasted_iota(jnp.int32, (rows, LANES), 1) < HEAD_DIM
    ones = jnp.ones((rows, LANES), jnp.bfloat16)
    contexts, pending = [], []
    for pair in range(WIDTH // LANES):
        at = pair * LANES
        queries = heads[:, at : at + LANES] * jnp.bfloat16(HEAD_DIM**-0.5)
        keys = heads[:, WIDTH + at : WIDTH + at + LANES]
        values = heads[:, 2 * WIDTH + at : 2 * WIDTH + at + LANES]
        nothing = jnp.zeros_like(queries)
        stacked = jnp.concatenate([jnp.where(low, queries, nothing), jnp.where(low, nothing, queries)], axis=0)
        scores = lax.dot_general(stacked, keys, (((1,), (1,)), ((), ())), preferred_element_type=jnp.float32)
        if bias is not None:
            scores = scores + jnp.concatenate([bias, bias], axis=0)
        weights = jnp.exp(scores - jnp.max(scores, axis=-1, keepdims=True)).astype(jnp.bfloat16)
        pending.append((weights, values))
    for weights, values in pending:
        sums = jnp.dot(weights, jnp.concatenate([values, ones], axis=1), preferred_element_type=jnp.float32)
        context = sums[:, :LANES] / sums[:, LANES:]
        contexts.append(jnp.where(low, context[:rows], context[rows:]))
    return jnp.concatenate(contexts, axis=1).astype(jnp.bfloat16)


def bit_groups():
    inner = lax.axis_size("dev").bit_length() - 1
    bits = inner + lax.axis_size("grp").bit_length() - 1
    far = [tuple(reversed(range(1, inner)))]
    near = [(0,), *((bit,) for bit in reversed(range(inner, bits)))]
    return near + far


def mask_of(index, group):
    return sum(((index >> (len(group) - 1 - at)) & 1) << bit for at, bit in enumerate(group))


def put(parts, scratch, out_refs, groups):
    if groups is None:
        out_refs[0][...] = parts.reshape(out_refs[0].shape)
        return
    scratch[...] = parts
    me = lax.axis_index(AXES)
    order = sum(groups, ())
    size = out_refs[0].shape[0]
    for place in range(size * len(out_refs)):
        out_refs[place // size][place % size, 0] = scratch[mask_of(place, order) ^ me]


def take(ref, groups):
    if groups is None:
        return ref[...]
    me = lax.axis_index(AXES)
    order = sum(groups, ())
    parts = []
    for device in range(ref.shape[0]):
        slot = device ^ me
        place = sum(((slot >> bit) & 1) << (len(order) - 1 - at) for at, bit in enumerate(order))
        parts.append(ref[place, 0])
    return jnp.stack(parts)


def space_kernel(video_ref, gain_ref, project_ref, output_ref, time_gain_ref, *refs):
    mixed_ref, sent_ref = refs[-2:]
    floats = video_ref[0].astype(jnp.float32)
    heads = jnp.dot(
        normed(floats, gain_ref[...]).astype(jnp.bfloat16), project_ref[...], preferred_element_type=jnp.float32
    ).astype(jnp.bfloat16)
    context = attend(heads, None)
    mixed = (floats + jnp.dot(context, output_ref[...], preferred_element_type=jnp.float32)).astype(jnp.bfloat16)
    mixed_ref[0] = mixed
    sent = normed(mixed.astype(jnp.float32), time_gain_ref[...])
    sent_ref[...] = sent.reshape(sent_ref.shape).astype(jnp.bfloat16)


def time_kernel(back, extra, patch_here, rows_ref, project_ref, *refs):
    *context_refs, bias_ref = refs[extra:]
    context_refs, scratch = (context_refs, None) if back is None else (context_refs[:-1], context_refs[-1])
    rows, width = bias_ref.shape[0], rows_ref.shape[-1]

    @pl.when(pl.program_id(0) == 0)
    def _():
        query = lax.broadcasted_iota(jnp.int32, (rows, rows), 0)
        key = lax.broadcasted_iota(jnp.int32, (rows, rows), 1)
        seen = (key <= query) & (lax.rem(query, patch_here) == lax.rem(key, patch_here))
        bias_ref[...] = jnp.where(seen, 0.0, MASKED)

    arrived = rows_ref[...].astype(jnp.float32).reshape(rows, width).astype(jnp.bfloat16)
    heads = jnp.dot(arrived, project_ref[...], preferred_element_type=jnp.float32).astype(jnp.bfloat16)
    context = attend(heads, bias_ref[...]).astype(jnp.float32)
    shape = context_refs[0].shape if back is None else scratch.shape
    put(context.reshape(shape).astype(jnp.bfloat16), scratch, context_refs, back)


def final_kernel(order, mixed_ref, context_ref, output_ref, *refs):
    out_ref = refs[-1]
    rows = mixed_ref.shape[1]
    context = take(context_ref, order).astype(jnp.float32).reshape(rows, WIDTH).astype(jnp.bfloat16)
    update = jnp.dot(context, output_ref[...], preferred_element_type=jnp.float32)
    out_ref[0] = (mixed_ref[0].astype(jnp.float32) + update).astype(jnp.bfloat16)


def whole(shape):
    return pl.BlockSpec(shape, lambda c: (0,) * len(shape))


def exchange_spec(count, patch_here, width):
    if patch_here % 8:
        return pl.BlockSpec((1, count * patch_here, width), lambda c: (c, 0, 0))
    return pl.BlockSpec((count, 1, patch_here, width), lambda c: (0, c, 0, 0))


def exchange_shape(count, clips, patch_here, width):
    if patch_here % 8:
        return jax.ShapeDtypeStruct((clips, count * patch_here, width), jnp.bfloat16)
    return jax.ShapeDtypeStruct((count, clips, patch_here, width), jnp.bfloat16)


def exchange(sent, count, patch_here):
    plain = sent.ndim == 3
    if plain:
        clips, _, width = sent.shape
        sent = sent.reshape(clips, count, patch_here, width).transpose(1, 0, 2, 3)
    arrived = lax.all_to_all(sent, AXES, split_axis=0, concat_axis=0, tiled=True)
    if plain:
        arrived = arrived.transpose(1, 0, 2, 3).reshape(clips, count * patch_here, width)
    return arrived


def in_hbm(array):
    return pltpu.with_memory_space_constraint(array, pltpu.HBM)


def after(rows, awaited):
    return pl.pallas_call(
        lambda *refs: None,
        in_specs=[ANYWHERE] * (1 + len(awaited)),
        out_specs=ANYWHERE,
        out_shape=jax.ShapeDtypeStruct(rows.shape, rows.dtype),
        input_output_aliases={0: 0},
        compiler_params=pltpu.CompilerParams(vmem_limit_bytes=2 * 1024 * 1024),
        name="after",
    )(rows, *awaited)


def swap(blocks, groups):
    devices = 1 << len(sum(groups, ()))
    rows = blocks[0].shape[1:]
    blocks = [block.reshape(1, *(1 << len(group) for group in groups[1:]), *rows) for block in blocks]
    for at, group in enumerate(groups):
        arrived = [
            lax.ppermute(block, AXES, [(device, device ^ mask_of(index, group)) for device in range(devices)])
            for index, block in enumerate(blocks)
            if index
        ]
        if len(group) > 1:
            awaited = arrived
        whole_buffer = jnp.concatenate([blocks[0], *arrived], axis=at)
        if at + 1 < len(groups):
            blocks = jnp.split(whole_buffer, 1 << len(groups[at + 1]), axis=at + 1)
    return whole_buffer.reshape(devices, *rows), awaited


def cost(macs, bytes_accessed, exps):
    return pl.CostEstimate(flops=2 * macs, bytes_accessed=bytes_accessed, transcendentals=exps)


def sent_specs(count, clips, patch_here, width, order):
    if order is None:
        return [exchange_shape(count, clips, patch_here, width)], [exchange_spec(count, patch_here, width)], []
    parts = 1 << len(order[0])
    shape = exchange_shape(count // parts, clips, patch_here, width)
    spec = exchange_spec(count // parts, patch_here, width)
    return [shape] * parts, [spec] * parts, [pltpu.VMEM((count, patch_here, width), jnp.bfloat16)]


def space_call(video, first, clips, space_gain, space_project, space_output, time_gain, count, before):
    rows, width = video.shape[1:]
    return pl.pallas_call(
        space_kernel,
        grid=(clips,),
        in_specs=[
            pl.BlockSpec((1, rows, width), lambda c: (first + c, 0, 0)),
            whole((1, width)),
            whole((width, 3 * WIDTH)),
            whole((WIDTH, width)),
            whole((1, width)),
        ]
        + [ANYWHERE] * len(before),
        out_specs=[pl.BlockSpec((1, rows, width), lambda c: (c, 0, 0)), exchange_spec(count, rows // count, width)],
        out_shape=[jax.ShapeDtypeStruct((clips, rows, width), jnp.bfloat16), exchange_shape(count, clips, rows // count, width)],
        cost_estimate=cost(
            clips * rows * (width * 4 * WIDTH + 8 * rows * WIDTH), 2 * (4 * width * WIDTH + 3 * clips * rows * width),
            clips * HEADS * rows * rows,
        ),
        compiler_params=pltpu.CompilerParams(vmem_limit_bytes=VMEM_LIMIT),
        name="space",
    )(video, space_gain, space_project, space_output, time_gain, *map(in_hbm, before))


def time_call(arrived, clips, rows, time_project, count, before, back):
    width = arrived.shape[-1]
    patch_here = rows // count
    shapes, specs, scratch = sent_specs(count, clips, patch_here, WIDTH, back)
    return pl.pallas_call(
        partial(time_kernel, back, len(before), patch_here),
        grid=(clips,),
        in_specs=[exchange_spec(count, patch_here, width), whole((width, 3 * WIDTH))] + [ANYWHERE] * len(before),
        out_specs=specs,
        out_shape=shapes,
        scratch_shapes=scratch + [pltpu.VMEM((rows, rows), jnp.float32)],
        cost_estimate=cost(
            clips * rows * (width * 3 * WIDTH + 8 * rows * WIDTH), 2 * (3 * width * WIDTH + 2 * clips * rows * width),
            clips * HEADS * rows * rows,
        ),
        compiler_params=pltpu.CompilerParams(vmem_limit_bytes=TIME_VMEM_LIMIT),
        name="time",
    )(arrived, in_hbm(time_project), *map(in_hbm, before))


def final_call(mixed, context, time_output, count, first, total, before, order):
    clips, rows, width = mixed.shape
    return pl.pallas_call(
        partial(final_kernel, order),
        grid=(clips,),
        in_specs=[
            pl.BlockSpec((1, rows, width), lambda c: (c, 0, 0)),
            exchange_spec(count, rows // count, WIDTH),
            whole((WIDTH, width)),
        ]
        + [ANYWHERE] * len(before),
        out_specs=pl.BlockSpec((1, rows, width), lambda c: (first + c, 0, 0)),
        out_shape=jax.ShapeDtypeStruct((total, rows, width), jnp.bfloat16),
        input_output_aliases={3: 0} if before else {},
        cost_estimate=cost(clips * rows * width * WIDTH, 2 * (width * WIDTH + 3 * clips * rows * width), 0),
        compiler_params=pltpu.CompilerParams(vmem_limit_bytes=FINAL_VMEM_LIMIT),
        name="final",
    )(mixed, context, time_output, *before)


def per_device(video_in, space_gain, space_project, space_output, time_gain, time_project, time_output):
    clip_count, frame_local, patch_count, width = video_in.shape
    count = lax.axis_size("grp") * lax.axis_size("dev")
    patch_here = patch_count // count
    video = video_in.reshape(clip_count, patch_count, width)
    weights = space_gain.reshape(1, width), space_project, space_output, time_gain.reshape(1, width)
    swappable = patch_here % 8 == 0 and count & (count - 1) == 0
    back = bit_groups() if swappable else None
    chunks = [(0, 1), (1, clip_count - 1)]
    mixed, arrived, out = [], [], []
    for first, clips in chunks:
        kept, sent = space_call(video, first, clips, *weights, count, mixed)
        mixed.append(kept)
        arrived.append(exchange(sent, count, patch_here))
    context = time_call(arrived[0], 1, patch_count, time_project, count, [], back)
    if swappable:
        early, awaited = swap(context, back)
    else:
        early, awaited = exchange(context[0], count, patch_here), []
    context = time_call(arrived[1], clip_count - 1, patch_count, time_project, count, context[:1], None)
    late = exchange(after(context[0], awaited) if awaited else context[0], count, patch_here)
    for (first, _), kept, context, groups in zip(chunks, mixed, (early, late), (back, None)):
        out = [final_call(kept, context, time_output, count, first, clip_count, out, groups)]
    return out[0].reshape(clip_count, frame_local, patch_count, width)


def solution(mesh):
    in_specs = (P(None, AXES, None, None), P(), P(), P(), P(), P(), P())
    return jax.shard_map(
        per_device, mesh=mesh, in_specs=in_specs, out_specs=P(None, AXES, None, None), check_vma=False
    )
```

time: 120 us -> 109 us (0.908)
  local copies, waits for them, and re-layouts: 17.4 us -> 1.16 us
  Pallas kernels: 22.3 us -> 31.2 us
  waiting for transfers between devices: 63.2 us -> 55.5 us
  starting transfers between devices: 15.2 us -> 20.5 us
  other arithmetic: 1.5 us -> 0.09 us
    all_to_all x4 -> x3, waiting for transfers between devices: 63.2 us -> 34.3 us  [exchange(): lax.all_to_all(sent, AXES, split_axis=0, concat_axis=0, tiled=True)]
    ppermute x0 -> x6, waiting for transfers between devices: none -> 21.3 us  [swap(): lax.ppermute(block, AXES, [(device, device ^ mask_of(index, group)) for d...]
    unnamed x34 -> x8, local copies, waits for them, and re-layouts: 17.4 us -> 1.16 us
    ppermute x0 -> x6, starting transfers between devices: none -> 7.78 us  [swap(): lax.ppermute(block, AXES, [(device, device ^ mask_of(index, group)) for d...]
    pallas_call x4 -> x5, Pallas kernels: 10.6 us -> 15.2 us  [the longest x2 11.4 us: time_call(): pl.pallas_call(partial(time_kernel, back, len(before), patch_here), grid=...]
    pallas_call x2, Pallas kernels: 11.7 us -> 16 us  [space_call(): pl.pallas_call(space_kernel, grid=(clips,), in_specs=[pl.BlockSpec((1, ro...]
    all_to_all x4 -> x3, starting transfers between devices: 15.2 us -> 12.8 us  [exchange(): lax.all_to_all(sent, AXES, split_axis=0, concat_axis=0, tiled=True)]
    reshape x1 -> x0, other arithmetic: 1.5 us -> none  [per_device(): jnp.concatenate(done, axis=0)]
  transfers between devices with their start and end apart: 4 -> 9, of which waited for: 4 -> 6; matrix products, arithmetic and copies ran while one was open for 0% -> 0% of each run, Pallas kernels for 13% -> 21%
where the time goes in v2:
time: 109 us
  waiting for transfers between devices  55.5 us (51%)
  Pallas kernels  31.2 us (29%)
  starting transfers between devices  20.5 us (19%)
  local copies, waits for them, and re-layouts  1.16 us (1%)
    all_to_all x3, waiting for transfers between devices, exchange(): lax.all_to_all(sent, AXES, split_axis=0, concat_axis=0, tiled=True)  34.3 us
    ppermute x6, waiting for transfers between devices, swap(): lax.ppermute(block, AXES, [(device, device ^ mask_of(index, group)) for d...  21.3 us
    pallas_call x2, Pallas kernels, space_call(): pl.pallas_call(space_kernel, grid=(clips,), in_specs=[pl.BlockSpec((1, ro...  16 us
    all_to_all x3, starting transfers between devices, exchange(): lax.all_to_all(sent, AXES, split_axis=0, concat_axis=0, tiled=True)  12.8 us
    pallas_call x2, Pallas kernels, time_call(): pl.pallas_call(partial(time_kernel, back, len(before), patch_here), grid=...  11.4 us
    ppermute x6, starting transfers between devices, swap(): lax.ppermute(block, AXES, [(device, device ^ mask_of(index, group)) for d...  7.78 us
    pallas_call x2, Pallas kernels, final_call(): pl.pallas_call(partial(final_kernel, order), grid=(clips,), in_specs=[pl....  3.84 us
  transfers between devices with their start and end apart: 9, of which 6 were waited for; matrix products, arithmetic and copies ran while one was open for 0% of the time, Pallas kernels for 21%

profile of v2, /device:TPU:0, one launch (start us, length us, event | category | flops | bytes accessed | tf_op | source)
XLA Modules:
  0.0 108.7 jit_solution(12160946067657685755)
XLA Ops:
  0.0 5.6 %space.2 = (bf16[1,256,1024]{2,1,0:T(8,128)(2,1)}, bf16[32,1,8,1024]{3,2,1,0:T(8,128)(2,1)}) custom-call(bf16[4,256,1024]{2,1,0:T(8,128)(2,1)} %bitcast.12, f32[1,1024]{1,0:T(1,128)} %bitcast.14, bf16[1024,1536]{1,0:T(8,128)(2,1)} %project_ref.5, bf16[512,1024]{1,0:T(8,128)(2,1)} %output_ref.5, f32[1,1024]{1,0:T(1,128)} %bitcast.16), custom_call_target="tpu_custom_call" | custom-call | flops 1610612736 | bytes 5767168 | tf_op jit(solution)/shard_map/space/pallas_call | solution.py:206
  5.6 7.3 %all-to-all-start.1 = ((bf16[32,1,8,1024]{3,2,1,0:T(8,128)(2,1)}), bf16[32,1,8,1024]{3,2,1,0:T(8,128)(2,1)S(1)}, u32[]{:S(2)}, u32[]{:S(2)}) async-start(bf16[32,1,8,1024]{3,2,1,0:T(8,128)(2,1)} %get-tuple-element.14), calls=%async_computation.1 | async-start | bytes 1048576 | tf_op jit(solution)/shard_map/all_to_all | solution.py:151
  12.9 10.4 %space.3 = (bf16[3,256,1024]{2,1,0:T(8,128)(2,1)}, bf16[32,3,8,1024]{3,2,1,0:T(8,128)(2,1)}) custom-call(bf16[4,256,1024]{2,1,0:T(8,128)(2,1)} %bitcast.13, f32[1,1024]{1,0:T(1,128)} %bitcast.15, bf16[1024,1536]{1,0:T(8,128)(2,1)} %project_ref.5, bf16[512,1024]{1,0:T(8,128)(2,1)} %output_ref.5, f32[1,1024]{1,0:T(1,128)} %bitcast.17, ...), custom_call_target="tpu_custom_call" | custom-call | flops 4831838208 | bytes 8912896 | tf_op jit(solution)/shard_map/space/pallas_call | solution.py:206
  23.3 5.9 %all-to-all-done.1.rows_ref = bf16[32,1,8,1024]{3,2,1,0:T(8,128)(2,1)S(1)} async-done(((bf16[32,1,8,1024]{3,2,1,0:T(8,128)(2,1)}), bf16[32,1,8,1024]{3,2,1,0:T(8,128)(2,1)S(1)}, u32[]{:S(2)}, u32[]{:S(2)}) %all-to-all-start.1) | async-done | bytes 524320 | tf_op jit(solution)/shard_map/all_to_all | solution.py:151
  29.3 2.7 %all-to-all-start = ((bf16[32,3,8,1024]{3,2,1,0:T(8,128)(2,1)}), bf16[32,3,8,1024]{3,2,1,0:T(8,128)(2,1)S(1)}, u32[]{:S(2)}, u32[]{:S(2)}) async-start(bf16[32,3,8,1024]{3,2,1,0:T(8,128)(2,1)} %get-tuple-element.13), calls=%async_computation | async-start | bytes 3145728 | tf_op jit(solution)/shard_map/all_to_all | solution.py:151
  32.0 3.6 %time.2 = (bf16[16,1,8,512]{3,2,1,0:T(8,128)(2,1)S(1)}, bf16[16,1,8,512]{3,2,1,0:T(8,128)(2,1)S(1)}) custom-call(bf16[32,1,8,1024]{3,2,1,0:T(8,128)(2,1)S(1)} %all-to-all-done.1.rows_ref, bf16[1024,1536]{1,0:T(8,128)(2,1)} %project_ref.7), custom_call_target="tpu_custom_call" | custom-call | flops 1342177280 | bytes 4194304 | tf_op jit(solution)/shard_map/time/pallas_call | solution.py:232
  35.6 0.0 copy-start.3
  35.6 1.7 %collective-permute-start = (bf16[1,2,2,4,1,8,512]{6,5,4,3,2,1,0:T(8,128)(2,1)S(1)}, bf16[1,2,2,4,1,8,512]{6,5,4,3,2,1,0:T(8,128)(2,1)S(1)}, u32[]{:S(2)}, u32[]{:S(2)}) collective-permute-start(bf16[1,2,2,4,1,8,512]{6,5,4,3,2,1,0:T(8,128)(2,1)S(1)} %bitcast.11), channel_id=1, source_target_pairs={{0,1},{1,0},{2,3},{3,2},{4,5},{5,4},{6,7},{7,6},{8,9},{9,8},{10,11... | collective-permute-start | bytes 393224 | tf_op jit(solution)/shard_map/ppermute | solution.py:179
  37.3 15.8 %collective-permute-done = bf16[1,2,2,4,1,8,512]{6,5,4,3,2,1,0:T(8,128)(2,1)S(1)} collective-permute-done((bf16[1,2,2,4,1,8,512]{6,5,4,3,2,1,0:T(8,128)(2,1)S(1)}, bf16[1,2,2,4,1,8,512]{6,5,4,3,2,1,0:T(8,128)(2,1)S(1)}, u32[]{:S(2)}, u32[]{:S(2)}) %collective-permute-start) | collective-permute-done | bytes 131104 | tf_op jit(solution)/shard_map/ppermute | solution.py:179
  53.0 1.6 %collective-permute-start.1 = (bf16[2,1,2,4,1,8,512]{6,5,4,3,2,1,0:T(8,128)(2,1)S(1)}, bf16[2,1,2,4,1,8,512]{6,5,4,3,2,1,0:T(8,128)(2,1)S(1)}, u32[]{:S(2)}, u32[]{:S(2)}) collective-permute-start(bf16[2,1,2,4,1,8,512]{6,5,4,3,2,1,0:T(8,128)(2,1)S(1)} %get-tuple-element.22), channel_id=1, source_target_pairs={{0,16},{1,17},{2,18},{3,19},{4,20},{5,21},{6,22},{7,23},{8,24},{9,... | collective-permute-start | bytes 393224 | tf_op jit(solution)/shard_map/ppermute | solution.py:179
  54.6 4.2 %collective-permute-done.1 = bf16[2,1,2,4,1,8,512]{6,5,4,3,2,1,0:T(8,128)(2,1)S(1)} collective-permute-done((bf16[2,1,2,4,1,8,512]{6,5,4,3,2,1,0:T(8,128)(2,1)S(1)}, bf16[2,1,2,4,1,8,512]{6,5,4,3,2,1,0:T(8,128)(2,1)S(1)}, u32[]{:S(2)}, u32[]{:S(2)}) %collective-permute-start.1) | collective-permute-done | bytes 131104 | tf_op jit(solution)/shard_map/ppermute | solution.py:179
  58.8 0.1 collective-permute-start.2
  58.9 1.3 %collective-permute-done.2 = bf16[2,2,1,4,1,8,512]{6,5,4,3,2,1,0:T(8,128)(2,1)S(1)} collective-permute-done((bf16[2,2,1,4,1,8,512]{6,5,4,3,2,1,0:T(8,128)(2,1)S(1)}, bf16[2,2,1,4,1,8,512]{6,5,4,3,2,1,0:T(8,128)(2,1)S(1)}, u32[]{:S(2)}, u32[]{:S(2)}) %collective-permute-start.2) | collective-permute-done | bytes 131104 | tf_op jit(solution)/shard_map/ppermute | solution.py:179
  60.2 0.1 collective-permute-start.3
  60.3 3.5 %collective-permute-start.4 = (bf16[2,2,2,1,1,8,512]{6,5,4,3,2,1,0:T(8,128)(2,1)S(1)}, bf16[2,2,2,1,1,8,512]{6,5,4,3,2,1,0:T(8,128)(2,1)S(1)}, u32[]{:S(2)}, u32[]{:S(2)}) collective-permute-start(bf16[2,2,2,1,1,8,512]{6,5,4,3,2,1,0:T(8,128)(2,1)S(1)} %get-tuple-element.19), channel_id=1, source_target_pairs={{0,4},{1,5},{2,6},{3,7},{4,0},{5,1},{6,2},{7,3},{8,12},{9,13},{10,... | collective-permute-start | bytes 196616 | tf_op jit(solution)/shard_map/ppermute | solution.py:179
  63.9 0.8 collective-permute-start.5
  64.7 8.9 %all-to-all-done.rows_ref = bf16[32,3,8,1024]{3,2,1,0:T(8,128)(2,1)S(1)} async-done(((bf16[32,3,8,1024]{3,2,1,0:T(8,128)(2,1)}), bf16[32,3,8,1024]{3,2,1,0:T(8,128)(2,1)S(1)}, u32[]{:S(2)}, u32[]{:S(2)}) %all-to-all-start) | async-done | bytes 1572896 | tf_op jit(solution)/shard_map/all_to_all | solution.py:151
  73.6 0.0 copy-done.3
  73.6 7.8 %time.3.refs_0_ = bf16[32,3,8,512]{3,2,1,0:T(8,128)(2,1)} custom-call(bf16[32,3,8,1024]{3,2,1,0:T(8,128)(2,1)S(1)} %all-to-all-done.rows_ref, bf16[1024,1536]{1,0:T(8,128)(2,1)} %project_ref.7, bf16[16,1,8,512]{3,2,1,0:T(8,128)(2,1)} %copy-done.3), custom_call_target="tpu_custom_call" | custom-call | flops 4026531840 | bytes 6291456 | tf_op jit(solution)/shard_map/time/pallas_call | solution.py:232
  81.4 0.0 copy-start
  81.4 0.0 collective-permute-done.3.refs_1_
  81.4 0.0 collective-permute-done.4.refs_2_
  81.4 0.0 collective-permute-done.5.refs_3_
  81.4 2.8 %all-to-all-start.2 = ((bf16[32,3,8,512]{3,2,1,0:T(8,128)(2,1)}), bf16[32,3,8,512]{3,2,1,0:T(8,128)(2,1)S(1)}, u32[]{:S(2)}, u32[]{:S(2)}) async-start(bf16[32,3,8,512]{3,2,1,0:T(8,128)(2,1)} %after.1), calls=%async_computation.2 | async-start | bytes 1572864 | tf_op jit(solution)/shard_map/all_to_all | solution.py:151
  84.2 0.0 copy-start.1
  84.2 0.0 copy-done
  84.2 0.0 copy-start.2
  84.2 1.1 %copy-done.2 = bf16[1,256,1024]{2,1,0:T(8,128)(2,1)S(1)} copy-done((bf16[1,256,1024]{2,1,0:T(8,128)(2,1)S(1)}, bf16[1,256,1024]{2,1,0:T(8,128)(2,1)}, u32[]{:S(2)}) %copy-start.2) | copy-done | bytes 524312
  85.4 1.3 %final.2.refs_0_ = bf16[4,256,1024]{2,1,0:T(8,128)(2,1)} custom-call(bf16[1,256,1024]{2,1,0:T(8,128)(2,1)S(1)} %copy-done.2, bf16[32,1,8,512]{3,2,1,0:T(8,128)(2,1)S(1)} %bitcast.9, bf16[512,1024]{1,0:T(8,128)(2,1)S(1)} %copy-done), custom_call_target="tpu_custom_call" | custom-call | flops 268435456 | bytes 2621440 | tf_op jit(solution)/shard_map/final/pallas_call | solution.py:250
  86.7 19.4 %all-to-all-done.2.context_ref = bf16[32,3,8,512]{3,2,1,0:T(8,128)(2,1)S(1)} async-done(((bf16[32,3,8,512]{3,2,1,0:T(8,128)(2,1)}), bf16[32,3,8,512]{3,2,1,0:T(8,128)(2,1)S(1)}, u32[]{:S(2)}, u32[]{:S(2)}) %all-to-all-start.2) | async-done | bytes 786464 | tf_op jit(solution)/shard_map/all_to_all | solution.py:151
  106.1 0.0 copy-done.1
  106.2 2.5 %final.3 = bf16[4,256,1024]{2,1,0:T(8,128)(2,1)} custom-call(bf16[3,256,1024]{2,1,0:T(8,128)(2,1)S(1)} %copy-done.1, bf16[32,3,8,512]{3,2,1,0:T(8,128)(2,1)S(1)} %all-to-all-done.2.context_ref, bf16[512,1024]{1,0:T(8,128)(2,1)S(1)} %copy-done, bf16[4,256,1024]{2,1,0:T(8,128)(2,1)} %final.2.refs_0_), custom_call_target="tpu_custom_call", output_to_operand_aliasing={{}: (3, {})} | custom-call | flops 805306368 | bytes 5767168 | tf_op jit(solution)/shard_map/final/pallas_call | solution.py:250
  (5 shorter events, 0.1 us)
Async XLA Ops:
  5.6 23.7 %all-to-all-start.1 = ((bf16[32,1,8,1024]{3,2,1,0:T(8,128)(2,1)}), bf16[32,1,8,1024]{3,2,1,0:T(8,128)(2,1)S(1)}, u32[]{:S(2)}, u32[]{:S(2)}) async-start(bf16[32,1,8,1024]{3,2,1,0:T(8,128)(2,1)} %get-tuple-element.14), calls=%async_computation.1 | async-start | bytes 1048576 | tf_op jit(solution)/shard_map/all_to_all | solution.py:151
  29.3 44.3 %all-to-all-start = ((bf16[32,3,8,1024]{3,2,1,0:T(8,128)(2,1)}), bf16[32,3,8,1024]{3,2,1,0:T(8,128)(2,1)S(1)}, u32[]{:S(2)}, u32[]{:S(2)}) async-start(bf16[32,3,8,1024]{3,2,1,0:T(8,128)(2,1)} %get-tuple-element.13), calls=%async_computation | async-start | bytes 3145728 | tf_op jit(solution)/shard_map/all_to_all | solution.py:151
  35.6 38.0 %copy-start.3 = (bf16[16,1,8,512]{3,2,1,0:T(8,128)(2,1)}, bf16[16,1,8,512]{3,2,1,0:T(8,128)(2,1)S(1)}, u32[]{:S(2)}) copy-start(bf16[16,1,8,512]{3,2,1,0:T(8,128)(2,1)S(1)} %get-tuple-element.15.refs_0_) | copy-start | bytes 393220
  35.6 17.5 %collective-permute-start = (bf16[1,2,2,4,1,8,512]{6,5,4,3,2,1,0:T(8,128)(2,1)S(1)}, bf16[1,2,2,4,1,8,512]{6,5,4,3,2,1,0:T(8,128)(2,1)S(1)}, u32[]{:S(2)}, u32[]{:S(2)}) collective-permute-start(bf16[1,2,2,4,1,8,512]{6,5,4,3,2,1,0:T(8,128)(2,1)S(1)} %bitcast.11), channel_id=1, source_target_pairs={{0,1},{1,0},{2,3},{3,2},{4,5},{5,4},{6,7},{7,6},{8,9},{9,8},{10,11... | collective-permute-start | bytes 393224 | tf_op jit(solution)/shard_map/ppermute | solution.py:179
  53.0 5.7 %collective-permute-start.1 = (bf16[2,1,2,4,1,8,512]{6,5,4,3,2,1,0:T(8,128)(2,1)S(1)}, bf16[2,1,2,4,1,8,512]{6,5,4,3,2,1,0:T(8,128)(2,1)S(1)}, u32[]{:S(2)}, u32[]{:S(2)}) collective-permute-start(bf16[2,1,2,4,1,8,512]{6,5,4,3,2,1,0:T(8,128)(2,1)S(1)} %get-tuple-element.22), channel_id=1, source_target_pairs={{0,16},{1,17},{2,18},{3,19},{4,20},{5,21},{6,22},{7,23},{8,24},{9,... | collective-permute-start | bytes 393224 | tf_op jit(solution)/shard_map/ppermute | solution.py:179
  58.8 1.4 %collective-permute-start.2 = (bf16[2,2,1,4,1,8,512]{6,5,4,3,2,1,0:T(8,128)(2,1)S(1)}, bf16[2,2,1,4,1,8,512]{6,5,4,3,2,1,0:T(8,128)(2,1)S(1)}, u32[]{:S(2)}, u32[]{:S(2)}) collective-permute-start(bf16[2,2,1,4,1,8,512]{6,5,4,3,2,1,0:T(8,128)(2,1)S(1)} %get-tuple-element.20), channel_id=1, source_target_pairs={{0,8},{1,9},{2,10},{3,11},{4,12},{5,13},{6,14},{7,15},{8,0},{9,1},... | collective-permute-start | bytes 393224 | tf_op jit(solution)/shard_map/ppermute | solution.py:179
  60.2 21.1 %collective-permute-start.3 = (bf16[2,2,2,1,1,8,512]{6,5,4,3,2,1,0:T(8,128)(2,1)S(1)}, bf16[2,2,2,1,1,8,512]{6,5,4,3,2,1,0:T(8,128)(2,1)S(1)}, u32[]{:S(2)}, u32[]{:S(2)}) collective-permute-start(bf16[2,2,2,1,1,8,512]{6,5,4,3,2,1,0:T(8,128)(2,1)S(1)} %get-tuple-element.18), channel_id=1, source_target_pairs={{0,2},{1,3},{2,0},{3,1},{4,6},{5,7},{6,4},{7,5},{8,10},{9,11},{10,... | collective-permute-start | bytes 196616 | tf_op jit(solution)/shard_map/ppermute | solution.py:179
  60.3 21.1 %collective-permute-start.4 = (bf16[2,2,2,1,1,8,512]{6,5,4,3,2,1,0:T(8,128)(2,1)S(1)}, bf16[2,2,2,1,1,8,512]{6,5,4,3,2,1,0:T(8,128)(2,1)S(1)}, u32[]{:S(2)}, u32[]{:S(2)}) collective-permute-start(bf16[2,2,2,1,1,8,512]{6,5,4,3,2,1,0:T(8,128)(2,1)S(1)} %get-tuple-element.19), channel_id=1, source_target_pairs={{0,4},{1,5},{2,6},{3,7},{4,0},{5,1},{6,2},{7,3},{8,12},{9,13},{10,... | collective-permute-start | bytes 196616 | tf_op jit(solution)/shard_map/ppermute | solution.py:179
  63.9 17.5 %collective-permute-start.5 = (bf16[2,2,2,1,1,8,512]{6,5,4,3,2,1,0:T(8,128)(2,1)S(1)}, bf16[2,2,2,1,1,8,512]{6,5,4,3,2,1,0:T(8,128)(2,1)S(1)}, u32[]{:S(2)}, u32[]{:S(2)}) collective-permute-start(bf16[2,2,2,1,1,8,512]{6,5,4,3,2,1,0:T(8,128)(2,1)S(1)} %get-tuple-element.17), channel_id=1, source_target_pairs={{0,6},{1,7},{2,4},{3,5},{4,2},{5,3},{6,0},{7,1},{8,14},{9,15},{10,... | collective-permute-start | bytes 196616 | tf_op jit(solution)/shard_map/ppermute | solution.py:179
  81.4 2.9 %copy-start = (bf16[512,1024]{1,0:T(8,128)(2,1)S(1)}, bf16[512,1024]{1,0:T(8,128)(2,1)}, u32[]{:S(2)}) copy-start(bf16[512,1024]{1,0:T(8,128)(2,1)} %output_ref.7) | copy-start | bytes 3145732
  81.4 24.8 %all-to-all-start.2 = ((bf16[32,3,8,512]{3,2,1,0:T(8,128)(2,1)}), bf16[32,3,8,512]{3,2,1,0:T(8,128)(2,1)S(1)}, u32[]{:S(2)}, u32[]{:S(2)}) async-start(bf16[32,3,8,512]{3,2,1,0:T(8,128)(2,1)} %after.1), calls=%async_computation.2 | async-start | bytes 1572864 | tf_op jit(solution)/shard_map/all_to_all | solution.py:151
  84.2 21.9 %copy-start.1 = (bf16[3,256,1024]{2,1,0:T(8,128)(2,1)S(1)}, bf16[3,256,1024]{2,1,0:T(8,128)(2,1)}, u32[]{:S(2)}) copy-start(bf16[3,256,1024]{2,1,0:T(8,128)(2,1)} %get-tuple-element.12.mixed_ref) | copy-start | bytes 4718596
  84.2 1.2 %copy-start.2 = (bf16[1,256,1024]{2,1,0:T(8,128)(2,1)S(1)}, bf16[1,256,1024]{2,1,0:T(8,128)(2,1)}, u32[]{:S(2)}) copy-start(bf16[1,256,1024]{2,1,0:T(8,128)(2,1)} %get-tuple-element.11.refs_0_.mixed_ref) | copy-start | bytes 1572868

commit v3 on v2

--- a/solution.py
+++ b/solution.py
@@ -13,6 +13,8 @@
 LANES = 128
 EPSILON = 1e-06
 MASKED = -1e30
+SPLIT = 2
+PIECES = 3
 ANYWHERE = pl.BlockSpec(memory_space=pl.ANY)
 AXES = ("grp", "dev")
 VMEM_LIMIT = 60 * 1024 * 1024
@@ -53,9 +55,7 @@
 def bit_groups():
     inner = lax.axis_size("dev").bit_length() - 1
     bits = inner + lax.axis_size("grp").bit_length() - 1
-    far = [tuple(reversed(range(1, inner)))]
-    near = [(0,), *((bit,) for bit in reversed(range(inner, bits)))]
-    return near + far
+    return [(inner,), (0, *reversed(range(inner + 1, bits))), tuple(reversed(range(1, inner)))]
 
 
 def mask_of(index, group):
@@ -87,8 +87,9 @@
     return jnp.stack(parts)
 
 
-def space_kernel(video_ref, gain_ref, project_ref, output_ref, time_gain_ref, *refs):
-    mixed_ref, sent_ref = refs[-2:]
+def space_kernel(groups, extra, video_ref, gain_ref, project_ref, output_ref, time_gain_ref, *refs):
+    mixed_ref, *sent_refs = refs[extra:]
+    sent_refs, scratch = (sent_refs, None) if groups is None else (sent_refs[:-1], sent_refs[-1])
     floats = video_ref[0].astype(jnp.float32)
     heads = jnp.dot(
         normed(floats, gain_ref[...]).astype(jnp.bfloat16), project_ref[...], preferred_element_type=jnp.float32
@@ -97,10 +98,11 @@
     mixed = (floats + jnp.dot(context, output_ref[...], preferred_element_type=jnp.float32)).astype(jnp.bfloat16)
     mixed_ref[0] = mixed
     sent = normed(mixed.astype(jnp.float32), time_gain_ref[...])
-    sent_ref[...] = sent.reshape(sent_ref.shape).astype(jnp.bfloat16)
-
-
-def time_kernel(back, extra, patch_here, rows_ref, project_ref, *refs):
+    shape = sent_refs[0].shape if groups is None else scratch.shape
+    put(sent.reshape(shape).astype(jnp.bfloat16), scratch, sent_refs, groups)
+
+
+def time_kernel(groups, back, extra, patch_here, rows_ref, project_ref, *refs):
     *context_refs, bias_ref = refs[extra:]
     context_refs, scratch = (context_refs, None) if back is None else (context_refs[:-1], context_refs[-1])
     rows, width = bias_ref.shape[0], rows_ref.shape[-1]
@@ -112,11 +114,47 @@
         seen = (key <= query) & (lax.rem(query, patch_here) == lax.rem(key, patch_here))
         bias_ref[...] = jnp.where(seen, 0.0, MASKED)
 
-    arrived = rows_ref[...].astype(jnp.float32).reshape(rows, width).astype(jnp.bfloat16)
+    arrived = take(rows_ref, groups).astype(jnp.float32).reshape(rows, width).astype(jnp.bfloat16)
     heads = jnp.dot(arrived, project_ref[...], preferred_element_type=jnp.float32).astype(jnp.bfloat16)
     context = attend(heads, bias_ref[...]).astype(jnp.float32)
     shape = context_refs[0].shape if back is None else scratch.shape
     put(context.reshape(shape).astype(jnp.bfloat16), scratch, context_refs, back)
+
+
+def time_wide_kernel(
+    patch_here, rows_ref, project_ref, before_ref, context_ref, bias_ref, project, heads, contexts, weight_sems, out_sems
+):
+    clips, rows, width = heads.shape[0], bias_ref.shape[0], rows_ref.shape[-1]
+    tile = heads.shape[2] // weight_sems.shape[0]
+
+    def columns(piece):
+        return pl.ds(piece * tile, tile)
+
+    def leaving(clip):
+        return pltpu.make_async_copy(contexts.at[clip], context_ref.at[:, clip], out_sems.at[clip])
+
+    weights = [
+        pltpu.make_async_copy(project_ref.at[:, columns(piece)], project.at[:, columns(piece)], weight_sems.at[piece])
+        for piece in range(weight_sems.shape[0])
+    ]
+    for copy in weights:
+        copy.start()
+    query = lax.broadcasted_iota(jnp.int32, (rows, rows), 0)
+    key = lax.broadcasted_iota(jnp.int32, (rows, rows), 1)
+    seen = (key <= query) & (lax.rem(query, patch_here) == lax.rem(key, patch_here))
+    bias_ref[...] = jnp.where(seen, 0.0, MASKED)
+    arrived = [rows_ref[:, clip].astype(jnp.float32).reshape(rows, width).astype(jnp.bfloat16) for clip in range(clips)]
+    for piece, copy in enumerate(weights):
+        copy.wait()
+        for at, one in enumerate(arrived):
+            got = jnp.dot(one, project[:, columns(piece)], preferred_element_type=jnp.float32).astype(jnp.bfloat16)
+            heads[at, :, columns(piece)] = got
+    for clip in range(clips):
+        context = attend(heads[clip], bias_ref[...])
+        contexts[clip] = context.astype(jnp.float32).reshape(contexts.shape[1:]).astype(jnp.bfloat16)
+        leaving(clip).start()
+    for clip in range(clips):
+        leaving(clip).wait()
 
 
 def final_kernel(order, mixed_ref, context_ref, output_ref, *refs):
@@ -125,6 +163,28 @@
     context = take(context_ref, order).astype(jnp.float32).reshape(rows, WIDTH).astype(jnp.bfloat16)
     update = jnp.dot(context, output_ref[...], preferred_element_type=jnp.float32)
     out_ref[0] = (mixed_ref[0].astype(jnp.float32) + update).astype(jnp.bfloat16)
+
+
+def final_wide_kernel(first, mixed_ref, context_ref, output_ref, before_ref, out_ref, done, sems):
+    clips, rows, _ = mixed_ref.shape
+    part = rows // SPLIT
+    copies = []
+    for clip in range(clips):
+        context = context_ref[:, clip].astype(jnp.float32).reshape(rows, WIDTH).astype(jnp.bfloat16)
+        for at in range(SPLIT):
+            here = slice(at * part, (at + 1) * part)
+            update = jnp.dot(context[here], output_ref[...], preferred_element_type=jnp.float32)
+            done[clip, here] = (mixed_ref[clip, here].astype(jnp.float32) + update).astype(jnp.bfloat16)
+            copies.append(
+                pltpu.make_async_copy(
+                    done.at[clip, pl.ds(at * part, part)],
+                    out_ref.at[first + clip, pl.ds(at * part, part)],
+                    sems.at[clip, at],
+                )
+            )
+            copies[-1].start()
+    for copy in copies:
+        copy.wait()
 
 
 def whole(shape):
@@ -167,10 +227,11 @@
         input_output_aliases={0: 0},
         compiler_params=pltpu.CompilerParams(vmem_limit_bytes=2 * 1024 * 1024),
         name="after",
-    )(rows, *awaited)
+    )(in_hbm(rows), *awaited)
 
 
 def swap(blocks, groups):
+    steps = []
     devices = 1 << len(sum(groups, ()))
     rows = blocks[0].shape[1:]
     blocks = [block.reshape(1, *(1 << len(group) for group in groups[1:]), *rows) for block in blocks]
@@ -180,12 +241,11 @@
             for index, block in enumerate(blocks)
             if index
         ]
-        if len(group) > 1:
-            awaited = arrived
+        steps.append(arrived)
         whole_buffer = jnp.concatenate([blocks[0], *arrived], axis=at)
         if at + 1 < len(groups):
             blocks = jnp.split(whole_buffer, 1 << len(groups[at + 1]), axis=at + 1)
-    return whole_buffer.reshape(devices, *rows), awaited
+    return whole_buffer.reshape(devices, *rows), steps
 
 
 def cost(macs, bytes_accessed, exps):
@@ -201,10 +261,11 @@
     return [shape] * parts, [spec] * parts, [pltpu.VMEM((count, patch_here, width), jnp.bfloat16)]
 
 
-def space_call(video, first, clips, space_gain, space_project, space_output, time_gain, count, before):
+def space_call(video, first, clips, space_gain, space_project, space_output, time_gain, count, before, groups):
     rows, width = video.shape[1:]
-    return pl.pallas_call(
-        space_kernel,
+    shapes, specs, scratch = sent_specs(count, clips, rows // count, width, groups)
+    mixed, *sent = pl.pallas_call(
+        partial(space_kernel, groups, len(before)),
         grid=(clips,),
         in_specs=[
             pl.BlockSpec((1, rows, width), lambda c: (first + c, 0, 0)),
@@ -214,8 +275,9 @@
             whole((1, width)),
         ]
         + [ANYWHERE] * len(before),
-        out_specs=[pl.BlockSpec((1, rows, width), lambda c: (c, 0, 0)), exchange_spec(count, rows // count, width)],
-        out_shape=[jax.ShapeDtypeStruct((clips, rows, width), jnp.bfloat16), exchange_shape(count, clips, rows // count, width)],
+        out_specs=[pl.BlockSpec((1, rows, width), lambda c: (c, 0, 0)), *specs],
+        out_shape=[jax.ShapeDtypeStruct((clips, rows, width), jnp.bfloat16), *shapes],
+        scratch_shapes=scratch,
         cost_estimate=cost(
             clips * rows * (width * 4 * WIDTH + 8 * rows * WIDTH), 2 * (4 * width * WIDTH + 3 * clips * rows * width),
             clips * HEADS * rows * rows,
@@ -223,14 +285,15 @@
         compiler_params=pltpu.CompilerParams(vmem_limit_bytes=VMEM_LIMIT),
         name="space",
     )(video, space_gain, space_project, space_output, time_gain, *map(in_hbm, before))
-
-
-def time_call(arrived, clips, rows, time_project, count, before, back):
+    return mixed, sent
+
+
+def time_call(arrived, clips, rows, time_project, count, before, groups, back):
     width = arrived.shape[-1]
     patch_here = rows // count
     shapes, specs, scratch = sent_specs(count, clips, patch_here, WIDTH, back)
     return pl.pallas_call(
-        partial(time_kernel, back, len(before), patch_here),
+        partial(time_kernel, groups, back, len(before), patch_here),
         grid=(clips,),
         in_specs=[exchange_spec(count, patch_here, width), whole((width, 3 * WIDTH))] + [ANYWHERE] * len(before),
         out_specs=specs,
@@ -243,6 +306,31 @@
         compiler_params=pltpu.CompilerParams(vmem_limit_bytes=TIME_VMEM_LIMIT),
         name="time",
     )(arrived, in_hbm(time_project), *map(in_hbm, before))
+
+
+def time_wide_call(arrived, clips, rows, time_project, count, before):
+    width = arrived.shape[-1]
+    patch_here = rows // count
+    return pl.pallas_call(
+        partial(time_wide_kernel, patch_here),
+        in_specs=[pl.BlockSpec(memory_space=pltpu.VMEM), ANYWHERE, ANYWHERE],
+        out_specs=ANYWHERE,
+        out_shape=pltpu.HBM((count, clips, patch_here, WIDTH), jnp.bfloat16),
+        scratch_shapes=[
+            pltpu.VMEM((rows, rows), jnp.float32),
+            pltpu.VMEM((width, 3 * WIDTH), jnp.bfloat16),
+            pltpu.VMEM((clips, rows, 3 * WIDTH), jnp.bfloat16),
+            pltpu.VMEM((clips, count, patch_here, WIDTH), jnp.bfloat16),
+            pltpu.SemaphoreType.DMA((PIECES,)),
+            pltpu.SemaphoreType.DMA((clips,)),
+        ],
+        cost_estimate=cost(
+            clips * rows * (width * 3 * WIDTH + 8 * rows * WIDTH), 2 * (3 * width * WIDTH + 2 * clips * rows * width),
+            clips * HEADS * rows * rows,
+        ),
+        compiler_params=pltpu.CompilerParams(vmem_limit_bytes=TIME_VMEM_LIMIT),
+        name="time",
+    )(arrived, in_hbm(time_project), in_hbm(before))
 
 
 def final_call(mixed, context, time_output, count, first, total, before, order):
@@ -265,6 +353,22 @@
     )(mixed, context, time_output, *before)
 
 
+def final_wide_call(mixed, context, time_output, first, total, before):
+    clips, rows, width = mixed.shape
+    vmem = pl.BlockSpec(memory_space=pltpu.VMEM)
+    return pl.pallas_call(
+        partial(final_wide_kernel, first),
+        in_specs=[vmem, vmem, vmem, ANYWHERE],
+        out_specs=ANYWHERE,
+        out_shape=jax.ShapeDtypeStruct((total, rows, width), jnp.bfloat16),
+        scratch_shapes=[pltpu.VMEM((clips, rows, width), jnp.bfloat16), pltpu.SemaphoreType.DMA((clips, SPLIT))],
+        input_output_aliases={3: 0},
+        cost_estimate=cost(clips * rows * width * WIDTH, 2 * (width * WIDTH + 3 * clips * rows * width), 0),
+        compiler_params=pltpu.CompilerParams(vmem_limit_bytes=FINAL_VMEM_LIMIT),
+        name="final",
+    )(mixed, context, time_output, before)
+
+
 def per_device(video_in, space_gain, space_project, space_output, time_gain, time_project, time_output):
     clip_count, frame_local, patch_count, width = video_in.shape
     count = lax.axis_size("grp") * lax.axis_size("dev")
@@ -272,23 +376,31 @@
     video = video_in.reshape(clip_count, patch_count, width)
     weights = space_gain.reshape(1, width), space_project, space_output, time_gain.reshape(1, width)
     swappable = patch_here % 8 == 0 and count & (count - 1) == 0
-    back = bit_groups() if swappable else None
-    chunks = [(0, 1), (1, clip_count - 1)]
-    mixed, arrived, out = [], [], []
-    for first, clips in chunks:
-        kept, sent = space_call(video, first, clips, *weights, count, mixed)
-        mixed.append(kept)
-        arrived.append(exchange(sent, count, patch_here))
-    context = time_call(arrived[0], 1, patch_count, time_project, count, [], back)
-    if swappable:
-        early, awaited = swap(context, back)
-    else:
-        early, awaited = exchange(context[0], count, patch_here), []
-    context = time_call(arrived[1], clip_count - 1, patch_count, time_project, count, context[:1], None)
-    late = exchange(after(context[0], awaited) if awaited else context[0], count, patch_here)
-    for (first, _), kept, context, groups in zip(chunks, mixed, (early, late), (back, None)):
-        out = [final_call(kept, context, time_output, count, first, clip_count, out, groups)]
-    return out[0].reshape(clip_count, frame_local, patch_count, width)
+    if not swappable:
+        return plainly(video, weights, time_project, time_output, count).reshape(video_in.shape)
+    others = clip_count - 1
+    back = bit_groups()
+    there = [back[2], back[0], back[1]]
+    kept, sent = space_call(video, 0, 1, *weights, count, [], there)
+    kept_others, sent_others = space_call(video, 1, others, *weights, count, [kept], None)
+    arrived, steps = swap(sent, there)
+    arrived_others = exchange(after(sent_others[0], steps[0]), count, patch_here)
+    context = time_call(arrived, 1, patch_count, time_project, count, [], there, back)
+    returned, steps = swap(context, back)
+    context = time_wide_call(arrived_others, others, patch_count, time_project, count, context[0])
+    returned_others = exchange(after(context, steps[-1]), count, patch_here)
+    out = final_call(kept, returned, time_output, count, 0, clip_count, [], back)
+    out = final_wide_call(kept_others, returned_others, time_output, 1, clip_count, out)
+    return out.reshape(clip_count, frame_local, patch_count, width)
+
+
+def plainly(video, weights, time_project, time_output, count):
+    clips, rows, _ = video.shape
+    kept, sent = space_call(video, 0, clips, *weights, count, [], None)
+    arrived = exchange(sent[0], count, rows // count)
+    context = time_call(arrived, clips, rows, time_project, count, [], None, None)
+    returned = exchange(context[0], count, rows // count)
+    return final_call(kept, returned, time_output, count, 0, clips, [], None)
 
 
 def solution(mesh):

time: 109 us -> 104 us (0.954)
  waiting for transfers between devices: 55.5 us -> 44.6 us
  starting transfers between devices: 20.5 us -> 27.9 us
  Pallas kernels: 31.2 us -> 29.9 us
    all_to_all x3 -> x2, waiting for transfers between devices: 34.3 us -> 19.4 us  [exchange(): lax.all_to_all(sent, AXES, split_axis=0, concat_axis=0, tiled=True)]
    ppermute x6 -> x14, starting transfers between devices: 7.78 us -> 17.6 us  [swap(): lax.ppermute(block, AXES, [(device, device ^ mask_of(index, group)) for d...]
    ppermute x6 -> x14, waiting for transfers between devices: 21.3 us -> 25.1 us  [swap(): lax.ppermute(block, AXES, [(device, device ^ mask_of(index, group)) for d...]
    pallas_call x2 -> x1, Pallas kernels: 3.84 us -> 1.32 us  [final_call(): pl.pallas_call(partial(final_kernel, order), grid=(clips,), in_specs=[pl....]
    all_to_all x3 -> x2, starting transfers between devices: 12.8 us -> 10.3 us  [exchange(): lax.all_to_all(sent, AXES, split_axis=0, concat_axis=0, tiled=True)]
    pallas_call x4 -> x5, Pallas kernels: 27.4 us -> 28.5 us  [the longest x2 16 us: space_call(): pl.pallas_call(partial(space_kernel, groups, len(before)), grid=(clips,),...]
  transfers between devices with their start and end apart: 9 -> 16, of which waited for: 6 -> 9; matrix products, arithmetic and copies ran while one was open for 0% -> 0% of each run, Pallas kernels for 21% -> 22%
where the time goes in v3:
time: 104 us
  waiting for transfers between devices  44.6 us (43%)
  Pallas kernels  29.9 us (29%)
  starting transfers between devices  27.9 us (27%)
  local copies, waits for them, and re-layouts  1.23 us (1%)
    ppermute x14, waiting for transfers between devices, swap(): lax.ppermute(block, AXES, [(device, device ^ mask_of(index, group)) for d...  25.1 us
    all_to_all x2, waiting for transfers between devices, exchange(): lax.all_to_all(sent, AXES, split_axis=0, concat_axis=0, tiled=True)  19.4 us
    ppermute x14, starting transfers between devices, swap(): lax.ppermute(block, AXES, [(device, device ^ mask_of(index, group)) for d...  17.6 us
    pallas_call x2, Pallas kernels, space_call(): pl.pallas_call(partial(space_kernel, groups, len(before)), grid=(clips,),...  16 us
    all_to_all x2, starting transfers between devices, exchange(): lax.all_to_all(sent, AXES, split_axis=0, concat_axis=0, tiled=True)  10.3 us
    pallas_call x1, Pallas kernels, time_wide_call(): pl.pallas_call(partial(time_wide_kernel, patch_here), in_specs=[pl.BlockS...  7.09 us
    pallas_call x1, Pallas kernels, time_call(): pl.pallas_call(partial(time_kernel, groups, back, len(before), patch_here...  3.69 us
  transfers between devices with their start and end apart: 16, of which 9 were waited for; matrix products, arithmetic and copies ran while one was open for 0% of the time, Pallas kernels for 22%

profile of v3, /device:TPU:0, one launch (start us, length us, event | category | flops | bytes accessed | tf_op | source)
XLA Modules:
  0.0 104.0 jit_solution(2146954706614513784)
XLA Ops:
  0.0 5.6 %space.2 = (bf16[1,256,1024]{2,1,0:T(8,128)(2,1)}, bf16[8,1,8,1024]{3,2,1,0:T(8,128)(2,1)}, bf16[8,1,8,1024]{3,2,1,0:T(8,128)(2,1)}, bf16[8,1,8,1024]{3,2,1,0:T(8,128)(2,1)}, bf16[8,1,8,1024]{3,2,1,0:T(8,128)(2,1)}) custom-call(bf16[4,256,1024]{2,1,0:T(8,128)(2,1)} %bitcast.18, f32[1,1024]{1,0:T(1,128)} %bitcast.21, bf16[1024,1536]{1,0:T(8,128)(2,1)} %project_ref.5, ...), custom_call_target="tpu_custom_call" | custom-call | flops 1610612736 | bytes 5767168 | tf_op jit(solution)/shard_map/space/pallas_call | solution.py:267
  5.6 3.0 %collective-permute-start = (bf16[1,2,4,1,8,1024]{5,4,3,2,1,0:T(8,128)(2,1)}, bf16[1,2,4,1,8,1024]{5,4,3,2,1,0:T(8,128)(2,1)S(1)}, u32[]{:S(2)}, u32[]{:S(2)}) collective-permute-start(bf16[1,2,4,1,8,1024]{5,4,3,2,1,0:T(8,128)(2,1)} %bitcast.27), channel_id=1, source_target_pairs={{0,2},{1,3},{2,0},{3,1},{4,6},{5,7},{6,4},{7,5},{8,10},{9,11},{10,... | collective-permute-start | bytes 393224 | tf_op jit(solution)/shard_map/ppermute | solution.py:240
  8.6 2.6 %collective-permute-start.1 = (bf16[1,2,4,1,8,1024]{5,4,3,2,1,0:T(8,128)(2,1)}, bf16[1,2,4,1,8,1024]{5,4,3,2,1,0:T(8,128)(2,1)S(1)}, u32[]{:S(2)}, u32[]{:S(2)}) collective-permute-start(bf16[1,2,4,1,8,1024]{5,4,3,2,1,0:T(8,128)(2,1)} %bitcast.26), channel_id=1, source_target_pairs={{0,4},{1,5},{2,6},{3,7},{4,0},{5,1},{6,2},{7,3},{8,12},{9,13},{10,... | collective-permute-start | bytes 393224 | tf_op jit(solution)/shard_map/ppermute | solution.py:240
  11.2 10.4 %space.3 = (bf16[3,256,1024]{2,1,0:T(8,128)(2,1)}, bf16[32,3,8,1024]{3,2,1,0:T(8,128)(2,1)}) custom-call(bf16[4,256,1024]{2,1,0:T(8,128)(2,1)} %bitcast.19, f32[1,1024]{1,0:T(1,128)} %bitcast.22, bf16[1024,1536]{1,0:T(8,128)(2,1)} %project_ref.5, bf16[512,1024]{1,0:T(8,128)(2,1)} %output_ref.5, f32[1,1024]{1,0:T(1,128)} %bitcast.24, ...), custom_call_target="tpu_custom_call" | custom-call | flops 4831838208 | bytes 8912896 | tf_op jit(solution)/shard_map/space/pallas_call | solution.py:267
  21.6 0.1 collective-permute-done.1.refs_2_
  21.8 6.0 %all-to-all-start = ((bf16[32,3,8,1024]{3,2,1,0:T(8,128)(2,1)}), bf16[32,3,8,1024]{3,2,1,0:T(8,128)(2,1)S(1)}, u32[]{:S(2)}, u32[]{:S(2)}) async-start(bf16[32,3,8,1024]{3,2,1,0:T(8,128)(2,1)} %after.2), calls=%async_computation | async-start | bytes 3145728 | tf_op jit(solution)/shard_map/all_to_all | solution.py:211
  27.7 0.1 pad_maximum_fusion
  27.9 0.3 collective-permute-start.3
  28.2 1.3 %collective-permute-done.3 = bf16[4,1,4,1,8,1024]{5,4,3,2,1,0:T(8,128)(2,1)S(1)} collective-permute-done((bf16[4,1,4,1,8,1024]{5,4,3,2,1,0:T(8,128)(2,1)S(1)}, bf16[4,1,4,1,8,1024]{5,4,3,2,1,0:T(8,128)(2,1)S(1)}, u32[]{:S(2)}, u32[]{:S(2)}) %collective-permute-start.3) | collective-permute-done | bytes 262176 | tf_op jit(solution)/shard_map/ppermute | solution.py:240
  29.5 2.7 %collective-permute-start.6 = (bf16[4,2,1,1,8,1024]{5,4,3,2,1,0:T(8,128)(2,1)S(1)}, bf16[4,2,1,1,8,1024]{5,4,3,2,1,0:T(8,128)(2,1)S(1)}, u32[]{:S(2)}, u32[]{:S(2)}) collective-permute-start(bf16[4,2,1,1,8,1024]{5,4,3,2,1,0:T(8,128)(2,1)S(1)} %get-tuple-element.25), channel_id=1, source_target_pairs={{0,17},{1,16},{2,19},{3,18},{4,21},{5,20},{6,23},{7,22},{8,25},{9,... | collective-permute-start | bytes 393224 | tf_op jit(solution)/shard_map/ppermute | solution.py:240
  32.2 0.6 collective-permute-start.5
  32.8 0.3 collective-permute-start.4
  33.1 17.4 %collective-permute-done.6 = bf16[4,2,1,1,8,1024]{5,4,3,2,1,0:T(8,128)(2,1)S(1)} collective-permute-done((bf16[4,2,1,1,8,1024]{5,4,3,2,1,0:T(8,128)(2,1)S(1)}, bf16[4,2,1,1,8,1024]{5,4,3,2,1,0:T(8,128)(2,1)S(1)}, u32[]{:S(2)}, u32[]{:S(2)}) %collective-permute-start.6) | collective-permute-done | bytes 131104 | tf_op jit(solution)/shard_map/ppermute | solution.py:240
  50.5 1.2 %collective-permute-done.5 = bf16[4,2,1,1,8,1024]{5,4,3,2,1,0:T(8,128)(2,1)S(1)} collective-permute-done((bf16[4,2,1,1,8,1024]{5,4,3,2,1,0:T(8,128)(2,1)S(1)}, bf16[4,2,1,1,8,1024]{5,4,3,2,1,0:T(8,128)(2,1)S(1)}, u32[]{:S(2)}, u32[]{:S(2)}) %collective-permute-start.5) | collective-permute-done | bytes 131104 | tf_op jit(solution)/shard_map/ppermute | solution.py:240
  51.8 3.7 %time.2 = (bf16[16,1,8,512]{3,2,1,0:T(8,128)(2,1)S(1)}, bf16[16,1,8,512]{3,2,1,0:T(8,128)(2,1)S(1)}) custom-call(bf16[32,1,8,1024]{3,2,1,0:T(8,128)(2,1)S(1)} %bitcast.15, bf16[1024,1536]{1,0:T(8,128)(2,1)} %project_ref.7), custom_call_target="tpu_custom_call" | custom-call | flops 1342177280 | bytes 4194304 | tf_op jit(solution)/shard_map/time/pallas_call | solution.py:295
  55.5 0.1 collective-permute-start.7
  55.6 1.3 %collective-permute-done.7 = bf16[1,4,4,1,8,512]{5,4,3,2,1,0:T(8,128)(2,1)S(1)} collective-permute-done((bf16[1,4,4,1,8,512]{5,4,3,2,1,0:T(8,128)(2,1)S(1)}, bf16[1,4,4,1,8,512]{5,4,3,2,1,0:T(8,128)(2,1)S(1)}, u32[]{:S(2)}, u32[]{:S(2)}) %collective-permute-start.7) | collective-permute-done | bytes 131104 | tf_op jit(solution)/shard_map/ppermute | solution.py:240
  57.0 0.5 collective-permute-start.10
  57.5 2.5 %collective-permute-start.9 = (bf16[2,1,4,1,8,512]{5,4,3,2,1,0:T(8,128)(2,1)S(1)}, bf16[2,1,4,1,8,512]{5,4,3,2,1,0:T(8,128)(2,1)S(1)}, u32[]{:S(2)}, u32[]{:S(2)}) collective-permute-start(bf16[2,1,4,1,8,512]{5,4,3,2,1,0:T(8,128)(2,1)S(1)} %get-tuple-element.36), channel_id=1, source_target_pairs={{0,1},{1,0},{2,3},{3,2},{4,5},{5,4},{6,7},{7,6},{8,9},{9,8},{10,11... | collective-permute-start | bytes 196616 | tf_op jit(solution)/shard_map/ppermute | solution.py:240
  59.9 0.6 collective-permute-start.8
  60.5 2.4 %collective-permute-done.10 = bf16[2,1,4,1,8,512]{5,4,3,2,1,0:T(8,128)(2,1)S(1)} collective-permute-done((bf16[2,1,4,1,8,512]{5,4,3,2,1,0:T(8,128)(2,1)S(1)}, bf16[2,1,4,1,8,512]{5,4,3,2,1,0:T(8,128)(2,1)S(1)}, u32[]{:S(2)}, u32[]{:S(2)}) %collective-permute-start.10) | collective-permute-done | bytes 65568 | tf_op jit(solution)/shard_map/ppermute | solution.py:240
  62.9 0.6 collective-permute-done.9
  63.5 0.7 collective-permute-done.8
  64.3 1.2 %collective-permute-start.11 = (bf16[2,4,1,1,8,512]{5,4,3,2,1,0:T(8,128)(2,1)S(1)}, bf16[2,4,1,1,8,512]{5,4,3,2,1,0:T(8,128)(2,1)S(1)}, u32[]{:S(2)}, u32[]{:S(2)}) collective-permute-start(bf16[2,4,1,1,8,512]{5,4,3,2,1,0:T(8,128)(2,1)S(1)} %get-tuple-element.32), channel_id=1, source_target_pairs={{0,2},{1,3},{2,0},{3,1},{4,6},{5,7},{6,4},{7,5},{8,10},{9,11},{10,... | collective-permute-start | bytes 196616 | tf_op jit(solution)/shard_map/ppermute | solution.py:240
  65.5 1.4 %collective-permute-start.12 = (bf16[2,4,1,1,8,512]{5,4,3,2,1,0:T(8,128)(2,1)S(1)}, bf16[2,4,1,1,8,512]{5,4,3,2,1,0:T(8,128)(2,1)S(1)}, u32[]{:S(2)}, u32[]{:S(2)}) collective-permute-start(bf16[2,4,1,1,8,512]{5,4,3,2,1,0:T(8,128)(2,1)S(1)} %get-tuple-element.31), channel_id=1, source_target_pairs={{0,4},{1,5},{2,6},{3,7},{4,0},{5,1},{6,2},{7,3},{8,12},{9,13},{10,... | collective-permute-start | bytes 196616 | tf_op jit(solution)/shard_map/ppermute | solution.py:240
  66.9 1.8 %collective-permute-start.13 = (bf16[2,4,1,1,8,512]{5,4,3,2,1,0:T(8,128)(2,1)S(1)}, bf16[2,4,1,1,8,512]{5,4,3,2,1,0:T(8,128)(2,1)S(1)}, u32[]{:S(2)}, u32[]{:S(2)}) collective-permute-start(bf16[2,4,1,1,8,512]{5,4,3,2,1,0:T(8,128)(2,1)S(1)} %get-tuple-element.30), channel_id=1, source_target_pairs={{0,6},{1,7},{2,4},{3,5},{4,2},{5,3},{6,0},{7,1},{8,14},{9,15},{10,... | collective-permute-start | bytes 196616 | tf_op jit(solution)/shard_map/ppermute | solution.py:240
  68.7 7.1 %time.3.refs_0_ = bf16[32,3,8,512]{3,2,1,0:T(8,128)(2,1)} custom-call(bf16[32,3,8,1024]{3,2,1,0:T(8,128)(2,1)S(1)} %all-to-all-done.rows_ref, bf16[1024,1536]{1,0:T(8,128)(2,1)} %project_ref.7, bf16[16,1,8,512]{3,2,1,0:T(8,128)(2,1)} %copy-done.3), custom_call_target="tpu_custom_call" | custom-call | flops 4026531840 | bytes 6291456 | tf_op jit(solution)/shard_map/time/pallas_call | solution.py:314
  75.9 4.3 %all-to-all-start.1 = ((bf16[32,3,8,512]{3,2,1,0:T(8,128)(2,1)}), bf16[32,3,8,512]{3,2,1,0:T(8,128)(2,1)S(1)}, u32[]{:S(2)}, u32[]{:S(2)}) async-start(bf16[32,3,8,512]{3,2,1,0:T(8,128)(2,1)} %after.3), calls=%async_computation.1 | async-start | bytes 1572864 | tf_op jit(solution)/shard_map/all_to_all | solution.py:211
  80.3 1.1 %copy-done.2 = bf16[1,256,1024]{2,1,0:T(8,128)(2,1)S(1)} copy-done((bf16[1,256,1024]{2,1,0:T(8,128)(2,1)S(1)}, bf16[1,256,1024]{2,1,0:T(8,128)(2,1)}, u32[]{:S(2)}) %copy-start.2) | copy-done | bytes 524312
  81.4 1.3 %final.2.before_ref = bf16[4,256,1024]{2,1,0:T(8,128)(2,1)} custom-call(bf16[1,256,1024]{2,1,0:T(8,128)(2,1)S(1)} %copy-done.2, bf16[32,1,8,512]{3,2,1,0:T(8,128)(2,1)S(1)} %bitcast.14, bf16[512,1024]{1,0:T(8,128)(2,1)S(1)} %copy-done), custom_call_target="tpu_custom_call" | custom-call | flops 268435456 | bytes 2621440 | tf_op jit(solution)/shard_map/final/pallas_call | solution.py:338
  82.8 19.4 %all-to-all-done.1.context_ref = bf16[32,3,8,512]{3,2,1,0:T(8,128)(2,1)S(1)} async-done(((bf16[32,3,8,512]{3,2,1,0:T(8,128)(2,1)}), bf16[32,3,8,512]{3,2,1,0:T(8,128)(2,1)S(1)}, u32[]{:S(2)}, u32[]{:S(2)}) %all-to-all-start.1) | async-done | bytes 786464 | tf_op jit(solution)/shard_map/all_to_all | solution.py:211
  102.2 1.8 %final.3 = bf16[4,256,1024]{2,1,0:T(8,128)(2,1)} custom-call(bf16[3,256,1024]{2,1,0:T(8,128)(2,1)S(1)} %copy-done.1, bf16[32,3,8,512]{3,2,1,0:T(8,128)(2,1)S(1)} %all-to-all-done.1.context_ref, bf16[512,1024]{1,0:T(8,128)(2,1)S(1)} %copy-done, bf16[4,256,1024]{2,1,0:T(8,128)(2,1)} %final.2.before_ref), custom_call_target="tpu_custom_call", output_to_operand_aliasing={{}: (3, {})} | custom-call | flops 805306368 | bytes 5767168 | tf_op jit(solution)/shard_map/final/pallas_call | solution.py:359
  (26 shorter events, 0.3 us)
Async XLA Ops:
  5.6 16.0 %collective-permute-start = (bf16[1,2,4,1,8,1024]{5,4,3,2,1,0:T(8,128)(2,1)}, bf16[1,2,4,1,8,1024]{5,4,3,2,1,0:T(8,128)(2,1)S(1)}, u32[]{:S(2)}, u32[]{:S(2)}) collective-permute-start(bf16[1,2,4,1,8,1024]{5,4,3,2,1,0:T(8,128)(2,1)} %bitcast.27), channel_id=1, source_target_pairs={{0,2},{1,3},{2,0},{3,1},{4,6},{5,7},{6,4},{7,5},{8,10},{9,11},{10,... | collective-permute-start | bytes 393224 | tf_op jit(solution)/shard_map/ppermute | solution.py:240
  8.6 13.1 %collective-permute-start.1 = (bf16[1,2,4,1,8,1024]{5,4,3,2,1,0:T(8,128)(2,1)}, bf16[1,2,4,1,8,1024]{5,4,3,2,1,0:T(8,128)(2,1)S(1)}, u32[]{:S(2)}, u32[]{:S(2)}) collective-permute-start(bf16[1,2,4,1,8,1024]{5,4,3,2,1,0:T(8,128)(2,1)} %bitcast.26), channel_id=1, source_target_pairs={{0,4},{1,5},{2,6},{3,7},{4,0},{5,1},{6,2},{7,3},{8,12},{9,13},{10,... | collective-permute-start | bytes 393224 | tf_op jit(solution)/shard_map/ppermute | solution.py:240
  11.2 10.5 %collective-permute-start.2 = (bf16[1,2,4,1,8,1024]{5,4,3,2,1,0:T(8,128)(2,1)}, bf16[1,2,4,1,8,1024]{5,4,3,2,1,0:T(8,128)(2,1)S(1)}, u32[]{:S(2)}, u32[]{:S(2)}) collective-permute-start(bf16[1,2,4,1,8,1024]{5,4,3,2,1,0:T(8,128)(2,1)} %bitcast.25), channel_id=1, source_target_pairs={{0,6},{1,7},{2,4},{3,5},{4,2},{5,3},{6,0},{7,1},{8,14},{9,15},{10,... | collective-permute-start | bytes 393224 | tf_op jit(solution)/shard_map/ppermute | solution.py:240
  21.8 6.0 %copy-start.4 = (bf16[8,1,8,1024]{3,2,1,0:T(8,128)(2,1)S(1)}, bf16[8,1,8,1024]{3,2,1,0:T(8,128)(2,1)}, u32[]{:S(2)}) copy-start(bf16[8,1,8,1024]{3,2,1,0:T(8,128)(2,1)} %get-tuple-element.20) | copy-start | bytes 393220
  21.8 47.0 %all-to-all-start = ((bf16[32,3,8,1024]{3,2,1,0:T(8,128)(2,1)}), bf16[32,3,8,1024]{3,2,1,0:T(8,128)(2,1)S(1)}, u32[]{:S(2)}, u32[]{:S(2)}) async-start(bf16[32,3,8,1024]{3,2,1,0:T(8,128)(2,1)} %after.2), calls=%async_computation | async-start | bytes 3145728 | tf_op jit(solution)/shard_map/all_to_all | solution.py:211
  27.9 1.6 %collective-permute-start.3 = (bf16[4,1,4,1,8,1024]{5,4,3,2,1,0:T(8,128)(2,1)S(1)}, bf16[4,1,4,1,8,1024]{5,4,3,2,1,0:T(8,128)(2,1)S(1)}, u32[]{:S(2)}, u32[]{:S(2)}) collective-permute-start(bf16[4,1,4,1,8,1024]{5,4,3,2,1,0:T(8,128)(2,1)S(1)} %get-tuple-element.28), channel_id=1, source_target_pairs={{0,8},{1,9},{2,10},{3,11},{4,12},{5,13},{6,14},{7,15},{8,0},{9,1},... | collective-permute-start | bytes 786440 | tf_op jit(solution)/shard_map/ppermute | solution.py:240
  29.5 21.0 %collective-permute-start.6 = (bf16[4,2,1,1,8,1024]{5,4,3,2,1,0:T(8,128)(2,1)S(1)}, bf16[4,2,1,1,8,1024]{5,4,3,2,1,0:T(8,128)(2,1)S(1)}, u32[]{:S(2)}, u32[]{:S(2)}) collective-permute-start(bf16[4,2,1,1,8,1024]{5,4,3,2,1,0:T(8,128)(2,1)S(1)} %get-tuple-element.25), channel_id=1, source_target_pairs={{0,17},{1,16},{2,19},{3,18},{4,21},{5,20},{6,23},{7,22},{8,25},{9,... | collective-permute-start | bytes 393224 | tf_op jit(solution)/shard_map/ppermute | solution.py:240
  32.2 19.5 %collective-permute-start.5 = (bf16[4,2,1,1,8,1024]{5,4,3,2,1,0:T(8,128)(2,1)S(1)}, bf16[4,2,1,1,8,1024]{5,4,3,2,1,0:T(8,128)(2,1)S(1)}, u32[]{:S(2)}, u32[]{:S(2)}) collective-permute-start(bf16[4,2,1,1,8,1024]{5,4,3,2,1,0:T(8,128)(2,1)S(1)} %get-tuple-element.26), channel_id=1, source_target_pairs={{0,1},{1,0},{2,3},{3,2},{4,5},{5,4},{6,7},{7,6},{8,9},{9,8},{10,11... | collective-permute-start | bytes 393224 | tf_op jit(solution)/shard_map/ppermute | solution.py:240
  32.8 18.9 %collective-permute-start.4 = (bf16[4,2,1,1,8,1024]{5,4,3,2,1,0:T(8,128)(2,1)S(1)}, bf16[4,2,1,1,8,1024]{5,4,3,2,1,0:T(8,128)(2,1)S(1)}, u32[]{:S(2)}, u32[]{:S(2)}) collective-permute-start(bf16[4,2,1,1,8,1024]{5,4,3,2,1,0:T(8,128)(2,1)S(1)} %get-tuple-element.24), channel_id=1, source_target_pairs={{0,16},{1,17},{2,18},{3,19},{4,20},{5,21},{6,22},{7,23},{8,24},{9,... | collective-permute-start | bytes 393224 | tf_op jit(solution)/shard_map/ppermute | solution.py:240
  55.5 13.2 %copy-start.3 = (bf16[16,1,8,512]{3,2,1,0:T(8,128)(2,1)}, bf16[16,1,8,512]{3,2,1,0:T(8,128)(2,1)S(1)}, u32[]{:S(2)}) copy-start(bf16[16,1,8,512]{3,2,1,0:T(8,128)(2,1)S(1)} %get-tuple-element.21.before_ref) | copy-start | bytes 393220
  55.5 1.4 %collective-permute-start.7 = (bf16[1,4,4,1,8,512]{5,4,3,2,1,0:T(8,128)(2,1)S(1)}, bf16[1,4,4,1,8,512]{5,4,3,2,1,0:T(8,128)(2,1)S(1)}, u32[]{:S(2)}, u32[]{:S(2)}) collective-permute-start(bf16[1,4,4,1,8,512]{5,4,3,2,1,0:T(8,128)(2,1)S(1)} %bitcast.17), channel_id=1, source_target_pairs={{0,8},{1,9},{2,10},{3,11},{4,12},{5,13},{6,14},{7,15},{8,0},{9,1},... | collective-permute-start | bytes 393224 | tf_op jit(solution)/shard_map/ppermute | solution.py:240
  57.0 5.9 %collective-permute-start.10 = (bf16[2,1,4,1,8,512]{5,4,3,2,1,0:T(8,128)(2,1)S(1)}, bf16[2,1,4,1,8,512]{5,4,3,2,1,0:T(8,128)(2,1)S(1)}, u32[]{:S(2)}, u32[]{:S(2)}) collective-permute-start(bf16[2,1,4,1,8,512]{5,4,3,2,1,0:T(8,128)(2,1)S(1)} %get-tuple-element.35), channel_id=1, source_target_pairs={{0,17},{1,16},{2,19},{3,18},{4,21},{5,20},{6,23},{7,22},{8,25},{9,... | collective-permute-start | bytes 196616 | tf_op jit(solution)/shard_map/ppermute | solution.py:240
  57.5 6.0 %collective-permute-start.9 = (bf16[2,1,4,1,8,512]{5,4,3,2,1,0:T(8,128)(2,1)S(1)}, bf16[2,1,4,1,8,512]{5,4,3,2,1,0:T(8,128)(2,1)S(1)}, u32[]{:S(2)}, u32[]{:S(2)}) collective-permute-start(bf16[2,1,4,1,8,512]{5,4,3,2,1,0:T(8,128)(2,1)S(1)} %get-tuple-element.36), channel_id=1, source_target_pairs={{0,1},{1,0},{2,3},{3,2},{4,5},{5,4},{6,7},{7,6},{8,9},{9,8},{10,11... | collective-permute-start | bytes 196616 | tf_op jit(solution)/shard_map/ppermute | solution.py:240
  59.9 4.3 %collective-permute-start.8 = (bf16[2,1,4,1,8,512]{5,4,3,2,1,0:T(8,128)(2,1)S(1)}, bf16[2,1,4,1,8,512]{5,4,3,2,1,0:T(8,128)(2,1)S(1)}, u32[]{:S(2)}, u32[]{:S(2)}) collective-permute-start(bf16[2,1,4,1,8,512]{5,4,3,2,1,0:T(8,128)(2,1)S(1)} %get-tuple-element.34), channel_id=1, source_target_pairs={{0,16},{1,17},{2,18},{3,19},{4,20},{5,21},{6,22},{7,23},{8,24},{9,... | collective-permute-start | bytes 196616 | tf_op jit(solution)/shard_map/ppermute | solution.py:240
  64.3 11.6 %collective-permute-start.11 = (bf16[2,4,1,1,8,512]{5,4,3,2,1,0:T(8,128)(2,1)S(1)}, bf16[2,4,1,1,8,512]{5,4,3,2,1,0:T(8,128)(2,1)S(1)}, u32[]{:S(2)}, u32[]{:S(2)}) collective-permute-start(bf16[2,4,1,1,8,512]{5,4,3,2,1,0:T(8,128)(2,1)S(1)} %get-tuple-element.32), channel_id=1, source_target_pairs={{0,2},{1,3},{2,0},{3,1},{4,6},{5,7},{6,4},{7,5},{8,10},{9,11},{10,... | collective-permute-start | bytes 196616 | tf_op jit(solution)/shard_map/ppermute | solution.py:240
  65.5 10.4 %collective-permute-start.12 = (bf16[2,4,1,1,8,512]{5,4,3,2,1,0:T(8,128)(2,1)S(1)}, bf16[2,4,1,1,8,512]{5,4,3,2,1,0:T(8,128)(2,1)S(1)}, u32[]{:S(2)}, u32[]{:S(2)}) collective-permute-start(bf16[2,4,1,1,8,512]{5,4,3,2,1,0:T(8,128)(2,1)S(1)} %get-tuple-element.31), channel_id=1, source_target_pairs={{0,4},{1,5},{2,6},{3,7},{4,0},{5,1},{6,2},{7,3},{8,12},{9,13},{10,... | collective-permute-start | bytes 196616 | tf_op jit(solution)/shard_map/ppermute | solution.py:240
  66.9 8.9 %collective-permute-start.13 = (bf16[2,4,1,1,8,512]{5,4,3,2,1,0:T(8,128)(2,1)S(1)}, bf16[2,4,1,1,8,512]{5,4,3,2,1,0:T(8,128)(2,1)S(1)}, u32[]{:S(2)}, u32[]{:S(2)}) collective-permute-start(bf16[2,4,1,1,8,512]{5,4,3,2,1,0:T(8,128)(2,1)S(1)} %get-tuple-element.30), channel_id=1, source_target_pairs={{0,6},{1,7},{2,4},{3,5},{4,2},{5,3},{6,0},{7,1},{8,14},{9,15},{10,... | collective-permute-start | bytes 196616 | tf_op jit(solution)/shard_map/ppermute | solution.py:240
  75.8 4.4 %copy-start = (bf16[512,1024]{1,0:T(8,128)(2,1)S(1)}, bf16[512,1024]{1,0:T(8,128)(2,1)}, u32[]{:S(2)}) copy-start(bf16[512,1024]{1,0:T(8,128)(2,1)} %output_ref.7) | copy-start | bytes 3145732
  75.9 26.3 %all-to-all-start.1 = ((bf16[32,3,8,512]{3,2,1,0:T(8,128)(2,1)}), bf16[32,3,8,512]{3,2,1,0:T(8,128)(2,1)S(1)}, u32[]{:S(2)}, u32[]{:S(2)}) async-start(bf16[32,3,8,512]{3,2,1,0:T(8,128)(2,1)} %after.3), calls=%async_computation.1 | async-start | bytes 1572864 | tf_op jit(solution)/shard_map/all_to_all | solution.py:211
  80.3 21.9 %copy-start.1 = (bf16[3,256,1024]{2,1,0:T(8,128)(2,1)S(1)}, bf16[3,256,1024]{2,1,0:T(8,128)(2,1)}, u32[]{:S(2)}) copy-start(bf16[3,256,1024]{2,1,0:T(8,128)(2,1)} %get-tuple-element.15.mixed_ref) | copy-start | bytes 4718596
  80.3 1.2 %copy-start.2 = (bf16[1,256,1024]{2,1,0:T(8,128)(2,1)S(1)}, bf16[1,256,1024]{2,1,0:T(8,128)(2,1)}, u32[]{:S(2)}) copy-start(bf16[1,256,1024]{2,1,0:T(8,128)(2,1)} %get-tuple-element.14.refs_0_.mixed_ref) | copy-start | bytes 1572868

commit v4 on v3

--- a/solution.py
+++ b/solution.py
@@ -13,6 +13,7 @@
 LANES = 128
 EPSILON = 1e-06
 MASKED = -1e30
+SPACE_VMEM_LIMIT = 40 * 1024 * 1024
 SPLIT = 2
 PIECES = 3
 ANYWHERE = pl.BlockSpec(memory_space=pl.ANY)
@@ -87,6 +88,37 @@
     return jnp.stack(parts)
 
 
+def space_first_kernel(
+    groups, video_ref, gain_ref, project_ref, output_ref, time_gain_ref, mixed_ref, project, output, *refs
+):
+    *sent_refs, frame, gains, mixed, scratch, sems = refs
+    parts = sent_refs[0].shape[0]
+    frame_copy = pltpu.make_async_copy(video_ref.at[0], frame, sems.at[0])
+    gain_copy = pltpu.make_async_copy(gain_ref, gains.at[pl.ds(0, 1)], sems.at[1])
+    weight_copies = [
+        pltpu.make_async_copy(project_ref, project, sems.at[2]),
+        pltpu.make_async_copy(output_ref, output, sems.at[3]),
+        pltpu.make_async_copy(time_gain_ref, gains.at[pl.ds(1, 1)], sems.at[4]),
+    ]
+    mixed_copy = pltpu.make_async_copy(mixed, mixed_ref.at[0], sems.at[5])
+    for copy in (gain_copy, frame_copy, *weight_copies):
+        copy.start()
+    gain_copy.wait()
+    frame_copy.wait()
+    floats = frame[...].astype(jnp.float32)
+    rows = normed(floats, gains[0:1]).astype(jnp.bfloat16)
+    for copy in weight_copies:
+        copy.wait()
+    heads = jnp.dot(rows, project[...], preferred_element_type=jnp.float32).astype(jnp.bfloat16)
+    context = attend(heads, None)
+    here = (floats + jnp.dot(context, output[...], preferred_element_type=jnp.float32)).astype(jnp.bfloat16)
+    mixed[...] = here
+    mixed_copy.start()
+    sent = normed(here.astype(jnp.float32), gains[1:2])
+    put(sent.reshape(scratch.shape).astype(jnp.bfloat16), scratch, sent_refs, groups)
+    mixed_copy.wait()
+
+
 def space_kernel(groups, extra, video_ref, gain_ref, project_ref, output_ref, time_gain_ref, *refs):
     mixed_ref, *sent_refs = refs[extra:]
     sent_refs, scratch = (sent_refs, None) if groups is None else (sent_refs[:-1], sent_refs[-1])
@@ -218,6 +250,29 @@
     return pltpu.with_memory_space_constraint(array, pltpu.HBM)
 
 
+def in_vmem(array):
+    return pltpu.with_memory_space_constraint(array, pltpu.VMEM)
+
+
+def load_kernel(array_ref, awaited_ref, loaded_ref, sem):
+    copy = pltpu.make_async_copy(array_ref, loaded_ref, sem)
+    copy.start()
+    copy.wait()
+
+
+def load(array, awaited):
+    return pl.pallas_call(
+        load_kernel,
+        in_specs=[ANYWHERE, ANYWHERE],
+        out_specs=pl.BlockSpec(memory_space=pltpu.VMEM),
+        out_shape=pltpu.VMEM(array.shape, array.dtype),
+        scratch_shapes=[pltpu.SemaphoreType.DMA],
+        cost_estimate=cost(0, 4 * array.size, 0),
+        compiler_params=pltpu.CompilerParams(vmem_limit_bytes=2 * 1024 * 1024),
+        name="load",
+    )(in_hbm(array), awaited)
+
+
 def after(rows, awaited):
     return pl.pallas_call(
         lambda *refs: None,
@@ -263,6 +318,7 @@
 
 def space_call(video, first, clips, space_gain, space_project, space_output, time_gain, count, before, groups):
     rows, width = video.shape[1:]
+    vmem = pl.BlockSpec(memory_space=pltpu.VMEM)
     shapes, specs, scratch = sent_specs(count, clips, rows // count, width, groups)
     mixed, *sent = pl.pallas_call(
         partial(space_kernel, groups, len(before)),
@@ -276,26 +332,55 @@
         ]
         + [ANYWHERE] * len(before),
         out_specs=[pl.BlockSpec((1, rows, width), lambda c: (c, 0, 0)), *specs],
-        out_shape=[jax.ShapeDtypeStruct((clips, rows, width), jnp.bfloat16), *shapes],
+        out_shape=[pltpu.HBM((clips, rows, width), jnp.bfloat16), *(pltpu.HBM(shape.shape, jnp.bfloat16) for shape in shapes)],
         scratch_shapes=scratch,
         cost_estimate=cost(
             clips * rows * (width * 4 * WIDTH + 8 * rows * WIDTH), 2 * (4 * width * WIDTH + 3 * clips * rows * width),
             clips * HEADS * rows * rows,
         ),
-        compiler_params=pltpu.CompilerParams(vmem_limit_bytes=VMEM_LIMIT),
+        compiler_params=pltpu.CompilerParams(vmem_limit_bytes=SPACE_VMEM_LIMIT),
         name="space",
-    )(video, space_gain, space_project, space_output, time_gain, *map(in_hbm, before))
+    )(in_hbm(video), in_hbm(space_gain), in_vmem(space_project), in_vmem(space_output), in_hbm(time_gain), *map(in_hbm, before))
     return mixed, sent
 
 
-def time_call(arrived, clips, rows, time_project, count, before, groups, back):
+def space_first_call(video, space_gain, space_project, space_output, time_gain, count, groups):
+    rows, width = video.shape[1:]
+    patch_here = rows // count
+    vmem = pl.BlockSpec(memory_space=pltpu.VMEM)
+    shapes, _, scratch = sent_specs(count, 1, patch_here, width, groups)
+    mixed, project, output, *sent = pl.pallas_call(
+        partial(space_first_kernel, groups),
+        in_specs=[ANYWHERE] * 5,
+        out_specs=[ANYWHERE, vmem, vmem, *[vmem] * len(shapes)],
+        out_shape=[
+            pltpu.HBM((1, rows, width), jnp.bfloat16),
+            pltpu.VMEM(space_project.shape, jnp.bfloat16),
+            pltpu.VMEM(space_output.shape, jnp.bfloat16),
+            *[pltpu.VMEM(shape.shape, jnp.bfloat16) for shape in shapes],
+        ],
+        scratch_shapes=[
+            pltpu.VMEM((rows, width), jnp.bfloat16),
+            pltpu.VMEM((2, width), jnp.float32),
+            pltpu.VMEM((rows, width), jnp.bfloat16),
+            *scratch,
+            pltpu.SemaphoreType.DMA((6,)),
+        ],
+        cost_estimate=cost(rows * (width * 4 * WIDTH + 8 * rows * WIDTH), 2 * (4 * width * WIDTH + 3 * rows * width), 0),
+        compiler_params=pltpu.CompilerParams(vmem_limit_bytes=SPACE_VMEM_LIMIT),
+        name="space",
+    )(*map(in_hbm, (video, space_gain, space_project, space_output, time_gain)))
+    return mixed, project, output, sent
+
+
+def time_call(arrived, clips, rows, time_project, count, before, groups, back, project=None):
     width = arrived.shape[-1]
     patch_here = rows // count
     shapes, specs, scratch = sent_specs(count, clips, patch_here, WIDTH, back)
     return pl.pallas_call(
         partial(time_kernel, groups, back, len(before), patch_here),
         grid=(clips,),
-        in_specs=[exchange_spec(count, patch_here, width), whole((width, 3 * WIDTH))] + [ANYWHERE] * len(before),
+        in_specs=[exchange_spec(count, patch_here, width), whole((width, 3 * WIDTH)) if project is None else pl.BlockSpec(memory_space=pltpu.VMEM)] + [ANYWHERE] * len(before),
         out_specs=specs,
         out_shape=shapes,
         scratch_shapes=scratch + [pltpu.VMEM((rows, rows), jnp.float32)],
@@ -305,7 +390,7 @@
         ),
         compiler_params=pltpu.CompilerParams(vmem_limit_bytes=TIME_VMEM_LIMIT),
         name="time",
-    )(arrived, in_hbm(time_project), *map(in_hbm, before))
+    )(arrived, in_hbm(time_project) if project is None else in_vmem(project), *map(in_hbm, before))
 
 
 def time_wide_call(arrived, clips, rows, time_project, count, before):
@@ -381,11 +466,13 @@
     others = clip_count - 1
     back = bit_groups()
     there = [back[2], back[0], back[1]]
-    kept, sent = space_call(video, 0, 1, *weights, count, [], there)
+    kept, project, output, sent = space_first_call(video, *weights, count, there)
+    weights = weights[0], project, output, weights[3]
     kept_others, sent_others = space_call(video, 1, others, *weights, count, [kept], None)
     arrived, steps = swap(sent, there)
     arrived_others = exchange(after(sent_others[0], steps[0]), count, patch_here)
-    context = time_call(arrived, 1, patch_count, time_project, count, [], there, back)
+    loaded = load(time_project, steps[1][0])
+    context = time_call(arrived, 1, patch_count, time_project, count, [], there, back, loaded)
     returned, steps = swap(context, back)
     context = time_wide_call(arrived_others, others, patch_count, time_project, count, context[0])
     returned_others = exchange(after(context, steps[-1]), count, patch_here)

time: 104 us -> 101 us (0.971)
  Pallas kernels: 29.9 us -> 28.1 us
  waiting for transfers between devices: 44.6 us -> 43.5 us
    pallas_call x0 -> x2, Pallas kernels: none -> 6.99 us  [the longest x1 5.09 us: space_first_call(): pl.pallas_call(partial(space_first_kernel, groups), in_specs=[ANYWHERE] *...]
    pallas_call x2 -> x1, Pallas kernels: 16 us -> 9.09 us  [space_call(): pl.pallas_call(partial(space_kernel, groups, len(before)), grid=(clips,),...]
    pallas_call x1, Pallas kernels: 3.69 us -> 1.8 us  [time_call(): pl.pallas_call(partial(time_kernel, groups, back, len(before), patch_here...]
    ppermute x14, waiting for transfers between devices: 25.1 us -> 24.1 us  [swap(): lax.ppermute(block, AXES, [(device, device ^ mask_of(index, group)) for d...]
  transfers between devices with their start and end apart: 16 -> 16, of which waited for: 9 -> 8; matrix products, arithmetic and copies ran while one was open for 0% -> 0% of each run, Pallas kernels for 22% -> 21%
where the time goes in v4:
time: 101 us
  waiting for transfers between devices  43.5 us (43%)
  Pallas kernels  28.1 us (28%)
  starting transfers between devices  27.9 us (28%)
  local copies, waits for them, and re-layouts  1.23 us (1%)
    ppermute x14, waiting for transfers between devices, swap(): lax.ppermute(block, AXES, [(device, device ^ mask_of(index, group)) for d...  24.1 us
    all_to_all x2, waiting for transfers between devices, exchange(): lax.all_to_all(sent, AXES, split_axis=0, concat_axis=0, tiled=True)  19.4 us
    ppermute x14, starting transfers between devices, swap(): lax.ppermute(block, AXES, [(device, device ^ mask_of(index, group)) for d...  17.6 us
    all_to_all x2, starting transfers between devices, exchange(): lax.all_to_all(sent, AXES, split_axis=0, concat_axis=0, tiled=True)  10.3 us
    pallas_call x1, Pallas kernels, space_call(): pl.pallas_call(partial(space_kernel, groups, len(before)), grid=(clips,),...  9.09 us
    pallas_call x1, Pallas kernels, time_wide_call(): pl.pallas_call(partial(time_wide_kernel, patch_here), in_specs=[pl.BlockS...  7.1 us
    pallas_call x1, Pallas kernels, space_first_call(): pl.pallas_call(partial(space_first_kernel, groups), in_specs=[ANYWHERE] *...  5.09 us
  transfers between devices with their start and end apart: 16, of which 8 were waited for; matrix products, arithmetic and copies ran while one was open for 0% of the time, Pallas kernels for 21%

profile of v4, /device:TPU:0, one launch (start us, length us, event | category | flops | bytes accessed | tf_op | source)
XLA Modules:
  0.0 101.2 jit_solution(9349550890486608844)
XLA Ops:
  0.0 5.1 %space.2 = (bf16[1,256,1024]{2,1,0:T(8,128)(2,1)}, bf16[1024,1536]{1,0:T(8,128)(2,1)S(1)}, bf16[512,1024]{1,0:T(8,128)(2,1)S(1)}, bf16[8,1,8,1024]{3,2,1,0:T(8,1...) custom-call(bf16[4,256,1024]{2,1,0:T(8,128)(2,1)} %bitcast.22, ...), custom_call_target="tpu_custom_call" | custom-call | flops 1610612736 | bytes 5767168 | tf_op jit(solution)/shard_map/space/pallas_call | solution.py:352
  5.1 3.1 %collective-permute-start = (bf16[1,2,4,1,8,1024]{5,4,3,2,1,0:T(8,128)(2,1)S(1)}, bf16[1,2,4,1,8,1024]{5,4,3,2,1,0:T(8,128)(2,1)S(1)}, u32[]{:S(2)}, u32[]{:S(2)}) collective-permute-start(bf16[1,2,4,1,8,1024]{5,4,3,2,1,0:T(8,128)(2,1)S(1)} %bitcast.20), channel_id=1, source_target_pairs={{0,2},{1,3},{2,0},{3,1},{4,6},{5,7},{6,4},{7,5},{8,10},{9,11},{10,... | collective-permute-start | bytes 393224 | tf_op jit(solution)/shard_map/ppermute | solution.py:295
  8.2 2.6 %collective-permute-start.1 = (bf16[1,2,4,1,8,1024]{5,4,3,2,1,0:T(8,128)(2,1)S(1)}, bf16[1,2,4,1,8,1024]{5,4,3,2,1,0:T(8,128)(2,1)S(1)}, u32[]{:S(2)}, u32[]{:S(2)}) collective-permute-start(bf16[1,2,4,1,8,1024]{5,4,3,2,1,0:T(8,128)(2,1)S(1)} %bitcast.19), channel_id=1, source_target_pairs={{0,4},{1,5},{2,6},{3,7},{4,0},{5,1},{6,2},{7,3},{8,12},{9,13},{10,... | collective-permute-start | bytes 393224 | tf_op jit(solution)/shard_map/ppermute | solution.py:295
  10.8 9.1 %space.3 = (bf16[3,256,1024]{2,1,0:T(8,128)(2,1)}, bf16[32,3,8,1024]{3,2,1,0:T(8,128)(2,1)}) custom-call(bf16[4,256,1024]{2,1,0:T(8,128)(2,1)} %bitcast.23, f32[1,1024]{1,0:T(1,128)} %bitcast.25, bf16[1024,1536]{1,0:T(8,128)(2,1)S(1)} %get-tuple-element.16.project_ref, bf16[512,1024]{1,0:T(8,128)(2,1)S(1)} %get-tuple-element.17.output_ref, ...), custom_call_target="tpu_custom_call" | custom-call | flops 4831838208 | bytes 8912896 | tf_op jit(solution)/shard_map/space/pallas_call | solution.py:323
  19.9 1.2 %collective-permute-done.1.refs_2_ = bf16[1,2,4,1,8,1024]{5,4,3,2,1,0:T(8,128)(2,1)S(1)} collective-permute-done((bf16[1,2,4,1,8,1024]{5,4,3,2,1,0:T(8,128)(2,1)S(1)}, bf16[1,2,4,1,8,1024]{5,4,3,2,1,0:T(8,128)(2,1)S(1)}, u32[]{:S(2)}, u32[]{:S(2)}) %collective-permute-start.1) | collective-permute-done | bytes 131104 | tf_op jit(solution)/shard_map/ppermute | solution.py:295
  21.1 5.2 %all-to-all-start = ((bf16[32,3,8,1024]{3,2,1,0:T(8,128)(2,1)}), bf16[32,3,8,1024]{3,2,1,0:T(8,128)(2,1)S(1)}, u32[]{:S(2)}, u32[]{:S(2)}) async-start(bf16[32,3,8,1024]{3,2,1,0:T(8,128)(2,1)} %after.2), calls=%async_computation | async-start | bytes 3145728 | tf_op jit(solution)/shard_map/all_to_all | solution.py:243
  26.3 0.1 pad_maximum_fusion
  26.5 0.3 collective-permute-start.3
  26.8 1.3 %collective-permute-done.3.awaited_ref = bf16[4,1,4,1,8,1024]{5,4,3,2,1,0:T(8,128)(2,1)S(1)} collective-permute-done((bf16[4,1,4,1,8,1024]{5,4,3,2,1,0:T(8,128)(2,1)S(1)}, bf16[4,1,4,1,8,1024]{5,4,3,2,1,0:T(8,128)(2,1)S(1)}, u32[]{:S(2)}, u32[]{:S(2)}) %collective-permute-start.3) | collective-permute-done | bytes 262176 | tf_op jit(solution)/shard_map/ppermute | solution.py:295
  28.1 1.8 %collective-permute-start.4 = (bf16[4,2,1,1,8,1024]{5,4,3,2,1,0:T(8,128)(2,1)S(1)}, bf16[4,2,1,1,8,1024]{5,4,3,2,1,0:T(8,128)(2,1)S(1)}, u32[]{:S(2)}, u32[]{:S(2)}) collective-permute-start(bf16[4,2,1,1,8,1024]{5,4,3,2,1,0:T(8,128)(2,1)S(1)} %get-tuple-element.28), channel_id=1, source_target_pairs={{0,16},{1,17},{2,18},{3,19},{4,20},{5,21},{6,22},{7,23},{8,24},{9,... | collective-permute-start | bytes 393224 | tf_op jit(solution)/shard_map/ppermute | solution.py:295
  30.0 1.5 %collective-permute-start.6 = (bf16[4,2,1,1,8,1024]{5,4,3,2,1,0:T(8,128)(2,1)S(1)}, bf16[4,2,1,1,8,1024]{5,4,3,2,1,0:T(8,128)(2,1)S(1)}, u32[]{:S(2)}, u32[]{:S(2)}) collective-permute-start(bf16[4,2,1,1,8,1024]{5,4,3,2,1,0:T(8,128)(2,1)S(1)} %get-tuple-element.29), channel_id=1, source_target_pairs={{0,17},{1,16},{2,19},{3,18},{4,21},{5,20},{6,23},{7,22},{8,25},{9,... | collective-permute-start | bytes 393224 | tf_op jit(solution)/shard_map/ppermute | solution.py:295
  31.4 0.3 collective-permute-start.5
  31.7 1.9 %load.1.project_ref = bf16[1024,1536]{1,0:T(8,128)(2,1)S(1)} custom-call(bf16[1024,1536]{1,0:T(8,128)(2,1)} %project_ref.3, bf16[4,1,4,1,8,1024]{5,4,3,2,1,0:T(8,128)(2,1)S(1)} %collective-permute-done.3.awaited_ref), custom_call_target="tpu_custom_call" | custom-call | bytes 6291456 | tf_op jit(solution)/shard_map/load/pallas_call | solution.py:264
  33.6 16.6 %collective-permute-done.4 = bf16[4,2,1,1,8,1024]{5,4,3,2,1,0:T(8,128)(2,1)S(1)} collective-permute-done((bf16[4,2,1,1,8,1024]{5,4,3,2,1,0:T(8,128)(2,1)S(1)}, bf16[4,2,1,1,8,1024]{5,4,3,2,1,0:T(8,128)(2,1)S(1)}, u32[]{:S(2)}, u32[]{:S(2)}) %collective-permute-start.4) | collective-permute-done | bytes 131104 | tf_op jit(solution)/shard_map/ppermute | solution.py:295
  50.2 0.2 collective-permute-done.5
  50.4 0.1 pad_maximum_fusion.1
  50.4 1.8 %time.2 = (bf16[16,1,8,512]{3,2,1,0:T(8,128)(2,1)S(1)}, bf16[16,1,8,512]{3,2,1,0:T(8,128)(2,1)S(1)}) custom-call(bf16[32,1,8,1024]{3,2,1,0:T(8,128)(2,1)S(1)} %bitcast.15, bf16[1024,1536]{1,0:T(8,128)(2,1)S(1)} %load.1.project_ref), custom_call_target="tpu_custom_call" | custom-call | flops 1342177280 | bytes 4194304 | tf_op jit(solution)/shard_map/time/pallas_call | solution.py:380
  52.2 0.1 collective-permute-start.7
  52.3 1.3 %collective-permute-done.7 = bf16[1,4,4,1,8,512]{5,4,3,2,1,0:T(8,128)(2,1)S(1)} collective-permute-done((bf16[1,4,4,1,8,512]{5,4,3,2,1,0:T(8,128)(2,1)S(1)}, bf16[1,4,4,1,8,512]{5,4,3,2,1,0:T(8,128)(2,1)S(1)}, u32[]{:S(2)}, u32[]{:S(2)}) %collective-permute-start.7) | collective-permute-done | bytes 131104 | tf_op jit(solution)/shard_map/ppermute | solution.py:295
  53.7 1.5 %collective-permute-start.8 = (bf16[2,1,4,1,8,512]{5,4,3,2,1,0:T(8,128)(2,1)S(1)}, bf16[2,1,4,1,8,512]{5,4,3,2,1,0:T(8,128)(2,1)S(1)}, u32[]{:S(2)}, u32[]{:S(2)}) collective-permute-start(bf16[2,1,4,1,8,512]{5,4,3,2,1,0:T(8,128)(2,1)S(1)} %get-tuple-element.38), channel_id=1, source_target_pairs={{0,16},{1,17},{2,18},{3,19},{4,20},{5,21},{6,22},{7,23},{8,24},{9,... | collective-permute-start | bytes 196616 | tf_op jit(solution)/shard_map/ppermute | solution.py:295
  55.2 2.0 %collective-permute-start.9 = (bf16[2,1,4,1,8,512]{5,4,3,2,1,0:T(8,128)(2,1)S(1)}, bf16[2,1,4,1,8,512]{5,4,3,2,1,0:T(8,128)(2,1)S(1)}, u32[]{:S(2)}, u32[]{:S(2)}) collective-permute-start(bf16[2,1,4,1,8,512]{5,4,3,2,1,0:T(8,128)(2,1)S(1)} %get-tuple-element.40), channel_id=1, source_target_pairs={{0,1},{1,0},{2,3},{3,2},{4,5},{5,4},{6,7},{7,6},{8,9},{9,8},{10,11... | collective-permute-start | bytes 196616 | tf_op jit(solution)/shard_map/ppermute | solution.py:295
  57.2 1.0 %collective-permute-done.8 = bf16[2,1,4,1,8,512]{5,4,3,2,1,0:T(8,128)(2,1)S(1)} collective-permute-done((bf16[2,1,4,1,8,512]{5,4,3,2,1,0:T(8,128)(2,1)S(1)}, bf16[2,1,4,1,8,512]{5,4,3,2,1,0:T(8,128)(2,1)S(1)}, u32[]{:S(2)}, u32[]{:S(2)}) %collective-permute-start.8) | collective-permute-done | bytes 65568 | tf_op jit(solution)/shard_map/ppermute | solution.py:295
  58.3 2.4 %collective-permute-done.10 = bf16[2,1,4,1,8,512]{5,4,3,2,1,0:T(8,128)(2,1)S(1)} collective-permute-done((bf16[2,1,4,1,8,512]{5,4,3,2,1,0:T(8,128)(2,1)S(1)}, bf16[2,1,4,1,8,512]{5,4,3,2,1,0:T(8,128)(2,1)S(1)}, u32[]{:S(2)}, u32[]{:S(2)}) %collective-permute-start.10) | collective-permute-done | bytes 65568 | tf_op jit(solution)/shard_map/ppermute | solution.py:295
  60.7 2.9 %collective-permute-start.13 = (bf16[2,4,1,1,8,512]{5,4,3,2,1,0:T(8,128)(2,1)S(1)}, bf16[2,4,1,1,8,512]{5,4,3,2,1,0:T(8,128)(2,1)S(1)}, u32[]{:S(2)}, u32[]{:S(2)}) collective-permute-start(bf16[2,4,1,1,8,512]{5,4,3,2,1,0:T(8,128)(2,1)S(1)} %get-tuple-element.34), channel_id=1, source_target_pairs={{0,6},{1,7},{2,4},{3,5},{4,2},{5,3},{6,0},{7,1},{8,14},{9,15},{10,... | collective-permute-start | bytes 196616 | tf_op jit(solution)/shard_map/ppermute | solution.py:295
  63.6 1.6 %collective-permute-start.11 = (bf16[2,4,1,1,8,512]{5,4,3,2,1,0:T(8,128)(2,1)S(1)}, bf16[2,4,1,1,8,512]{5,4,3,2,1,0:T(8,128)(2,1)S(1)}, u32[]{:S(2)}, u32[]{:S(2)}) collective-permute-start(bf16[2,4,1,1,8,512]{5,4,3,2,1,0:T(8,128)(2,1)S(1)} %get-tuple-element.36), channel_id=1, source_target_pairs={{0,2},{1,3},{2,0},{3,1},{4,6},{5,7},{6,4},{7,5},{8,10},{9,11},{10,... | collective-permute-start | bytes 196616 | tf_op jit(solution)/shard_map/ppermute | solution.py:295
  65.2 7.1 %time.3.refs_0_ = bf16[32,3,8,512]{3,2,1,0:T(8,128)(2,1)} custom-call(bf16[32,3,8,1024]{3,2,1,0:T(8,128)(2,1)S(1)} %all-to-all-done.rows_ref, bf16[1024,1536]{1,0:T(8,128)(2,1)} %project_ref.3, bf16[16,1,8,512]{3,2,1,0:T(8,128)(2,1)} %copy-done.3), custom_call_target="tpu_custom_call" | custom-call | flops 4026531840 | bytes 6291456 | tf_op jit(solution)/shard_map/time/pallas_call | solution.py:399
  72.3 0.0 copy-start
  72.4 5.1 %all-to-all-start.1 = ((bf16[32,3,8,512]{3,2,1,0:T(8,128)(2,1)}), bf16[32,3,8,512]{3,2,1,0:T(8,128)(2,1)S(1)}, u32[]{:S(2)}, u32[]{:S(2)}) async-start(bf16[32,3,8,512]{3,2,1,0:T(8,128)(2,1)} %after.3), calls=%async_computation.1 | async-start | bytes 1572864 | tf_op jit(solution)/shard_map/all_to_all | solution.py:243
  77.5 1.1 %copy-done.2 = bf16[1,256,1024]{2,1,0:T(8,128)(2,1)S(1)} copy-done((bf16[1,256,1024]{2,1,0:T(8,128)(2,1)S(1)}, bf16[1,256,1024]{2,1,0:T(8,128)(2,1)}, u32[]{:S(2)}) %copy-start.2) | copy-done | bytes 524312
  78.7 1.3 %final.2.before_ref = bf16[4,256,1024]{2,1,0:T(8,128)(2,1)} custom-call(bf16[1,256,1024]{2,1,0:T(8,128)(2,1)S(1)} %copy-done.2, bf16[32,1,8,512]{3,2,1,0:T(8,128)(2,1)S(1)} %bitcast.14, bf16[512,1024]{1,0:T(8,128)(2,1)S(1)} %copy-done), custom_call_target="tpu_custom_call" | custom-call | flops 268435456 | bytes 2621440 | tf_op jit(solution)/shard_map/final/pallas_call | solution.py:423
  80.0 19.4 %all-to-all-done.1.context_ref = bf16[32,3,8,512]{3,2,1,0:T(8,128)(2,1)S(1)} async-done(((bf16[32,3,8,512]{3,2,1,0:T(8,128)(2,1)}), bf16[32,3,8,512]{3,2,1,0:T(8,128)(2,1)S(1)}, u32[]{:S(2)}, u32[]{:S(2)}) %all-to-all-start.1) | async-done | bytes 786464 | tf_op jit(solution)/shard_map/all_to_all | solution.py:243
  99.4 1.8 %final.3 = bf16[4,256,1024]{2,1,0:T(8,128)(2,1)} custom-call(bf16[3,256,1024]{2,1,0:T(8,128)(2,1)S(1)} %copy-done.1, bf16[32,3,8,512]{3,2,1,0:T(8,128)(2,1)S(1)} %all-to-all-done.1.context_ref, bf16[512,1024]{1,0:T(8,128)(2,1)S(1)} %copy-done, bf16[4,256,1024]{2,1,0:T(8,128)(2,1)} %final.2.before_ref), custom_call_target="tpu_custom_call", output_to_operand_aliasing={{}: (3, {})} | custom-call | flops 805306368 | bytes 5767168 | tf_op jit(solution)/shard_map/final/pallas_call | solution.py:444
  (25 shorter events, 0.3 us)
Async XLA Ops:
  5.1 14.8 %collective-permute-start = (bf16[1,2,4,1,8,1024]{5,4,3,2,1,0:T(8,128)(2,1)S(1)}, bf16[1,2,4,1,8,1024]{5,4,3,2,1,0:T(8,128)(2,1)S(1)}, u32[]{:S(2)}, u32[]{:S(2)}) collective-permute-start(bf16[1,2,4,1,8,1024]{5,4,3,2,1,0:T(8,128)(2,1)S(1)} %bitcast.20), channel_id=1, source_target_pairs={{0,2},{1,3},{2,0},{3,1},{4,6},{5,7},{6,4},{7,5},{8,10},{9,11},{10,... | collective-permute-start | bytes 393224 | tf_op jit(solution)/shard_map/ppermute | solution.py:295
  8.2 12.9 %collective-permute-start.1 = (bf16[1,2,4,1,8,1024]{5,4,3,2,1,0:T(8,128)(2,1)S(1)}, bf16[1,2,4,1,8,1024]{5,4,3,2,1,0:T(8,128)(2,1)S(1)}, u32[]{:S(2)}, u32[]{:S(2)}) collective-permute-start(bf16[1,2,4,1,8,1024]{5,4,3,2,1,0:T(8,128)(2,1)S(1)} %bitcast.19), channel_id=1, source_target_pairs={{0,4},{1,5},{2,6},{3,7},{4,0},{5,1},{6,2},{7,3},{8,12},{9,13},{10,... | collective-permute-start | bytes 393224 | tf_op jit(solution)/shard_map/ppermute | solution.py:295
  10.8 10.3 %collective-permute-start.2 = (bf16[1,2,4,1,8,1024]{5,4,3,2,1,0:T(8,128)(2,1)S(1)}, bf16[1,2,4,1,8,1024]{5,4,3,2,1,0:T(8,128)(2,1)S(1)}, u32[]{:S(2)}, u32[]{:S(2)}) collective-permute-start(bf16[1,2,4,1,8,1024]{5,4,3,2,1,0:T(8,128)(2,1)S(1)} %bitcast.18), channel_id=1, source_target_pairs={{0,6},{1,7},{2,4},{3,5},{4,2},{5,3},{6,0},{7,1},{8,14},{9,15},{10,... | collective-permute-start | bytes 393224 | tf_op jit(solution)/shard_map/ppermute | solution.py:295
  21.1 44.1 %all-to-all-start = ((bf16[32,3,8,1024]{3,2,1,0:T(8,128)(2,1)}), bf16[32,3,8,1024]{3,2,1,0:T(8,128)(2,1)S(1)}, u32[]{:S(2)}, u32[]{:S(2)}) async-start(bf16[32,3,8,1024]{3,2,1,0:T(8,128)(2,1)} %after.2), calls=%async_computation | async-start | bytes 3145728 | tf_op jit(solution)/shard_map/all_to_all | solution.py:243
  26.5 1.6 %collective-permute-start.3 = (bf16[4,1,4,1,8,1024]{5,4,3,2,1,0:T(8,128)(2,1)S(1)}, bf16[4,1,4,1,8,1024]{5,4,3,2,1,0:T(8,128)(2,1)S(1)}, u32[]{:S(2)}, u32[]{:S(2)}) collective-permute-start(bf16[4,1,4,1,8,1024]{5,4,3,2,1,0:T(8,128)(2,1)S(1)} %get-tuple-element.32), channel_id=1, source_target_pairs={{0,8},{1,9},{2,10},{3,11},{4,12},{5,13},{6,14},{7,15},{8,0},{9,1},... | collective-permute-start | bytes 786440 | tf_op jit(solution)/shard_map/ppermute | solution.py:295
  28.1 22.1 %collective-permute-start.4 = (bf16[4,2,1,1,8,1024]{5,4,3,2,1,0:T(8,128)(2,1)S(1)}, bf16[4,2,1,1,8,1024]{5,4,3,2,1,0:T(8,128)(2,1)S(1)}, u32[]{:S(2)}, u32[]{:S(2)}) collective-permute-start(bf16[4,2,1,1,8,1024]{5,4,3,2,1,0:T(8,128)(2,1)S(1)} %get-tuple-element.28), channel_id=1, source_target_pairs={{0,16},{1,17},{2,18},{3,19},{4,20},{5,21},{6,22},{7,23},{8,24},{9,... | collective-permute-start | bytes 393224 | tf_op jit(solution)/shard_map/ppermute | solution.py:295
  30.0 20.2 %collective-permute-start.6 = (bf16[4,2,1,1,8,1024]{5,4,3,2,1,0:T(8,128)(2,1)S(1)}, bf16[4,2,1,1,8,1024]{5,4,3,2,1,0:T(8,128)(2,1)S(1)}, u32[]{:S(2)}, u32[]{:S(2)}) collective-permute-start(bf16[4,2,1,1,8,1024]{5,4,3,2,1,0:T(8,128)(2,1)S(1)} %get-tuple-element.29), channel_id=1, source_target_pairs={{0,17},{1,16},{2,19},{3,18},{4,21},{5,20},{6,23},{7,22},{8,25},{9,... | collective-permute-start | bytes 393224 | tf_op jit(solution)/shard_map/ppermute | solution.py:295
  31.4 18.9 %collective-permute-start.5 = (bf16[4,2,1,1,8,1024]{5,4,3,2,1,0:T(8,128)(2,1)S(1)}, bf16[4,2,1,1,8,1024]{5,4,3,2,1,0:T(8,128)(2,1)S(1)}, u32[]{:S(2)}, u32[]{:S(2)}) collective-permute-start(bf16[4,2,1,1,8,1024]{5,4,3,2,1,0:T(8,128)(2,1)S(1)} %get-tuple-element.30), channel_id=1, source_target_pairs={{0,1},{1,0},{2,3},{3,2},{4,5},{5,4},{6,7},{7,6},{8,9},{9,8},{10,11... | collective-permute-start | bytes 393224 | tf_op jit(solution)/shard_map/ppermute | solution.py:295
  52.2 13.0 %copy-start.3 = (bf16[16,1,8,512]{3,2,1,0:T(8,128)(2,1)}, bf16[16,1,8,512]{3,2,1,0:T(8,128)(2,1)S(1)}, u32[]{:S(2)}) copy-start(bf16[16,1,8,512]{3,2,1,0:T(8,128)(2,1)S(1)} %get-tuple-element.25.before_ref) | copy-start | bytes 393220
  52.2 1.4 %collective-permute-start.7 = (bf16[1,4,4,1,8,512]{5,4,3,2,1,0:T(8,128)(2,1)S(1)}, bf16[1,4,4,1,8,512]{5,4,3,2,1,0:T(8,128)(2,1)S(1)}, u32[]{:S(2)}, u32[]{:S(2)}) collective-permute-start(bf16[1,4,4,1,8,512]{5,4,3,2,1,0:T(8,128)(2,1)S(1)} %bitcast.21), channel_id=1, source_target_pairs={{0,8},{1,9},{2,10},{3,11},{4,12},{5,13},{6,14},{7,15},{8,0},{9,1},... | collective-permute-start | bytes 393224 | tf_op jit(solution)/shard_map/ppermute | solution.py:295
  53.7 4.6 %collective-permute-start.8 = (bf16[2,1,4,1,8,512]{5,4,3,2,1,0:T(8,128)(2,1)S(1)}, bf16[2,1,4,1,8,512]{5,4,3,2,1,0:T(8,128)(2,1)S(1)}, u32[]{:S(2)}, u32[]{:S(2)}) collective-permute-start(bf16[2,1,4,1,8,512]{5,4,3,2,1,0:T(8,128)(2,1)S(1)} %get-tuple-element.38), channel_id=1, source_target_pairs={{0,16},{1,17},{2,18},{3,19},{4,20},{5,21},{6,22},{7,23},{8,24},{9,... | collective-permute-start | bytes 196616 | tf_op jit(solution)/shard_map/ppermute | solution.py:295
  55.2 5.5 %collective-permute-start.10 = (bf16[2,1,4,1,8,512]{5,4,3,2,1,0:T(8,128)(2,1)S(1)}, bf16[2,1,4,1,8,512]{5,4,3,2,1,0:T(8,128)(2,1)S(1)}, u32[]{:S(2)}, u32[]{:S(2)}) collective-permute-start(bf16[2,1,4,1,8,512]{5,4,3,2,1,0:T(8,128)(2,1)S(1)} %get-tuple-element.39), channel_id=1, source_target_pairs={{0,17},{1,16},{2,19},{3,18},{4,21},{5,20},{6,23},{7,22},{8,25},{9,... | collective-permute-start | bytes 196616 | tf_op jit(solution)/shard_map/ppermute | solution.py:295
  55.2 5.5 %collective-permute-start.9 = (bf16[2,1,4,1,8,512]{5,4,3,2,1,0:T(8,128)(2,1)S(1)}, bf16[2,1,4,1,8,512]{5,4,3,2,1,0:T(8,128)(2,1)S(1)}, u32[]{:S(2)}, u32[]{:S(2)}) collective-permute-start(bf16[2,1,4,1,8,512]{5,4,3,2,1,0:T(8,128)(2,1)S(1)} %get-tuple-element.40), channel_id=1, source_target_pairs={{0,1},{1,0},{2,3},{3,2},{4,5},{5,4},{6,7},{7,6},{8,9},{9,8},{10,11... | collective-permute-start | bytes 196616 | tf_op jit(solution)/shard_map/ppermute | solution.py:295
  60.7 11.6 %collective-permute-start.13 = (bf16[2,4,1,1,8,512]{5,4,3,2,1,0:T(8,128)(2,1)S(1)}, bf16[2,4,1,1,8,512]{5,4,3,2,1,0:T(8,128)(2,1)S(1)}, u32[]{:S(2)}, u32[]{:S(2)}) collective-permute-start(bf16[2,4,1,1,8,512]{5,4,3,2,1,0:T(8,128)(2,1)S(1)} %get-tuple-element.34), channel_id=1, source_target_pairs={{0,6},{1,7},{2,4},{3,5},{4,2},{5,3},{6,0},{7,1},{8,14},{9,15},{10,... | collective-permute-start | bytes 196616 | tf_op jit(solution)/shard_map/ppermute | solution.py:295
  63.6 8.7 %collective-permute-start.12 = (bf16[2,4,1,1,8,512]{5,4,3,2,1,0:T(8,128)(2,1)S(1)}, bf16[2,4,1,1,8,512]{5,4,3,2,1,0:T(8,128)(2,1)S(1)}, u32[]{:S(2)}, u32[]{:S(2)}) collective-permute-start(bf16[2,4,1,1,8,512]{5,4,3,2,1,0:T(8,128)(2,1)S(1)} %get-tuple-element.35), channel_id=1, source_target_pairs={{0,4},{1,5},{2,6},{3,7},{4,0},{5,1},{6,2},{7,3},{8,12},{9,13},{10,... | collective-permute-start | bytes 196616 | tf_op jit(solution)/shard_map/ppermute | solution.py:295
  63.6 8.7 %collective-permute-start.11 = (bf16[2,4,1,1,8,512]{5,4,3,2,1,0:T(8,128)(2,1)S(1)}, bf16[2,4,1,1,8,512]{5,4,3,2,1,0:T(8,128)(2,1)S(1)}, u32[]{:S(2)}, u32[]{:S(2)}) collective-permute-start(bf16[2,4,1,1,8,512]{5,4,3,2,1,0:T(8,128)(2,1)S(1)} %get-tuple-element.36), channel_id=1, source_target_pairs={{0,2},{1,3},{2,0},{3,1},{4,6},{5,7},{6,4},{7,5},{8,10},{9,11},{10,... | collective-permute-start | bytes 196616 | tf_op jit(solution)/shard_map/ppermute | solution.py:295
  72.3 5.2 %copy-start = (bf16[512,1024]{1,0:T(8,128)(2,1)S(1)}, bf16[512,1024]{1,0:T(8,128)(2,1)}, u32[]{:S(2)}) copy-start(bf16[512,1024]{1,0:T(8,128)(2,1)} %output_ref.5) | copy-start | bytes 3145732
  72.4 27.0 %all-to-all-start.1 = ((bf16[32,3,8,512]{3,2,1,0:T(8,128)(2,1)}), bf16[32,3,8,512]{3,2,1,0:T(8,128)(2,1)S(1)}, u32[]{:S(2)}, u32[]{:S(2)}) async-start(bf16[32,3,8,512]{3,2,1,0:T(8,128)(2,1)} %after.3), calls=%async_computation.1 | async-start | bytes 1572864 | tf_op jit(solution)/shard_map/all_to_all | solution.py:243
  77.5 21.9 %copy-start.1 = (bf16[3,256,1024]{2,1,0:T(8,128)(2,1)S(1)}, bf16[3,256,1024]{2,1,0:T(8,128)(2,1)}, u32[]{:S(2)}) copy-start(bf16[3,256,1024]{2,1,0:T(8,128)(2,1)} %get-tuple-element.19.mixed_ref) | copy-start | bytes 4718596
  77.5 1.2 %copy-start.2 = (bf16[1,256,1024]{2,1,0:T(8,128)(2,1)S(1)}, bf16[1,256,1024]{2,1,0:T(8,128)(2,1)}, u32[]{:S(2)}) copy-start(bf16[1,256,1024]{2,1,0:T(8,128)(2,1)} %get-tuple-element.18.refs_0_.mixed_ref) | copy-start | bytes 1572868

commit v5 on v4

--- a/solution.py
+++ b/solution.py
@@ -464,8 +464,8 @@
     if not swappable:
         return plainly(video, weights, time_project, time_output, count).reshape(video_in.shape)
     others = clip_count - 1
-    back = bit_groups()
-    there = [back[2], back[0], back[1]]
+    core, near, far = bit_groups()
+    there, back = [far, core, near], [near, far, core]
     kept, project, output, sent = space_first_call(video, *weights, count, there)
     weights = weights[0], project, output, weights[3]
     kept_others, sent_others = space_call(video, 1, others, *weights, count, [kept], None)
@@ -475,7 +475,7 @@
     context = time_call(arrived, 1, patch_count, time_project, count, [], there, back, loaded)
     returned, steps = swap(context, back)
     context = time_wide_call(arrived_others, others, patch_count, time_project, count, context[0])
-    returned_others = exchange(after(context, steps[-1]), count, patch_here)
+    returned_others = exchange(after(context, steps[1]), count, patch_here)
     out = final_call(kept, returned, time_output, count, 0, clip_count, [], back)
     out = final_wide_call(kept_others, returned_others, time_output, 1, clip_count, out)
     return out.reshape(clip_count, frame_local, patch_count, width)

time: 101 us -> 101 us (level)
  starting transfers between devices: 27.9 us -> 26 us
  waiting for transfers between devices: 43.5 us -> 44.6 us
    all_to_all x2, starting transfers between devices: 10.3 us -> 8.1 us  [exchange(): lax.all_to_all(sent, AXES, split_axis=0, concat_axis=0, tiled=True)]
    all_to_all x2, waiting for transfers between devices: 19.4 us -> 21 us  [exchange(): lax.all_to_all(sent, AXES, split_axis=0, concat_axis=0, tiled=True)]
  transfers between devices with their start and end apart: 16 -> 16, of which waited for: 8 -> 9; matrix products, arithmetic and copies ran while one was open for 0% -> 0% of each run, Pallas kernels for 21% -> 21%
where the time goes in v5:
time: 101 us; the launch traced here: 100 us
  waiting for transfers between devices  44.6 us (44%)
  Pallas kernels  28.1 us (28%)
  starting transfers between devices  26 us (26%)
  local copies, waits for them, and re-layouts  1.25 us (1%)
    ppermute x14, waiting for transfers between devices, swap(): lax.ppermute(block, AXES, [(device, device ^ mask_of(index, group)) for d...  23.6 us
    all_to_all x2, waiting for transfers between devices, exchange(): lax.all_to_all(sent, AXES, split_axis=0, concat_axis=0, tiled=True)  21 us
    ppermute x14, starting transfers between devices, swap(): lax.ppermute(block, AXES, [(device, device ^ mask_of(index, group)) for d...  17.9 us
    pallas_call x1, Pallas kernels, space_call(): pl.pallas_call(partial(space_kernel, groups, len(before)), grid=(clips,),...  9.09 us
    all_to_all x2, starting transfers between devices, exchange(): lax.all_to_all(sent, AXES, split_axis=0, concat_axis=0, tiled=True)  8.1 us
    pallas_call x1, Pallas kernels, time_wide_call(): pl.pallas_call(partial(time_wide_kernel, patch_here), in_specs=[pl.BlockS...  7.1 us
    pallas_call x1, Pallas kernels, space_first_call(): pl.pallas_call(partial(space_first_kernel, groups), in_specs=[ANYWHERE] *...  5.09 us
  transfers between devices with their start and end apart: 16, of which 9 were waited for; matrix products, arithmetic and copies ran while one was open for 0% of the time, Pallas kernels for 21%

profile of v5, /device:TPU:0, one launch (start us, length us, event | category | flops | bytes accessed | tf_op | source)
XLA Modules:
  0.0 100.4 jit_solution(17425897929005608803)
XLA Ops:
  0.0 5.1 %space.2 = (bf16[1,256,1024]{2,1,0:T(8,128)(2,1)}, bf16[1024,1536]{1,0:T(8,128)(2,1)S(1)}, bf16[512,1024]{1,0:T(8,128)(2,1)S(1)}, bf16[8,1,8,1024]{3,2,1,0:T(8,1...) custom-call(bf16[4,256,1024]{2,1,0:T(8,128)(2,1)} %bitcast.26, ...), custom_call_target="tpu_custom_call" | custom-call | flops 1610612736 | bytes 5767168 | tf_op jit(solution)/shard_map/space/pallas_call | solution.py:352
  5.1 3.1 %collective-permute-start = (bf16[1,2,4,1,8,1024]{5,4,3,2,1,0:T(8,128)(2,1)S(1)}, bf16[1,2,4,1,8,1024]{5,4,3,2,1,0:T(8,128)(2,1)S(1)}, u32[]{:S(2)}, u32[]{:S(2)}) collective-permute-start(bf16[1,2,4,1,8,1024]{5,4,3,2,1,0:T(8,128)(2,1)S(1)} %bitcast.22), channel_id=1, source_target_pairs={{0,2},{1,3},{2,0},{3,1},{4,6},{5,7},{6,4},{7,5},{8,10},{9,11},{10,... | collective-permute-start | bytes 393224 | tf_op jit(solution)/shard_map/ppermute | solution.py:295
  8.2 2.6 %collective-permute-start.1 = (bf16[1,2,4,1,8,1024]{5,4,3,2,1,0:T(8,128)(2,1)S(1)}, bf16[1,2,4,1,8,1024]{5,4,3,2,1,0:T(8,128)(2,1)S(1)}, u32[]{:S(2)}, u32[]{:S(2)}) collective-permute-start(bf16[1,2,4,1,8,1024]{5,4,3,2,1,0:T(8,128)(2,1)S(1)} %bitcast.21), channel_id=1, source_target_pairs={{0,4},{1,5},{2,6},{3,7},{4,0},{5,1},{6,2},{7,3},{8,12},{9,13},{10,... | collective-permute-start | bytes 393224 | tf_op jit(solution)/shard_map/ppermute | solution.py:295
  10.8 9.1 %space.3 = (bf16[3,256,1024]{2,1,0:T(8,128)(2,1)}, bf16[32,3,8,1024]{3,2,1,0:T(8,128)(2,1)}) custom-call(bf16[4,256,1024]{2,1,0:T(8,128)(2,1)} %bitcast.27, f32[1,1024]{1,0:T(1,128)} %bitcast.29, bf16[1024,1536]{1,0:T(8,128)(2,1)S(1)} %get-tuple-element.18.project_ref, bf16[512,1024]{1,0:T(8,128)(2,1)S(1)} %get-tuple-element.19.output_ref, ...), custom_call_target="tpu_custom_call" | custom-call | flops 4831838208 | bytes 8912896 | tf_op jit(solution)/shard_map/space/pallas_call | solution.py:323
  19.9 1.2 %collective-permute-done.1.refs_2_ = bf16[1,2,4,1,8,1024]{5,4,3,2,1,0:T(8,128)(2,1)S(1)} collective-permute-done((bf16[1,2,4,1,8,1024]{5,4,3,2,1,0:T(8,128)(2,1)S(1)}, bf16[1,2,4,1,8,1024]{5,4,3,2,1,0:T(8,128)(2,1)S(1)}, u32[]{:S(2)}, u32[]{:S(2)}) %collective-permute-start.1) | collective-permute-done | bytes 131104 | tf_op jit(solution)/shard_map/ppermute | solution.py:295
  21.1 5.2 %all-to-all-start = ((bf16[32,3,8,1024]{3,2,1,0:T(8,128)(2,1)}), bf16[32,3,8,1024]{3,2,1,0:T(8,128)(2,1)S(1)}, u32[]{:S(2)}, u32[]{:S(2)}) async-start(bf16[32,3,8,1024]{3,2,1,0:T(8,128)(2,1)} %after.2), calls=%async_computation | async-start | bytes 3145728 | tf_op jit(solution)/shard_map/all_to_all | solution.py:243
  26.5 0.3 collective-permute-start.3
  26.8 1.3 %collective-permute-done.3.awaited_ref = bf16[4,1,4,1,8,1024]{5,4,3,2,1,0:T(8,128)(2,1)S(1)} collective-permute-done((bf16[4,1,4,1,8,1024]{5,4,3,2,1,0:T(8,128)(2,1)S(1)}, bf16[4,1,4,1,8,1024]{5,4,3,2,1,0:T(8,128)(2,1)S(1)}, u32[]{:S(2)}, u32[]{:S(2)}) %collective-permute-start.3) | collective-permute-done | bytes 262176 | tf_op jit(solution)/shard_map/ppermute | solution.py:295
  28.1 1.8 %collective-permute-start.4 = (bf16[4,2,1,1,8,1024]{5,4,3,2,1,0:T(8,128)(2,1)S(1)}, bf16[4,2,1,1,8,1024]{5,4,3,2,1,0:T(8,128)(2,1)S(1)}, u32[]{:S(2)}, u32[]{:S(2)}) collective-permute-start(bf16[4,2,1,1,8,1024]{5,4,3,2,1,0:T(8,128)(2,1)S(1)} %get-tuple-element.32), channel_id=1, source_target_pairs={{0,16},{1,17},{2,18},{3,19},{4,20},{5,21},{6,22},{7,23},{8,24},{9,... | collective-permute-start | bytes 393224 | tf_op jit(solution)/shard_map/ppermute | solution.py:295
  30.0 1.5 %collective-permute-start.6 = (bf16[4,2,1,1,8,1024]{5,4,3,2,1,0:T(8,128)(2,1)S(1)}, bf16[4,2,1,1,8,1024]{5,4,3,2,1,0:T(8,128)(2,1)S(1)}, u32[]{:S(2)}, u32[]{:S(2)}) collective-permute-start(bf16[4,2,1,1,8,1024]{5,4,3,2,1,0:T(8,128)(2,1)S(1)} %get-tuple-element.33), channel_id=1, source_target_pairs={{0,17},{1,16},{2,19},{3,18},{4,21},{5,20},{6,23},{7,22},{8,25},{9,... | collective-permute-start | bytes 393224 | tf_op jit(solution)/shard_map/ppermute | solution.py:295
  31.4 0.3 collective-permute-start.5
  31.7 1.9 %load.1.project_ref = bf16[1024,1536]{1,0:T(8,128)(2,1)S(1)} custom-call(bf16[1024,1536]{1,0:T(8,128)(2,1)} %project_ref.3, bf16[4,1,4,1,8,1024]{5,4,3,2,1,0:T(8,128)(2,1)S(1)} %collective-permute-done.3.awaited_ref), custom_call_target="tpu_custom_call" | custom-call | bytes 6291456 | tf_op jit(solution)/shard_map/load/pallas_call | solution.py:264
  33.6 16.6 %collective-permute-done.4 = bf16[4,2,1,1,8,1024]{5,4,3,2,1,0:T(8,128)(2,1)S(1)} collective-permute-done((bf16[4,2,1,1,8,1024]{5,4,3,2,1,0:T(8,128)(2,1)S(1)}, bf16[4,2,1,1,8,1024]{5,4,3,2,1,0:T(8,128)(2,1)S(1)}, u32[]{:S(2)}, u32[]{:S(2)}) %collective-permute-start.4) | collective-permute-done | bytes 131104 | tf_op jit(solution)/shard_map/ppermute | solution.py:295
  50.2 0.2 collective-permute-done.5
  50.4 1.8 %time.2 = (bf16[8,1,8,512]{3,2,1,0:T(8,128)(2,1)S(1)}, bf16[8,1,8,512]{3,2,1,0:T(8,128)(2,1)S(1)}, bf16[8,1,8,512]{3,2,1,0:T(8,128)(2,1)S(1)}, bf16[8,1,8,512]{3,2,1,0:T(8,128)(2,1)S(1)}) custom-call(bf16[32,1,8,1024]{3,2,1,0:T(8,128)(2,1)S(1)} %bitcast.17, bf16[1024,1536]{1,0:T(8,128)(2,1)S(1)} %load.1.project_ref), custom_call_target="tpu_custom_call" | custom-call | flops 1342177280 | bytes 4194304 | tf_op jit(solution)/shard_map/time/pallas_call | solution.py:380
  52.2 0.1 collective-permute-start.8
  52.3 1.5 %collective-permute-start.7 = (bf16[1,4,2,1,8,512]{5,4,3,2,1,0:T(8,128)(2,1)S(1)}, bf16[1,4,2,1,8,512]{5,4,3,2,1,0:T(8,128)(2,1)S(1)}, u32[]{:S(2)}, u32[]{:S(2)}) collective-permute-start(bf16[1,4,2,1,8,512]{5,4,3,2,1,0:T(8,128)(2,1)S(1)} %bitcast.24), channel_id=1, source_target_pairs={{0,16},{1,17},{2,18},{3,19},{4,20},{5,21},{6,22},{7,23},{8,24},{9,... | collective-permute-start | bytes 196616 | tf_op jit(solution)/shard_map/ppermute | solution.py:295
  53.8 1.9 %collective-permute-start.9 = (bf16[1,4,2,1,8,512]{5,4,3,2,1,0:T(8,128)(2,1)S(1)}, bf16[1,4,2,1,8,512]{5,4,3,2,1,0:T(8,128)(2,1)S(1)}, u32[]{:S(2)}, u32[]{:S(2)}) collective-permute-start(bf16[1,4,2,1,8,512]{5,4,3,2,1,0:T(8,128)(2,1)S(1)} %bitcast.23), channel_id=1, source_target_pairs={{0,17},{1,16},{2,19},{3,18},{4,21},{5,20},{6,23},{7,22},{8,25},{9,... | collective-permute-start | bytes 196616 | tf_op jit(solution)/shard_map/ppermute | solution.py:295
  55.8 1.4 %collective-permute-done.8 = bf16[1,4,2,1,8,512]{5,4,3,2,1,0:T(8,128)(2,1)S(1)} collective-permute-done((bf16[1,4,2,1,8,512]{5,4,3,2,1,0:T(8,128)(2,1)S(1)}, bf16[1,4,2,1,8,512]{5,4,3,2,1,0:T(8,128)(2,1)S(1)}, u32[]{:S(2)}, u32[]{:S(2)}) %collective-permute-start.8) | collective-permute-done | bytes 65568 | tf_op jit(solution)/shard_map/ppermute | solution.py:295
  57.2 1.8 %collective-permute-done.9 = bf16[1,4,2,1,8,512]{5,4,3,2,1,0:T(8,128)(2,1)S(1)} collective-permute-done((bf16[1,4,2,1,8,512]{5,4,3,2,1,0:T(8,128)(2,1)S(1)}, bf16[1,4,2,1,8,512]{5,4,3,2,1,0:T(8,128)(2,1)S(1)}, u32[]{:S(2)}, u32[]{:S(2)}) %collective-permute-start.9) | collective-permute-done | bytes 65568 | tf_op jit(solution)/shard_map/ppermute | solution.py:295
  59.1 2.1 %collective-permute-start.12 = (bf16[4,1,2,1,8,512]{5,4,3,2,1,0:T(8,128)(2,1)S(1)}, bf16[4,1,2,1,8,512]{5,4,3,2,1,0:T(8,128)(2,1)S(1)}, u32[]{:S(2)}, u32[]{:S(2)}) collective-permute-start(bf16[4,1,2,1,8,512]{5,4,3,2,1,0:T(8,128)(2,1)S(1)} %get-tuple-element.40), channel_id=1, source_target_pairs={{0,6},{1,7},{2,4},{3,5},{4,2},{5,3},{6,0},{7,1},{8,14},{9,15},{10,... | collective-permute-start | bytes 196616 | tf_op jit(solution)/shard_map/ppermute | solution.py:295
  61.2 1.2 %collective-permute-start.11 = (bf16[4,1,2,1,8,512]{5,4,3,2,1,0:T(8,128)(2,1)S(1)}, bf16[4,1,2,1,8,512]{5,4,3,2,1,0:T(8,128)(2,1)S(1)}, u32[]{:S(2)}, u32[]{:S(2)}) collective-permute-start(bf16[4,1,2,1,8,512]{5,4,3,2,1,0:T(8,128)(2,1)S(1)} %get-tuple-element.41), channel_id=1, source_target_pairs={{0,4},{1,5},{2,6},{3,7},{4,0},{5,1},{6,2},{7,3},{8,12},{9,13},{10,... | collective-permute-start | bytes 196616 | tf_op jit(solution)/shard_map/ppermute | solution.py:295
  62.3 1.2 %collective-permute-start.10 = (bf16[4,1,2,1,8,512]{5,4,3,2,1,0:T(8,128)(2,1)S(1)}, bf16[4,1,2,1,8,512]{5,4,3,2,1,0:T(8,128)(2,1)S(1)}, u32[]{:S(2)}, u32[]{:S(2)}) collective-permute-start(bf16[4,1,2,1,8,512]{5,4,3,2,1,0:T(8,128)(2,1)S(1)} %get-tuple-element.42), channel_id=1, source_target_pairs={{0,2},{1,3},{2,0},{3,1},{4,6},{5,7},{6,4},{7,5},{8,10},{9,11},{10,... | collective-permute-start | bytes 196616 | tf_op jit(solution)/shard_map/ppermute | solution.py:295
  63.5 3.0 %all-to-all-done.rows_ref = bf16[32,3,8,1024]{3,2,1,0:T(8,128)(2,1)S(1)} async-done(((bf16[32,3,8,1024]{3,2,1,0:T(8,128)(2,1)}), bf16[32,3,8,1024]{3,2,1,0:T(8,128)(2,1)S(1)}, u32[]{:S(2)}, u32[]{:S(2)}) %all-to-all-start) | async-done | bytes 1572896 | tf_op jit(solution)/shard_map/all_to_all | solution.py:243
  66.6 7.1 %time.3.refs_0_ = bf16[32,3,8,512]{3,2,1,0:T(8,128)(2,1)} custom-call(bf16[32,3,8,1024]{3,2,1,0:T(8,128)(2,1)S(1)} %all-to-all-done.rows_ref, bf16[1024,1536]{1,0:T(8,128)(2,1)} %project_ref.3, bf16[8,1,8,512]{3,2,1,0:T(8,128)(2,1)} %copy-done.3), custom_call_target="tpu_custom_call" | custom-call | flops 4026531840 | bytes 6291456 | tf_op jit(solution)/shard_map/time/pallas_call | solution.py:399
  73.7 2.9 %all-to-all-start.1 = ((bf16[32,3,8,512]{3,2,1,0:T(8,128)(2,1)}), bf16[32,3,8,512]{3,2,1,0:T(8,128)(2,1)S(1)}, u32[]{:S(2)}, u32[]{:S(2)}) async-start(bf16[32,3,8,512]{3,2,1,0:T(8,128)(2,1)} %after.3), calls=%async_computation.1 | async-start | bytes 1572864 | tf_op jit(solution)/shard_map/all_to_all | solution.py:243
  76.7 0.3 collective-permute-start.13
  77.0 1.1 %collective-permute-done.13 = bf16[4,4,1,1,8,512]{5,4,3,2,1,0:T(8,128)(2,1)S(1)} collective-permute-done((bf16[4,4,1,1,8,512]{5,4,3,2,1,0:T(8,128)(2,1)S(1)}, bf16[4,4,1,1,8,512]{5,4,3,2,1,0:T(8,128)(2,1)S(1)}, u32[]{:S(2)}, u32[]{:S(2)}) %collective-permute-start.13) | collective-permute-done | bytes 131104 | tf_op jit(solution)/shard_map/ppermute | solution.py:295
  78.2 1.1 %copy-done.2 = bf16[1,256,1024]{2,1,0:T(8,128)(2,1)S(1)} copy-done((bf16[1,256,1024]{2,1,0:T(8,128)(2,1)S(1)}, bf16[1,256,1024]{2,1,0:T(8,128)(2,1)}, u32[]{:S(2)}) %copy-start.2) | copy-done | bytes 524312
  79.3 1.3 %final.2.before_ref = bf16[4,256,1024]{2,1,0:T(8,128)(2,1)} custom-call(bf16[1,256,1024]{2,1,0:T(8,128)(2,1)S(1)} %copy-done.2, bf16[32,1,8,512]{3,2,1,0:T(8,128)(2,1)S(1)} %bitcast.16, bf16[512,1024]{1,0:T(8,128)(2,1)S(1)} %copy-done), custom_call_target="tpu_custom_call" | custom-call | flops 268435456 | bytes 2621440 | tf_op jit(solution)/shard_map/final/pallas_call | solution.py:423
  80.6 18.0 %all-to-all-done.1.context_ref = bf16[32,3,8,512]{3,2,1,0:T(8,128)(2,1)S(1)} async-done(((bf16[32,3,8,512]{3,2,1,0:T(8,128)(2,1)}), bf16[32,3,8,512]{3,2,1,0:T(8,128)(2,1)S(1)}, u32[]{:S(2)}, u32[]{:S(2)}) %all-to-all-start.1) | async-done | bytes 786464 | tf_op jit(solution)/shard_map/all_to_all | solution.py:243
  98.6 1.8 %final.3 = bf16[4,256,1024]{2,1,0:T(8,128)(2,1)} custom-call(bf16[3,256,1024]{2,1,0:T(8,128)(2,1)S(1)} %copy-done.1, bf16[32,3,8,512]{3,2,1,0:T(8,128)(2,1)S(1)} %all-to-all-done.1.context_ref, bf16[512,1024]{1,0:T(8,128)(2,1)S(1)} %copy-done, bf16[4,256,1024]{2,1,0:T(8,128)(2,1)} %final.2.before_ref), custom_call_target="tpu_custom_call", output_to_operand_aliasing={{}: (3, {})} | custom-call | flops 805306368 | bytes 5767168 | tf_op jit(solution)/shard_map/final/pallas_call | solution.py:444
  (26 shorter events, 0.4 us)
Async XLA Ops:
  5.1 14.8 %collective-permute-start = (bf16[1,2,4,1,8,1024]{5,4,3,2,1,0:T(8,128)(2,1)S(1)}, bf16[1,2,4,1,8,1024]{5,4,3,2,1,0:T(8,128)(2,1)S(1)}, u32[]{:S(2)}, u32[]{:S(2)}) collective-permute-start(bf16[1,2,4,1,8,1024]{5,4,3,2,1,0:T(8,128)(2,1)S(1)} %bitcast.22), channel_id=1, source_target_pairs={{0,2},{1,3},{2,0},{3,1},{4,6},{5,7},{6,4},{7,5},{8,10},{9,11},{10,... | collective-permute-start | bytes 393224 | tf_op jit(solution)/shard_map/ppermute | solution.py:295
  8.2 12.9 %collective-permute-start.1 = (bf16[1,2,4,1,8,1024]{5,4,3,2,1,0:T(8,128)(2,1)S(1)}, bf16[1,2,4,1,8,1024]{5,4,3,2,1,0:T(8,128)(2,1)S(1)}, u32[]{:S(2)}, u32[]{:S(2)}) collective-permute-start(bf16[1,2,4,1,8,1024]{5,4,3,2,1,0:T(8,128)(2,1)S(1)} %bitcast.21), channel_id=1, source_target_pairs={{0,4},{1,5},{2,6},{3,7},{4,0},{5,1},{6,2},{7,3},{8,12},{9,13},{10,... | collective-permute-start | bytes 393224 | tf_op jit(solution)/shard_map/ppermute | solution.py:295
  10.8 10.3 %collective-permute-start.2 = (bf16[1,2,4,1,8,1024]{5,4,3,2,1,0:T(8,128)(2,1)S(1)}, bf16[1,2,4,1,8,1024]{5,4,3,2,1,0:T(8,128)(2,1)S(1)}, u32[]{:S(2)}, u32[]{:S(2)}) collective-permute-start(bf16[1,2,4,1,8,1024]{5,4,3,2,1,0:T(8,128)(2,1)S(1)} %bitcast.20), channel_id=1, source_target_pairs={{0,6},{1,7},{2,4},{3,5},{4,2},{5,3},{6,0},{7,1},{8,14},{9,15},{10,... | collective-permute-start | bytes 393224 | tf_op jit(solution)/shard_map/ppermute | solution.py:295
  21.1 45.5 %all-to-all-start = ((bf16[32,3,8,1024]{3,2,1,0:T(8,128)(2,1)}), bf16[32,3,8,1024]{3,2,1,0:T(8,128)(2,1)S(1)}, u32[]{:S(2)}, u32[]{:S(2)}) async-start(bf16[32,3,8,1024]{3,2,1,0:T(8,128)(2,1)} %after.2), calls=%async_computation | async-start | bytes 3145728 | tf_op jit(solution)/shard_map/all_to_all | solution.py:243
  26.5 1.6 %collective-permute-start.3 = (bf16[4,1,4,1,8,1024]{5,4,3,2,1,0:T(8,128)(2,1)S(1)}, bf16[4,1,4,1,8,1024]{5,4,3,2,1,0:T(8,128)(2,1)S(1)}, u32[]{:S(2)}, u32[]{:S(2)}) collective-permute-start(bf16[4,1,4,1,8,1024]{5,4,3,2,1,0:T(8,128)(2,1)S(1)} %get-tuple-element.36), channel_id=1, source_target_pairs={{0,8},{1,9},{2,10},{3,11},{4,12},{5,13},{6,14},{7,15},{8,0},{9,1},... | collective-permute-start | bytes 786440 | tf_op jit(solution)/shard_map/ppermute | solution.py:295
  28.1 22.1 %collective-permute-start.4 = (bf16[4,2,1,1,8,1024]{5,4,3,2,1,0:T(8,128)(2,1)S(1)}, bf16[4,2,1,1,8,1024]{5,4,3,2,1,0:T(8,128)(2,1)S(1)}, u32[]{:S(2)}, u32[]{:S(2)}) collective-permute-start(bf16[4,2,1,1,8,1024]{5,4,3,2,1,0:T(8,128)(2,1)S(1)} %get-tuple-element.32), channel_id=1, source_target_pairs={{0,16},{1,17},{2,18},{3,19},{4,20},{5,21},{6,22},{7,23},{8,24},{9,... | collective-permute-start | bytes 393224 | tf_op jit(solution)/shard_map/ppermute | solution.py:295
  30.0 20.2 %collective-permute-start.6 = (bf16[4,2,1,1,8,1024]{5,4,3,2,1,0:T(8,128)(2,1)S(1)}, bf16[4,2,1,1,8,1024]{5,4,3,2,1,0:T(8,128)(2,1)S(1)}, u32[]{:S(2)}, u32[]{:S(2)}) collective-permute-start(bf16[4,2,1,1,8,1024]{5,4,3,2,1,0:T(8,128)(2,1)S(1)} %get-tuple-element.33), channel_id=1, source_target_pairs={{0,17},{1,16},{2,19},{3,18},{4,21},{5,20},{6,23},{7,22},{8,25},{9,... | collective-permute-start | bytes 393224 | tf_op jit(solution)/shard_map/ppermute | solution.py:295
  31.4 18.9 %collective-permute-start.5 = (bf16[4,2,1,1,8,1024]{5,4,3,2,1,0:T(8,128)(2,1)S(1)}, bf16[4,2,1,1,8,1024]{5,4,3,2,1,0:T(8,128)(2,1)S(1)}, u32[]{:S(2)}, u32[]{:S(2)}) collective-permute-start(bf16[4,2,1,1,8,1024]{5,4,3,2,1,0:T(8,128)(2,1)S(1)} %get-tuple-element.34), channel_id=1, source_target_pairs={{0,1},{1,0},{2,3},{3,2},{4,5},{5,4},{6,7},{7,6},{8,9},{9,8},{10,11... | collective-permute-start | bytes 393224 | tf_op jit(solution)/shard_map/ppermute | solution.py:295
  52.2 14.3 %copy-start.3 = (bf16[8,1,8,512]{3,2,1,0:T(8,128)(2,1)}, bf16[8,1,8,512]{3,2,1,0:T(8,128)(2,1)S(1)}, u32[]{:S(2)}) copy-start(bf16[8,1,8,512]{3,2,1,0:T(8,128)(2,1)S(1)} %get-tuple-element.27.before_ref) | copy-start | bytes 196612
  52.2 5.0 %collective-permute-start.8 = (bf16[1,4,2,1,8,512]{5,4,3,2,1,0:T(8,128)(2,1)S(1)}, bf16[1,4,2,1,8,512]{5,4,3,2,1,0:T(8,128)(2,1)S(1)}, u32[]{:S(2)}, u32[]{:S(2)}) collective-permute-start(bf16[1,4,2,1,8,512]{5,4,3,2,1,0:T(8,128)(2,1)S(1)} %bitcast.25), channel_id=1, source_target_pairs={{0,1},{1,0},{2,3},{3,2},{4,5},{5,4},{6,7},{7,6},{8,9},{9,8},{10,11... | collective-permute-start | bytes 196616 | tf_op jit(solution)/shard_map/ppermute | solution.py:295
  52.3 4.9 %collective-permute-start.7 = (bf16[1,4,2,1,8,512]{5,4,3,2,1,0:T(8,128)(2,1)S(1)}, bf16[1,4,2,1,8,512]{5,4,3,2,1,0:T(8,128)(2,1)S(1)}, u32[]{:S(2)}, u32[]{:S(2)}) collective-permute-start(bf16[1,4,2,1,8,512]{5,4,3,2,1,0:T(8,128)(2,1)S(1)} %bitcast.24), channel_id=1, source_target_pairs={{0,16},{1,17},{2,18},{3,19},{4,20},{5,21},{6,22},{7,23},{8,24},{9,... | collective-permute-start | bytes 196616 | tf_op jit(solution)/shard_map/ppermute | solution.py:295
  53.8 5.2 %collective-permute-start.9 = (bf16[1,4,2,1,8,512]{5,4,3,2,1,0:T(8,128)(2,1)S(1)}, bf16[1,4,2,1,8,512]{5,4,3,2,1,0:T(8,128)(2,1)S(1)}, u32[]{:S(2)}, u32[]{:S(2)}) collective-permute-start(bf16[1,4,2,1,8,512]{5,4,3,2,1,0:T(8,128)(2,1)S(1)} %bitcast.23), channel_id=1, source_target_pairs={{0,17},{1,16},{2,19},{3,18},{4,21},{5,20},{6,23},{7,22},{8,25},{9,... | collective-permute-start | bytes 196616 | tf_op jit(solution)/shard_map/ppermute | solution.py:295
  59.1 14.6 %collective-permute-start.12 = (bf16[4,1,2,1,8,512]{5,4,3,2,1,0:T(8,128)(2,1)S(1)}, bf16[4,1,2,1,8,512]{5,4,3,2,1,0:T(8,128)(2,1)S(1)}, u32[]{:S(2)}, u32[]{:S(2)}) collective-permute-start(bf16[4,1,2,1,8,512]{5,4,3,2,1,0:T(8,128)(2,1)S(1)} %get-tuple-element.40), channel_id=1, source_target_pairs={{0,6},{1,7},{2,4},{3,5},{4,2},{5,3},{6,0},{7,1},{8,14},{9,15},{10,... | collective-permute-start | bytes 196616 | tf_op jit(solution)/shard_map/ppermute | solution.py:295
  61.2 12.5 %collective-permute-start.11 = (bf16[4,1,2,1,8,512]{5,4,3,2,1,0:T(8,128)(2,1)S(1)}, bf16[4,1,2,1,8,512]{5,4,3,2,1,0:T(8,128)(2,1)S(1)}, u32[]{:S(2)}, u32[]{:S(2)}) collective-permute-start(bf16[4,1,2,1,8,512]{5,4,3,2,1,0:T(8,128)(2,1)S(1)} %get-tuple-element.41), channel_id=1, source_target_pairs={{0,4},{1,5},{2,6},{3,7},{4,0},{5,1},{6,2},{7,3},{8,12},{9,13},{10,... | collective-permute-start | bytes 196616 | tf_op jit(solution)/shard_map/ppermute | solution.py:295
  62.3 11.4 %collective-permute-start.10 = (bf16[4,1,2,1,8,512]{5,4,3,2,1,0:T(8,128)(2,1)S(1)}, bf16[4,1,2,1,8,512]{5,4,3,2,1,0:T(8,128)(2,1)S(1)}, u32[]{:S(2)}, u32[]{:S(2)}) collective-permute-start(bf16[4,1,2,1,8,512]{5,4,3,2,1,0:T(8,128)(2,1)S(1)} %get-tuple-element.42), channel_id=1, source_target_pairs={{0,2},{1,3},{2,0},{3,1},{4,6},{5,7},{6,4},{7,5},{8,10},{9,11},{10,... | collective-permute-start | bytes 196616 | tf_op jit(solution)/shard_map/ppermute | solution.py:295
  73.7 4.5 %copy-start = (bf16[512,1024]{1,0:T(8,128)(2,1)S(1)}, bf16[512,1024]{1,0:T(8,128)(2,1)}, u32[]{:S(2)}) copy-start(bf16[512,1024]{1,0:T(8,128)(2,1)} %output_ref.5) | copy-start | bytes 3145732
  73.7 24.9 %all-to-all-start.1 = ((bf16[32,3,8,512]{3,2,1,0:T(8,128)(2,1)}), bf16[32,3,8,512]{3,2,1,0:T(8,128)(2,1)S(1)}, u32[]{:S(2)}, u32[]{:S(2)}) async-start(bf16[32,3,8,512]{3,2,1,0:T(8,128)(2,1)} %after.3), calls=%async_computation.1 | async-start | bytes 1572864 | tf_op jit(solution)/shard_map/all_to_all | solution.py:243
  76.7 1.4 %collective-permute-start.13 = (bf16[4,4,1,1,8,512]{5,4,3,2,1,0:T(8,128)(2,1)S(1)}, bf16[4,4,1,1,8,512]{5,4,3,2,1,0:T(8,128)(2,1)S(1)}, u32[]{:S(2)}, u32[]{:S(2)}) collective-permute-start(bf16[4,4,1,1,8,512]{5,4,3,2,1,0:T(8,128)(2,1)S(1)} %get-tuple-element.38), channel_id=1, source_target_pairs={{0,8},{1,9},{2,10},{3,11},{4,12},{5,13},{6,14},{7,15},{8,0},{9,1},... | collective-permute-start | bytes 393224 | tf_op jit(solution)/shard_map/ppermute | solution.py:295
  78.1 20.5 %copy-start.1 = (bf16[3,256,1024]{2,1,0:T(8,128)(2,1)S(1)}, bf16[3,256,1024]{2,1,0:T(8,128)(2,1)}, u32[]{:S(2)}) copy-start(bf16[3,256,1024]{2,1,0:T(8,128)(2,1)} %get-tuple-element.21.mixed_ref) | copy-start | bytes 4718596
  78.2 1.2 %copy-start.2 = (bf16[1,256,1024]{2,1,0:T(8,128)(2,1)S(1)}, bf16[1,256,1024]{2,1,0:T(8,128)(2,1)}, u32[]{:S(2)}) copy-start(bf16[1,256,1024]{2,1,0:T(8,128)(2,1)} %get-tuple-element.20.refs_0_.mixed_ref) | copy-start | bytes 1572868

commit v6 on v5

--- a/solution.py
+++ b/solution.py
@@ -91,7 +91,7 @@
 def space_first_kernel(
     groups, video_ref, gain_ref, project_ref, output_ref, time_gain_ref, mixed_ref, project, output, *refs
 ):
-    *sent_refs, frame, gains, mixed, scratch, sems = refs
+    *sent_refs, frame, gains, scratch, sems = refs
     parts = sent_refs[0].shape[0]
     frame_copy = pltpu.make_async_copy(video_ref.at[0], frame, sems.at[0])
     gain_copy = pltpu.make_async_copy(gain_ref, gains.at[pl.ds(0, 1)], sems.at[1])
@@ -100,27 +100,34 @@
         pltpu.make_async_copy(output_ref, output, sems.at[3]),
         pltpu.make_async_copy(time_gain_ref, gains.at[pl.ds(1, 1)], sems.at[4]),
     ]
-    mixed_copy = pltpu.make_async_copy(mixed, mixed_ref.at[0], sems.at[5])
-    for copy in (gain_copy, frame_copy, *weight_copies):
+    for copy in (gain_copy, frame_copy, weight_copies[0]):
         copy.start()
     gain_copy.wait()
     frame_copy.wait()
+    for copy in weight_copies[1:]:
+        copy.start()
     floats = frame[...].astype(jnp.float32)
     rows = normed(floats, gains[0:1]).astype(jnp.bfloat16)
-    for copy in weight_copies:
-        copy.wait()
+    weight_copies[0].wait()
     heads = jnp.dot(rows, project[...], preferred_element_type=jnp.float32).astype(jnp.bfloat16)
     context = attend(heads, None)
+    for copy in weight_copies[1:]:
+        copy.wait()
     here = (floats + jnp.dot(context, output[...], preferred_element_type=jnp.float32)).astype(jnp.bfloat16)
-    mixed[...] = here
-    mixed_copy.start()
+    mixed_ref[0] = here
     sent = normed(here.astype(jnp.float32), gains[1:2])
     put(sent.reshape(scratch.shape).astype(jnp.bfloat16), scratch, sent_refs, groups)
-    mixed_copy.wait()
 
 
 def space_kernel(groups, extra, video_ref, gain_ref, project_ref, output_ref, time_gain_ref, *refs):
-    mixed_ref, *sent_refs = refs[extra:]
+    if extra:
+        before_ref, stored_ref, *refs = refs
+
+        @pl.when(pl.program_id(0) == 0)
+        def _():
+            stored_ref[...] = before_ref[...]
+
+    mixed_ref, *sent_refs = refs
     sent_refs, scratch = (sent_refs, None) if groups is None else (sent_refs[:-1], sent_refs[-1])
     floats = video_ref[0].astype(jnp.float32)
     heads = jnp.dot(
@@ -320,7 +327,7 @@
     rows, width = video.shape[1:]
     vmem = pl.BlockSpec(memory_space=pltpu.VMEM)
     shapes, specs, scratch = sent_specs(count, clips, rows // count, width, groups)
-    mixed, *sent = pl.pallas_call(
+    outputs = pl.pallas_call(
         partial(space_kernel, groups, len(before)),
         grid=(clips,),
         in_specs=[
@@ -330,9 +337,11 @@
             whole((WIDTH, width)),
             whole((1, width)),
         ]
-        + [ANYWHERE] * len(before),
-        out_specs=[pl.BlockSpec((1, rows, width), lambda c: (c, 0, 0)), *specs],
-        out_shape=[pltpu.HBM((clips, rows, width), jnp.bfloat16), *(pltpu.HBM(shape.shape, jnp.bfloat16) for shape in shapes)],
+        + [vmem] * len(before),
+        out_specs=[whole((1, rows, width))] * len(before)
+        + [pl.BlockSpec((1, rows, width), lambda c: (c, 0, 0)), *specs],
+        out_shape=[pltpu.HBM((1, rows, width), jnp.bfloat16)] * len(before)
+        + [pltpu.HBM((clips, rows, width), jnp.bfloat16), *(pltpu.HBM(shape.shape, jnp.bfloat16) for shape in shapes)],
         scratch_shapes=scratch,
         cost_estimate=cost(
             clips * rows * (width * 4 * WIDTH + 8 * rows * WIDTH), 2 * (4 * width * WIDTH + 3 * clips * rows * width),
@@ -340,8 +349,8 @@
         ),
         compiler_params=pltpu.CompilerParams(vmem_limit_bytes=SPACE_VMEM_LIMIT),
         name="space",
-    )(in_hbm(video), in_hbm(space_gain), in_vmem(space_project), in_vmem(space_output), in_hbm(time_gain), *map(in_hbm, before))
-    return mixed, sent
+    )(in_hbm(video), in_hbm(space_gain), in_vmem(space_project), in_vmem(space_output), in_hbm(time_gain), *map(in_vmem, before))
+    return outputs[: len(before)], outputs[len(before)], outputs[len(before) + 1 :]
 
 
 def space_first_call(video, space_gain, space_project, space_output, time_gain, count, groups):
@@ -352,9 +361,9 @@
     mixed, project, output, *sent = pl.pallas_call(
         partial(space_first_kernel, groups),
         in_specs=[ANYWHERE] * 5,
-        out_specs=[ANYWHERE, vmem, vmem, *[vmem] * len(shapes)],
+        out_specs=[vmem, vmem, vmem, *[vmem] * len(shapes)],
         out_shape=[
-            pltpu.HBM((1, rows, width), jnp.bfloat16),
+            pltpu.VMEM((1, rows, width), jnp.bfloat16),
             pltpu.VMEM(space_project.shape, jnp.bfloat16),
             pltpu.VMEM(space_output.shape, jnp.bfloat16),
             *[pltpu.VMEM(shape.shape, jnp.bfloat16) for shape in shapes],
@@ -362,9 +371,8 @@
         scratch_shapes=[
             pltpu.VMEM((rows, width), jnp.bfloat16),
             pltpu.VMEM((2, width), jnp.float32),
-            pltpu.VMEM((rows, width), jnp.bfloat16),
             *scratch,
-            pltpu.SemaphoreType.DMA((6,)),
+            pltpu.SemaphoreType.DMA((5,)),
         ],
         cost_estimate=cost(rows * (width * 4 * WIDTH + 8 * rows * WIDTH), 2 * (4 * width * WIDTH + 3 * rows * width), 0),
         compiler_params=pltpu.CompilerParams(vmem_limit_bytes=SPACE_VMEM_LIMIT),
@@ -468,7 +476,7 @@
     there, back = [far, core, near], [near, far, core]
     kept, project, output, sent = space_first_call(video, *weights, count, there)
     weights = weights[0], project, output, weights[3]
-    kept_others, sent_others = space_call(video, 1, others, *weights, count, [kept], None)
+    (kept,), kept_others, sent_others = space_call(video, 1, others, *weights, count, [kept], None)
     arrived, steps = swap(sent, there)
     arrived_others = exchange(after(sent_others[0], steps[0]), count, patch_here)
     loaded = load(time_project, steps[1][0])
@@ -483,7 +491,7 @@
 
 def plainly(video, weights, time_project, time_output, count):
     clips, rows, _ = video.shape
-    kept, sent = space_call(video, 0, clips, *weights, count, [], None)
+    _, kept, sent = space_call(video, 0, clips, *weights, count, [], None)
     arrived = exchange(sent[0], count, rows // count)
     context = time_call(arrived, clips, rows, time_project, count, [], None, None)
     returned = exchange(context[0], count, rows // count)

time: 101 us -> 100 us (0.990)
  no operation moved by 1% of the time
where the time goes in v6:
time: 100 us; the launch traced here: 99.8 us
  waiting for transfers between devices  44.6 us (45%)
  Pallas kernels  27.5 us (28%)
  starting transfers between devices  26 us (26%)
  local copies, waits for them, and re-layouts  1.25 us (1%)
    ppermute x14, waiting for transfers between devices, swap(): lax.ppermute(block, AXES, [(device, device ^ mask_of(index, group)) for d...  23.6 us
    all_to_all x2, waiting for transfers between devices, exchange(): lax.all_to_all(sent, AXES, split_axis=0, concat_axis=0, tiled=True)  21 us
    ppermute x14, starting transfers between devices, swap(): lax.ppermute(block, AXES, [(device, device ^ mask_of(index, group)) for d...  17.9 us
    pallas_call x1, Pallas kernels, space_call(): pl.pallas_call(partial(space_kernel, groups, len(before)), grid=(clips,),...  9.15 us
    all_to_all x2, starting transfers between devices, exchange(): lax.all_to_all(sent, AXES, split_axis=0, concat_axis=0, tiled=True)  8.1 us
    pallas_call x1, Pallas kernels, time_wide_call(): pl.pallas_call(partial(time_wide_kernel, patch_here), in_specs=[pl.BlockS...  7.1 us
    pallas_call x1, Pallas kernels, space_first_call(): pl.pallas_call(partial(space_first_kernel, groups), in_specs=[ANYWHERE] *...  4.5 us
  transfers between devices with their start and end apart: 16, of which 9 were waited for; matrix products, arithmetic and copies ran while one was open for 0% of the time, Pallas kernels for 21%

profile of v6, /device:TPU:0, one launch (start us, length us, event | category | flops | bytes accessed | tf_op | source)
XLA Modules:
  0.0 99.8 jit_solution(13732927472375757249)
XLA Ops:
  0.0 4.5 %space.2 = (bf16[1,256,1024]{2,1,0:T(8,128)(2,1)S(1)}, bf16[1024,1536]{1,0:T(8,128)(2,1)S(1)}, bf16[512,1024]{1,0:T(8,128)(2,1)S(1)}, bf16[8,1,8,1024]{3,2,1,0:T...) custom-call(bf16[4,256,1024]{2,1,0:T(8,128)(2,1)} %bitcast.26, ...), custom_call_target="tpu_custom_call" | custom-call | flops 1610612736 | bytes 5767168 | tf_op jit(solution)/shard_map/space/pallas_call | solution.py:361
  4.5 3.1 %collective-permute-start = (bf16[1,2,4,1,8,1024]{5,4,3,2,1,0:T(8,128)(2,1)S(1)}, bf16[1,2,4,1,8,1024]{5,4,3,2,1,0:T(8,128)(2,1)S(1)}, u32[]{:S(2)}, u32[]{:S(2)}) collective-permute-start(bf16[1,2,4,1,8,1024]{5,4,3,2,1,0:T(8,128)(2,1)S(1)} %bitcast.22), channel_id=1, source_target_pairs={{0,2},{1,3},{2,0},{3,1},{4,6},{5,7},{6,4},{7,5},{8,10},{9,11},{10,... | collective-permute-start | bytes 393224 | tf_op jit(solution)/shard_map/ppermute | solution.py:302
  7.6 2.6 %collective-permute-start.1 = (bf16[1,2,4,1,8,1024]{5,4,3,2,1,0:T(8,128)(2,1)S(1)}, bf16[1,2,4,1,8,1024]{5,4,3,2,1,0:T(8,128)(2,1)S(1)}, u32[]{:S(2)}, u32[]{:S(2)}) collective-permute-start(bf16[1,2,4,1,8,1024]{5,4,3,2,1,0:T(8,128)(2,1)S(1)} %bitcast.21), channel_id=1, source_target_pairs={{0,4},{1,5},{2,6},{3,7},{4,0},{5,1},{6,2},{7,3},{8,12},{9,13},{10,... | collective-permute-start | bytes 393224 | tf_op jit(solution)/shard_map/ppermute | solution.py:302
  10.2 9.2 %space.3 = (bf16[1,256,1024]{2,1,0:T(8,128)(2,1)}, bf16[3,256,1024]{2,1,0:T(8,128)(2,1)}, bf16[32,3,8,1024]{3,2,1,0:T(8,128)(2,1)}) custom-call(bf16[4,256,1024]{2,1,0:T(8,128)(2,1)} %bitcast.27, f32[1,1024]{1,0:T(1,128)} %bitcast.29, bf16[1024,1536]{1,0:T(8,128)(2,1)S(1)} %get-tuple-element.19.project_ref, ...), custom_call_target="tpu_custom_call" | custom-call | flops 4831838208 | bytes 8912896 | tf_op jit(solution)/shard_map/space/pallas_call | solution.py:330
  19.3 1.2 %collective-permute-done.1.refs_2_ = bf16[1,2,4,1,8,1024]{5,4,3,2,1,0:T(8,128)(2,1)S(1)} collective-permute-done((bf16[1,2,4,1,8,1024]{5,4,3,2,1,0:T(8,128)(2,1)S(1)}, bf16[1,2,4,1,8,1024]{5,4,3,2,1,0:T(8,128)(2,1)S(1)}, u32[]{:S(2)}, u32[]{:S(2)}) %collective-permute-start.1) | collective-permute-done | bytes 131104 | tf_op jit(solution)/shard_map/ppermute | solution.py:302
  20.5 5.2 %all-to-all-start = ((bf16[32,3,8,1024]{3,2,1,0:T(8,128)(2,1)}), bf16[32,3,8,1024]{3,2,1,0:T(8,128)(2,1)S(1)}, u32[]{:S(2)}, u32[]{:S(2)}) async-start(bf16[32,3,8,1024]{3,2,1,0:T(8,128)(2,1)} %after.2), calls=%async_computation | async-start | bytes 3145728 | tf_op jit(solution)/shard_map/all_to_all | solution.py:250
  25.9 0.3 collective-permute-start.3
  26.2 1.3 %collective-permute-done.3.awaited_ref = bf16[4,1,4,1,8,1024]{5,4,3,2,1,0:T(8,128)(2,1)S(1)} collective-permute-done((bf16[4,1,4,1,8,1024]{5,4,3,2,1,0:T(8,128)(2,1)S(1)}, bf16[4,1,4,1,8,1024]{5,4,3,2,1,0:T(8,128)(2,1)S(1)}, u32[]{:S(2)}, u32[]{:S(2)}) %collective-permute-start.3) | collective-permute-done | bytes 262176 | tf_op jit(solution)/shard_map/ppermute | solution.py:302
  27.5 1.8 %collective-permute-start.4 = (bf16[4,2,1,1,8,1024]{5,4,3,2,1,0:T(8,128)(2,1)S(1)}, bf16[4,2,1,1,8,1024]{5,4,3,2,1,0:T(8,128)(2,1)S(1)}, u32[]{:S(2)}, u32[]{:S(2)}) collective-permute-start(bf16[4,2,1,1,8,1024]{5,4,3,2,1,0:T(8,128)(2,1)S(1)} %get-tuple-element.34), channel_id=1, source_target_pairs={{0,16},{1,17},{2,18},{3,19},{4,20},{5,21},{6,22},{7,23},{8,24},{9,... | collective-permute-start | bytes 393224 | tf_op jit(solution)/shard_map/ppermute | solution.py:302
  29.4 1.5 %collective-permute-start.6 = (bf16[4,2,1,1,8,1024]{5,4,3,2,1,0:T(8,128)(2,1)S(1)}, bf16[4,2,1,1,8,1024]{5,4,3,2,1,0:T(8,128)(2,1)S(1)}, u32[]{:S(2)}, u32[]{:S(2)}) collective-permute-start(bf16[4,2,1,1,8,1024]{5,4,3,2,1,0:T(8,128)(2,1)S(1)} %get-tuple-element.35), channel_id=1, source_target_pairs={{0,17},{1,16},{2,19},{3,18},{4,21},{5,20},{6,23},{7,22},{8,25},{9,... | collective-permute-start | bytes 393224 | tf_op jit(solution)/shard_map/ppermute | solution.py:302
  30.8 0.3 collective-permute-start.5
  31.1 1.9 %load.1.project_ref = bf16[1024,1536]{1,0:T(8,128)(2,1)S(1)} custom-call(bf16[1024,1536]{1,0:T(8,128)(2,1)} %project_ref.3, bf16[4,1,4,1,8,1024]{5,4,3,2,1,0:T(8,128)(2,1)S(1)} %collective-permute-done.3.awaited_ref), custom_call_target="tpu_custom_call" | custom-call | bytes 6291456 | tf_op jit(solution)/shard_map/load/pallas_call | solution.py:271
  33.0 16.6 %collective-permute-done.4 = bf16[4,2,1,1,8,1024]{5,4,3,2,1,0:T(8,128)(2,1)S(1)} collective-permute-done((bf16[4,2,1,1,8,1024]{5,4,3,2,1,0:T(8,128)(2,1)S(1)}, bf16[4,2,1,1,8,1024]{5,4,3,2,1,0:T(8,128)(2,1)S(1)}, u32[]{:S(2)}, u32[]{:S(2)}) %collective-permute-start.4) | collective-permute-done | bytes 131104 | tf_op jit(solution)/shard_map/ppermute | solution.py:302
  49.6 0.2 collective-permute-done.5
  49.8 1.8 %time.2 = (bf16[8,1,8,512]{3,2,1,0:T(8,128)(2,1)S(1)}, bf16[8,1,8,512]{3,2,1,0:T(8,128)(2,1)S(1)}, bf16[8,1,8,512]{3,2,1,0:T(8,128)(2,1)S(1)}, bf16[8,1,8,512]{3,2,1,0:T(8,128)(2,1)S(1)}) custom-call(bf16[32,1,8,1024]{3,2,1,0:T(8,128)(2,1)S(1)} %bitcast.17, bf16[1024,1536]{1,0:T(8,128)(2,1)S(1)} %load.1.project_ref), custom_call_target="tpu_custom_call" | custom-call | flops 1342177280 | bytes 4194304 | tf_op jit(solution)/shard_map/time/pallas_call | solution.py:388
  51.6 0.1 collective-permute-start.8
  51.7 1.5 %collective-permute-start.7 = (bf16[1,4,2,1,8,512]{5,4,3,2,1,0:T(8,128)(2,1)S(1)}, bf16[1,4,2,1,8,512]{5,4,3,2,1,0:T(8,128)(2,1)S(1)}, u32[]{:S(2)}, u32[]{:S(2)}) collective-permute-start(bf16[1,4,2,1,8,512]{5,4,3,2,1,0:T(8,128)(2,1)S(1)} %bitcast.24), channel_id=1, source_target_pairs={{0,16},{1,17},{2,18},{3,19},{4,20},{5,21},{6,22},{7,23},{8,24},{9,... | collective-permute-start | bytes 196616 | tf_op jit(solution)/shard_map/ppermute | solution.py:302
  53.3 1.9 %collective-permute-start.9 = (bf16[1,4,2,1,8,512]{5,4,3,2,1,0:T(8,128)(2,1)S(1)}, bf16[1,4,2,1,8,512]{5,4,3,2,1,0:T(8,128)(2,1)S(1)}, u32[]{:S(2)}, u32[]{:S(2)}) collective-permute-start(bf16[1,4,2,1,8,512]{5,4,3,2,1,0:T(8,128)(2,1)S(1)} %bitcast.23), channel_id=1, source_target_pairs={{0,17},{1,16},{2,19},{3,18},{4,21},{5,20},{6,23},{7,22},{8,25},{9,... | collective-permute-start | bytes 196616 | tf_op jit(solution)/shard_map/ppermute | solution.py:302
  55.2 1.4 %collective-permute-done.8 = bf16[1,4,2,1,8,512]{5,4,3,2,1,0:T(8,128)(2,1)S(1)} collective-permute-done((bf16[1,4,2,1,8,512]{5,4,3,2,1,0:T(8,128)(2,1)S(1)}, bf16[1,4,2,1,8,512]{5,4,3,2,1,0:T(8,128)(2,1)S(1)}, u32[]{:S(2)}, u32[]{:S(2)}) %collective-permute-start.8) | collective-permute-done | bytes 65568 | tf_op jit(solution)/shard_map/ppermute | solution.py:302
  56.6 1.8 %collective-permute-done.9 = bf16[1,4,2,1,8,512]{5,4,3,2,1,0:T(8,128)(2,1)S(1)} collective-permute-done((bf16[1,4,2,1,8,512]{5,4,3,2,1,0:T(8,128)(2,1)S(1)}, bf16[1,4,2,1,8,512]{5,4,3,2,1,0:T(8,128)(2,1)S(1)}, u32[]{:S(2)}, u32[]{:S(2)}) %collective-permute-start.9) | collective-permute-done | bytes 65568 | tf_op jit(solution)/shard_map/ppermute | solution.py:302
  58.5 2.1 %collective-permute-start.12 = (bf16[4,1,2,1,8,512]{5,4,3,2,1,0:T(8,128)(2,1)S(1)}, bf16[4,1,2,1,8,512]{5,4,3,2,1,0:T(8,128)(2,1)S(1)}, u32[]{:S(2)}, u32[]{:S(2)}) collective-permute-start(bf16[4,1,2,1,8,512]{5,4,3,2,1,0:T(8,128)(2,1)S(1)} %get-tuple-element.42), channel_id=1, source_target_pairs={{0,6},{1,7},{2,4},{3,5},{4,2},{5,3},{6,0},{7,1},{8,14},{9,15},{10,... | collective-permute-start | bytes 196616 | tf_op jit(solution)/shard_map/ppermute | solution.py:302
  60.6 1.2 %collective-permute-start.11 = (bf16[4,1,2,1,8,512]{5,4,3,2,1,0:T(8,128)(2,1)S(1)}, bf16[4,1,2,1,8,512]{5,4,3,2,1,0:T(8,128)(2,1)S(1)}, u32[]{:S(2)}, u32[]{:S(2)}) collective-permute-start(bf16[4,1,2,1,8,512]{5,4,3,2,1,0:T(8,128)(2,1)S(1)} %get-tuple-element.43), channel_id=1, source_target_pairs={{0,4},{1,5},{2,6},{3,7},{4,0},{5,1},{6,2},{7,3},{8,12},{9,13},{10,... | collective-permute-start | bytes 196616 | tf_op jit(solution)/shard_map/ppermute | solution.py:302
  61.7 1.2 %collective-permute-start.10 = (bf16[4,1,2,1,8,512]{5,4,3,2,1,0:T(8,128)(2,1)S(1)}, bf16[4,1,2,1,8,512]{5,4,3,2,1,0:T(8,128)(2,1)S(1)}, u32[]{:S(2)}, u32[]{:S(2)}) collective-permute-start(bf16[4,1,2,1,8,512]{5,4,3,2,1,0:T(8,128)(2,1)S(1)} %get-tuple-element.44), channel_id=1, source_target_pairs={{0,2},{1,3},{2,0},{3,1},{4,6},{5,7},{6,4},{7,5},{8,10},{9,11},{10,... | collective-permute-start | bytes 196616 | tf_op jit(solution)/shard_map/ppermute | solution.py:302
  62.9 3.0 %all-to-all-done.rows_ref = bf16[32,3,8,1024]{3,2,1,0:T(8,128)(2,1)S(1)} async-done(((bf16[32,3,8,1024]{3,2,1,0:T(8,128)(2,1)}), bf16[32,3,8,1024]{3,2,1,0:T(8,128)(2,1)S(1)}, u32[]{:S(2)}, u32[]{:S(2)}) %all-to-all-start) | async-done | bytes 1572896 | tf_op jit(solution)/shard_map/all_to_all | solution.py:250
  66.0 7.1 %time.3.refs_0_ = bf16[32,3,8,512]{3,2,1,0:T(8,128)(2,1)} custom-call(bf16[32,3,8,1024]{3,2,1,0:T(8,128)(2,1)S(1)} %all-to-all-done.rows_ref, bf16[1024,1536]{1,0:T(8,128)(2,1)} %project_ref.3, bf16[8,1,8,512]{3,2,1,0:T(8,128)(2,1)} %copy-done.3), custom_call_target="tpu_custom_call" | custom-call | flops 4026531840 | bytes 6291456 | tf_op jit(solution)/shard_map/time/pallas_call | solution.py:407
  73.1 2.9 %all-to-all-start.1 = ((bf16[32,3,8,512]{3,2,1,0:T(8,128)(2,1)}), bf16[32,3,8,512]{3,2,1,0:T(8,128)(2,1)S(1)}, u32[]{:S(2)}, u32[]{:S(2)}) async-start(bf16[32,3,8,512]{3,2,1,0:T(8,128)(2,1)} %after.3), calls=%async_computation.1 | async-start | bytes 1572864 | tf_op jit(solution)/shard_map/all_to_all | solution.py:250
  76.1 0.3 collective-permute-start.13
  76.4 1.1 %collective-permute-done.13 = bf16[4,4,1,1,8,512]{5,4,3,2,1,0:T(8,128)(2,1)S(1)} collective-permute-done((bf16[4,4,1,1,8,512]{5,4,3,2,1,0:T(8,128)(2,1)S(1)}, bf16[4,4,1,1,8,512]{5,4,3,2,1,0:T(8,128)(2,1)S(1)}, u32[]{:S(2)}, u32[]{:S(2)}) %collective-permute-start.13) | collective-permute-done | bytes 131104 | tf_op jit(solution)/shard_map/ppermute | solution.py:302
  77.6 1.1 %copy-done.2 = bf16[1,256,1024]{2,1,0:T(8,128)(2,1)S(1)} copy-done((bf16[1,256,1024]{2,1,0:T(8,128)(2,1)S(1)}, bf16[1,256,1024]{2,1,0:T(8,128)(2,1)}, u32[]{:S(2)}) %copy-start.2) | copy-done | bytes 524312
  78.7 1.3 %final.2.before_ref = bf16[4,256,1024]{2,1,0:T(8,128)(2,1)} custom-call(bf16[1,256,1024]{2,1,0:T(8,128)(2,1)S(1)} %copy-done.2, bf16[32,1,8,512]{3,2,1,0:T(8,128)(2,1)S(1)} %bitcast.16, bf16[512,1024]{1,0:T(8,128)(2,1)S(1)} %copy-done), custom_call_target="tpu_custom_call" | custom-call | flops 268435456 | bytes 2621440 | tf_op jit(solution)/shard_map/final/pallas_call | solution.py:431
  80.0 18.0 %all-to-all-done.1.context_ref = bf16[32,3,8,512]{3,2,1,0:T(8,128)(2,1)S(1)} async-done(((bf16[32,3,8,512]{3,2,1,0:T(8,128)(2,1)}), bf16[32,3,8,512]{3,2,1,0:T(8,128)(2,1)S(1)}, u32[]{:S(2)}, u32[]{:S(2)}) %all-to-all-start.1) | async-done | bytes 786464 | tf_op jit(solution)/shard_map/all_to_all | solution.py:250
  98.0 1.8 %final.3 = bf16[4,256,1024]{2,1,0:T(8,128)(2,1)} custom-call(bf16[3,256,1024]{2,1,0:T(8,128)(2,1)S(1)} %copy-done.1, bf16[32,3,8,512]{3,2,1,0:T(8,128)(2,1)S(1)} %all-to-all-done.1.context_ref, bf16[512,1024]{1,0:T(8,128)(2,1)S(1)} %copy-done, bf16[4,256,1024]{2,1,0:T(8,128)(2,1)} %final.2.before_ref), custom_call_target="tpu_custom_call", output_to_operand_aliasing={{}: (3, {})} | custom-call | flops 805306368 | bytes 5767168 | tf_op jit(solution)/shard_map/final/pallas_call | solution.py:452
  (26 shorter events, 0.4 us)
Async XLA Ops:
  4.5 14.8 %collective-permute-start = (bf16[1,2,4,1,8,1024]{5,4,3,2,1,0:T(8,128)(2,1)S(1)}, bf16[1,2,4,1,8,1024]{5,4,3,2,1,0:T(8,128)(2,1)S(1)}, u32[]{:S(2)}, u32[]{:S(2)}) collective-permute-start(bf16[1,2,4,1,8,1024]{5,4,3,2,1,0:T(8,128)(2,1)S(1)} %bitcast.22), channel_id=1, source_target_pairs={{0,2},{1,3},{2,0},{3,1},{4,6},{5,7},{6,4},{7,5},{8,10},{9,11},{10,... | collective-permute-start | bytes 393224 | tf_op jit(solution)/shard_map/ppermute | solution.py:302
  7.6 12.9 %collective-permute-start.1 = (bf16[1,2,4,1,8,1024]{5,4,3,2,1,0:T(8,128)(2,1)S(1)}, bf16[1,2,4,1,8,1024]{5,4,3,2,1,0:T(8,128)(2,1)S(1)}, u32[]{:S(2)}, u32[]{:S(2)}) collective-permute-start(bf16[1,2,4,1,8,1024]{5,4,3,2,1,0:T(8,128)(2,1)S(1)} %bitcast.21), channel_id=1, source_target_pairs={{0,4},{1,5},{2,6},{3,7},{4,0},{5,1},{6,2},{7,3},{8,12},{9,13},{10,... | collective-permute-start | bytes 393224 | tf_op jit(solution)/shard_map/ppermute | solution.py:302
  10.2 10.3 %collective-permute-start.2 = (bf16[1,2,4,1,8,1024]{5,4,3,2,1,0:T(8,128)(2,1)S(1)}, bf16[1,2,4,1,8,1024]{5,4,3,2,1,0:T(8,128)(2,1)S(1)}, u32[]{:S(2)}, u32[]{:S(2)}) collective-permute-start(bf16[1,2,4,1,8,1024]{5,4,3,2,1,0:T(8,128)(2,1)S(1)} %bitcast.20), channel_id=1, source_target_pairs={{0,6},{1,7},{2,4},{3,5},{4,2},{5,3},{6,0},{7,1},{8,14},{9,15},{10,... | collective-permute-start | bytes 393224 | tf_op jit(solution)/shard_map/ppermute | solution.py:302
  20.5 45.5 %all-to-all-start = ((bf16[32,3,8,1024]{3,2,1,0:T(8,128)(2,1)}), bf16[32,3,8,1024]{3,2,1,0:T(8,128)(2,1)S(1)}, u32[]{:S(2)}, u32[]{:S(2)}) async-start(bf16[32,3,8,1024]{3,2,1,0:T(8,128)(2,1)} %after.2), calls=%async_computation | async-start | bytes 3145728 | tf_op jit(solution)/shard_map/all_to_all | solution.py:250
  25.9 1.6 %collective-permute-start.3 = (bf16[4,1,4,1,8,1024]{5,4,3,2,1,0:T(8,128)(2,1)S(1)}, bf16[4,1,4,1,8,1024]{5,4,3,2,1,0:T(8,128)(2,1)S(1)}, u32[]{:S(2)}, u32[]{:S(2)}) collective-permute-start(bf16[4,1,4,1,8,1024]{5,4,3,2,1,0:T(8,128)(2,1)S(1)} %get-tuple-element.38), channel_id=1, source_target_pairs={{0,8},{1,9},{2,10},{3,11},{4,12},{5,13},{6,14},{7,15},{8,0},{9,1},... | collective-permute-start | bytes 786440 | tf_op jit(solution)/shard_map/ppermute | solution.py:302
  27.5 22.1 %collective-permute-start.4 = (bf16[4,2,1,1,8,1024]{5,4,3,2,1,0:T(8,128)(2,1)S(1)}, bf16[4,2,1,1,8,1024]{5,4,3,2,1,0:T(8,128)(2,1)S(1)}, u32[]{:S(2)}, u32[]{:S(2)}) collective-permute-start(bf16[4,2,1,1,8,1024]{5,4,3,2,1,0:T(8,128)(2,1)S(1)} %get-tuple-element.34), channel_id=1, source_target_pairs={{0,16},{1,17},{2,18},{3,19},{4,20},{5,21},{6,22},{7,23},{8,24},{9,... | collective-permute-start | bytes 393224 | tf_op jit(solution)/shard_map/ppermute | solution.py:302
  29.4 20.2 %collective-permute-start.6 = (bf16[4,2,1,1,8,1024]{5,4,3,2,1,0:T(8,128)(2,1)S(1)}, bf16[4,2,1,1,8,1024]{5,4,3,2,1,0:T(8,128)(2,1)S(1)}, u32[]{:S(2)}, u32[]{:S(2)}) collective-permute-start(bf16[4,2,1,1,8,1024]{5,4,3,2,1,0:T(8,128)(2,1)S(1)} %get-tuple-element.35), channel_id=1, source_target_pairs={{0,17},{1,16},{2,19},{3,18},{4,21},{5,20},{6,23},{7,22},{8,25},{9,... | collective-permute-start | bytes 393224 | tf_op jit(solution)/shard_map/ppermute | solution.py:302
  30.8 18.9 %collective-permute-start.5 = (bf16[4,2,1,1,8,1024]{5,4,3,2,1,0:T(8,128)(2,1)S(1)}, bf16[4,2,1,1,8,1024]{5,4,3,2,1,0:T(8,128)(2,1)S(1)}, u32[]{:S(2)}, u32[]{:S(2)}) collective-permute-start(bf16[4,2,1,1,8,1024]{5,4,3,2,1,0:T(8,128)(2,1)S(1)} %get-tuple-element.36), channel_id=1, source_target_pairs={{0,1},{1,0},{2,3},{3,2},{4,5},{5,4},{6,7},{7,6},{8,9},{9,8},{10,11... | collective-permute-start | bytes 393224 | tf_op jit(solution)/shard_map/ppermute | solution.py:302
  51.6 14.4 %copy-start.3 = (bf16[8,1,8,512]{3,2,1,0:T(8,128)(2,1)}, bf16[8,1,8,512]{3,2,1,0:T(8,128)(2,1)S(1)}, u32[]{:S(2)}) copy-start(bf16[8,1,8,512]{3,2,1,0:T(8,128)(2,1)S(1)} %get-tuple-element.28.before_ref) | copy-start | bytes 196612
  51.6 5.0 %collective-permute-start.8 = (bf16[1,4,2,1,8,512]{5,4,3,2,1,0:T(8,128)(2,1)S(1)}, bf16[1,4,2,1,8,512]{5,4,3,2,1,0:T(8,128)(2,1)S(1)}, u32[]{:S(2)}, u32[]{:S(2)}) collective-permute-start(bf16[1,4,2,1,8,512]{5,4,3,2,1,0:T(8,128)(2,1)S(1)} %bitcast.25), channel_id=1, source_target_pairs={{0,1},{1,0},{2,3},{3,2},{4,5},{5,4},{6,7},{7,6},{8,9},{9,8},{10,11... | collective-permute-start | bytes 196616 | tf_op jit(solution)/shard_map/ppermute | solution.py:302
  51.7 4.9 %collective-permute-start.7 = (bf16[1,4,2,1,8,512]{5,4,3,2,1,0:T(8,128)(2,1)S(1)}, bf16[1,4,2,1,8,512]{5,4,3,2,1,0:T(8,128)(2,1)S(1)}, u32[]{:S(2)}, u32[]{:S(2)}) collective-permute-start(bf16[1,4,2,1,8,512]{5,4,3,2,1,0:T(8,128)(2,1)S(1)} %bitcast.24), channel_id=1, source_target_pairs={{0,16},{1,17},{2,18},{3,19},{4,20},{5,21},{6,22},{7,23},{8,24},{9,... | collective-permute-start | bytes 196616 | tf_op jit(solution)/shard_map/ppermute | solution.py:302
  53.3 5.2 %collective-permute-start.9 = (bf16[1,4,2,1,8,512]{5,4,3,2,1,0:T(8,128)(2,1)S(1)}, bf16[1,4,2,1,8,512]{5,4,3,2,1,0:T(8,128)(2,1)S(1)}, u32[]{:S(2)}, u32[]{:S(2)}) collective-permute-start(bf16[1,4,2,1,8,512]{5,4,3,2,1,0:T(8,128)(2,1)S(1)} %bitcast.23), channel_id=1, source_target_pairs={{0,17},{1,16},{2,19},{3,18},{4,21},{5,20},{6,23},{7,22},{8,25},{9,... | collective-permute-start | bytes 196616 | tf_op jit(solution)/shard_map/ppermute | solution.py:302
  58.5 14.6 %collective-permute-start.12 = (bf16[4,1,2,1,8,512]{5,4,3,2,1,0:T(8,128)(2,1)S(1)}, bf16[4,1,2,1,8,512]{5,4,3,2,1,0:T(8,128)(2,1)S(1)}, u32[]{:S(2)}, u32[]{:S(2)}) collective-permute-start(bf16[4,1,2,1,8,512]{5,4,3,2,1,0:T(8,128)(2,1)S(1)} %get-tuple-element.42), channel_id=1, source_target_pairs={{0,6},{1,7},{2,4},{3,5},{4,2},{5,3},{6,0},{7,1},{8,14},{9,15},{10,... | collective-permute-start | bytes 196616 | tf_op jit(solution)/shard_map/ppermute | solution.py:302
  60.6 12.5 %collective-permute-start.11 = (bf16[4,1,2,1,8,512]{5,4,3,2,1,0:T(8,128)(2,1)S(1)}, bf16[4,1,2,1,8,512]{5,4,3,2,1,0:T(8,128)(2,1)S(1)}, u32[]{:S(2)}, u32[]{:S(2)}) collective-permute-start(bf16[4,1,2,1,8,512]{5,4,3,2,1,0:T(8,128)(2,1)S(1)} %get-tuple-element.43), channel_id=1, source_target_pairs={{0,4},{1,5},{2,6},{3,7},{4,0},{5,1},{6,2},{7,3},{8,12},{9,13},{10,... | collective-permute-start | bytes 196616 | tf_op jit(solution)/shard_map/ppermute | solution.py:302
  61.7 11.4 %collective-permute-start.10 = (bf16[4,1,2,1,8,512]{5,4,3,2,1,0:T(8,128)(2,1)S(1)}, bf16[4,1,2,1,8,512]{5,4,3,2,1,0:T(8,128)(2,1)S(1)}, u32[]{:S(2)}, u32[]{:S(2)}) collective-permute-start(bf16[4,1,2,1,8,512]{5,4,3,2,1,0:T(8,128)(2,1)S(1)} %get-tuple-element.44), channel_id=1, source_target_pairs={{0,2},{1,3},{2,0},{3,1},{4,6},{5,7},{6,4},{7,5},{8,10},{9,11},{10,... | collective-permute-start | bytes 196616 | tf_op jit(solution)/shard_map/ppermute | solution.py:302
  73.1 4.5 %copy-start = (bf16[512,1024]{1,0:T(8,128)(2,1)S(1)}, bf16[512,1024]{1,0:T(8,128)(2,1)}, u32[]{:S(2)}) copy-start(bf16[512,1024]{1,0:T(8,128)(2,1)} %output_ref.5) | copy-start | bytes 3145732
  73.1 24.9 %all-to-all-start.1 = ((bf16[32,3,8,512]{3,2,1,0:T(8,128)(2,1)}), bf16[32,3,8,512]{3,2,1,0:T(8,128)(2,1)S(1)}, u32[]{:S(2)}, u32[]{:S(2)}) async-start(bf16[32,3,8,512]{3,2,1,0:T(8,128)(2,1)} %after.3), calls=%async_computation.1 | async-start | bytes 1572864 | tf_op jit(solution)/shard_map/all_to_all | solution.py:250
  76.1 1.4 %collective-permute-start.13 = (bf16[4,4,1,1,8,512]{5,4,3,2,1,0:T(8,128)(2,1)S(1)}, bf16[4,4,1,1,8,512]{5,4,3,2,1,0:T(8,128)(2,1)S(1)}, u32[]{:S(2)}, u32[]{:S(2)}) collective-permute-start(bf16[4,4,1,1,8,512]{5,4,3,2,1,0:T(8,128)(2,1)S(1)} %get-tuple-element.40), channel_id=1, source_target_pairs={{0,8},{1,9},{2,10},{3,11},{4,12},{5,13},{6,14},{7,15},{8,0},{9,1},... | collective-permute-start | bytes 393224 | tf_op jit(solution)/shard_map/ppermute | solution.py:302
  77.5 20.5 %copy-start.1 = (bf16[3,256,1024]{2,1,0:T(8,128)(2,1)S(1)}, bf16[3,256,1024]{2,1,0:T(8,128)(2,1)}, u32[]{:S(2)}) copy-start(bf16[3,256,1024]{2,1,0:T(8,128)(2,1)} %get-tuple-element.22.mixed_ref) | copy-start | bytes 4718596
  77.6 1.2 %copy-start.2 = (bf16[1,256,1024]{2,1,0:T(8,128)(2,1)S(1)}, bf16[1,256,1024]{2,1,0:T(8,128)(2,1)}, u32[]{:S(2)}) copy-start(bf16[1,256,1024]{2,1,0:T(8,128)(2,1)} %get-tuple-element.32.mixed_ref) | copy-start | bytes 1572868

commit v7 on v6

--- a/solution.py
+++ b/solution.py
@@ -333,8 +333,8 @@
         in_specs=[
             pl.BlockSpec((1, rows, width), lambda c: (first + c, 0, 0)),
             whole((1, width)),
-            whole((width, 3 * WIDTH)),
-            whole((WIDTH, width)),
+            vmem,
+            vmem,
             whole((1, width)),
         ]
         + [vmem] * len(before),

time: 100 us -> 100 us (level)
  no operation moved by 1% of the time
where the time goes in v7:
time: 100 us; the launch traced here: 99.8 us
  waiting for transfers between devices  44.6 us (45%)
  Pallas kernels  27.5 us (28%)
  starting transfers between devices  26 us (26%)
  local copies, waits for them, and re-layouts  1.25 us (1%)
    ppermute x14, waiting for transfers between devices, swap(): lax.ppermute(block, AXES, [(device, device ^ mask_of(index, group)) for d...  23.6 us
    all_to_all x2, waiting for transfers between devices, exchange(): lax.all_to_all(sent, AXES, split_axis=0, concat_axis=0, tiled=True)  21 us
    ppermute x14, starting transfers between devices, swap(): lax.ppermute(block, AXES, [(device, device ^ mask_of(index, group)) for d...  17.9 us
    pallas_call x1, Pallas kernels, space_call(): pl.pallas_call(partial(space_kernel, groups, len(before)), grid=(clips,),...  9.15 us
    all_to_all x2, starting transfers between devices, exchange(): lax.all_to_all(sent, AXES, split_axis=0, concat_axis=0, tiled=True)  8.1 us
    pallas_call x1, Pallas kernels, time_wide_call(): pl.pallas_call(partial(time_wide_kernel, patch_here), in_specs=[pl.BlockS...  7.1 us
    pallas_call x1, Pallas kernels, space_first_call(): pl.pallas_call(partial(space_first_kernel, groups), in_specs=[ANYWHERE] *...  4.5 us
  transfers between devices with their start and end apart: 16, of which 9 were waited for; matrix products, arithmetic and copies ran while one was open for 0% of the time, Pallas kernels for 21%

profile of v7, /device:TPU:0, one launch (start us, length us, event | category | flops | bytes accessed | tf_op | source)
XLA Modules:
  0.0 99.8 jit_solution(13732927472375757249)
XLA Ops:
  0.0 4.5 %space.2 = (bf16[1,256,1024]{2,1,0:T(8,128)(2,1)S(1)}, bf16[1024,1536]{1,0:T(8,128)(2,1)S(1)}, bf16[512,1024]{1,0:T(8,128)(2,1)S(1)}, bf16[8,1,8,1024]{3,2,1,0:T...) custom-call(bf16[4,256,1024]{2,1,0:T(8,128)(2,1)} %bitcast.26, ...), custom_call_target="tpu_custom_call" | custom-call | flops 1610612736 | bytes 5767168 | tf_op jit(solution)/shard_map/space/pallas_call | solution.py:361
  4.5 3.1 %collective-permute-start = (bf16[1,2,4,1,8,1024]{5,4,3,2,1,0:T(8,128)(2,1)S(1)}, bf16[1,2,4,1,8,1024]{5,4,3,2,1,0:T(8,128)(2,1)S(1)}, u32[]{:S(2)}, u32[]{:S(2)}) collective-permute-start(bf16[1,2,4,1,8,1024]{5,4,3,2,1,0:T(8,128)(2,1)S(1)} %bitcast.22), channel_id=1, source_target_pairs={{0,2},{1,3},{2,0},{3,1},{4,6},{5,7},{6,4},{7,5},{8,10},{9,11},{10,... | collective-permute-start | bytes 393224 | tf_op jit(solution)/shard_map/ppermute | solution.py:302
  7.6 2.6 %collective-permute-start.1 = (bf16[1,2,4,1,8,1024]{5,4,3,2,1,0:T(8,128)(2,1)S(1)}, bf16[1,2,4,1,8,1024]{5,4,3,2,1,0:T(8,128)(2,1)S(1)}, u32[]{:S(2)}, u32[]{:S(2)}) collective-permute-start(bf16[1,2,4,1,8,1024]{5,4,3,2,1,0:T(8,128)(2,1)S(1)} %bitcast.21), channel_id=1, source_target_pairs={{0,4},{1,5},{2,6},{3,7},{4,0},{5,1},{6,2},{7,3},{8,12},{9,13},{10,... | collective-permute-start | bytes 393224 | tf_op jit(solution)/shard_map/ppermute | solution.py:302
  10.2 9.2 %space.3 = (bf16[1,256,1024]{2,1,0:T(8,128)(2,1)}, bf16[3,256,1024]{2,1,0:T(8,128)(2,1)}, bf16[32,3,8,1024]{3,2,1,0:T(8,128)(2,1)}) custom-call(bf16[4,256,1024]{2,1,0:T(8,128)(2,1)} %bitcast.27, f32[1,1024]{1,0:T(1,128)} %bitcast.29, bf16[1024,1536]{1,0:T(8,128)(2,1)S(1)} %get-tuple-element.19.project_ref, ...), custom_call_target="tpu_custom_call" | custom-call | flops 4831838208 | bytes 8912896 | tf_op jit(solution)/shard_map/space/pallas_call | solution.py:330
  19.3 1.2 %collective-permute-done.1.refs_2_ = bf16[1,2,4,1,8,1024]{5,4,3,2,1,0:T(8,128)(2,1)S(1)} collective-permute-done((bf16[1,2,4,1,8,1024]{5,4,3,2,1,0:T(8,128)(2,1)S(1)}, bf16[1,2,4,1,8,1024]{5,4,3,2,1,0:T(8,128)(2,1)S(1)}, u32[]{:S(2)}, u32[]{:S(2)}) %collective-permute-start.1) | collective-permute-done | bytes 131104 | tf_op jit(solution)/shard_map/ppermute | solution.py:302
  20.5 5.2 %all-to-all-start = ((bf16[32,3,8,1024]{3,2,1,0:T(8,128)(2,1)}), bf16[32,3,8,1024]{3,2,1,0:T(8,128)(2,1)S(1)}, u32[]{:S(2)}, u32[]{:S(2)}) async-start(bf16[32,3,8,1024]{3,2,1,0:T(8,128)(2,1)} %after.2), calls=%async_computation | async-start | bytes 3145728 | tf_op jit(solution)/shard_map/all_to_all | solution.py:250
  25.9 0.3 collective-permute-start.3
  26.2 1.3 %collective-permute-done.3.awaited_ref = bf16[4,1,4,1,8,1024]{5,4,3,2,1,0:T(8,128)(2,1)S(1)} collective-permute-done((bf16[4,1,4,1,8,1024]{5,4,3,2,1,0:T(8,128)(2,1)S(1)}, bf16[4,1,4,1,8,1024]{5,4,3,2,1,0:T(8,128)(2,1)S(1)}, u32[]{:S(2)}, u32[]{:S(2)}) %collective-permute-start.3) | collective-permute-done | bytes 262176 | tf_op jit(solution)/shard_map/ppermute | solution.py:302
  27.5 1.8 %collective-permute-start.4 = (bf16[4,2,1,1,8,1024]{5,4,3,2,1,0:T(8,128)(2,1)S(1)}, bf16[4,2,1,1,8,1024]{5,4,3,2,1,0:T(8,128)(2,1)S(1)}, u32[]{:S(2)}, u32[]{:S(2)}) collective-permute-start(bf16[4,2,1,1,8,1024]{5,4,3,2,1,0:T(8,128)(2,1)S(1)} %get-tuple-element.34), channel_id=1, source_target_pairs={{0,16},{1,17},{2,18},{3,19},{4,20},{5,21},{6,22},{7,23},{8,24},{9,... | collective-permute-start | bytes 393224 | tf_op jit(solution)/shard_map/ppermute | solution.py:302
  29.4 1.5 %collective-permute-start.6 = (bf16[4,2,1,1,8,1024]{5,4,3,2,1,0:T(8,128)(2,1)S(1)}, bf16[4,2,1,1,8,1024]{5,4,3,2,1,0:T(8,128)(2,1)S(1)}, u32[]{:S(2)}, u32[]{:S(2)}) collective-permute-start(bf16[4,2,1,1,8,1024]{5,4,3,2,1,0:T(8,128)(2,1)S(1)} %get-tuple-element.35), channel_id=1, source_target_pairs={{0,17},{1,16},{2,19},{3,18},{4,21},{5,20},{6,23},{7,22},{8,25},{9,... | collective-permute-start | bytes 393224 | tf_op jit(solution)/shard_map/ppermute | solution.py:302
  30.8 0.3 collective-permute-start.5
  31.1 1.9 %load.1.project_ref = bf16[1024,1536]{1,0:T(8,128)(2,1)S(1)} custom-call(bf16[1024,1536]{1,0:T(8,128)(2,1)} %project_ref.3, bf16[4,1,4,1,8,1024]{5,4,3,2,1,0:T(8,128)(2,1)S(1)} %collective-permute-done.3.awaited_ref), custom_call_target="tpu_custom_call" | custom-call | bytes 6291456 | tf_op jit(solution)/shard_map/load/pallas_call | solution.py:271
  33.0 16.6 %collective-permute-done.4 = bf16[4,2,1,1,8,1024]{5,4,3,2,1,0:T(8,128)(2,1)S(1)} collective-permute-done((bf16[4,2,1,1,8,1024]{5,4,3,2,1,0:T(8,128)(2,1)S(1)}, bf16[4,2,1,1,8,1024]{5,4,3,2,1,0:T(8,128)(2,1)S(1)}, u32[]{:S(2)}, u32[]{:S(2)}) %collective-permute-start.4) | collective-permute-done | bytes 131104 | tf_op jit(solution)/shard_map/ppermute | solution.py:302
  49.6 0.2 collective-permute-done.5
  49.8 1.8 %time.2 = (bf16[8,1,8,512]{3,2,1,0:T(8,128)(2,1)S(1)}, bf16[8,1,8,512]{3,2,1,0:T(8,128)(2,1)S(1)}, bf16[8,1,8,512]{3,2,1,0:T(8,128)(2,1)S(1)}, bf16[8,1,8,512]{3,2,1,0:T(8,128)(2,1)S(1)}) custom-call(bf16[32,1,8,1024]{3,2,1,0:T(8,128)(2,1)S(1)} %bitcast.17, bf16[1024,1536]{1,0:T(8,128)(2,1)S(1)} %load.1.project_ref), custom_call_target="tpu_custom_call" | custom-call | flops 1342177280 | bytes 4194304 | tf_op jit(solution)/shard_map/time/pallas_call | solution.py:388
  51.6 0.1 collective-permute-start.8
  51.7 1.5 %collective-permute-start.7 = (bf16[1,4,2,1,8,512]{5,4,3,2,1,0:T(8,128)(2,1)S(1)}, bf16[1,4,2,1,8,512]{5,4,3,2,1,0:T(8,128)(2,1)S(1)}, u32[]{:S(2)}, u32[]{:S(2)}) collective-permute-start(bf16[1,4,2,1,8,512]{5,4,3,2,1,0:T(8,128)(2,1)S(1)} %bitcast.24), channel_id=1, source_target_pairs={{0,16},{1,17},{2,18},{3,19},{4,20},{5,21},{6,22},{7,23},{8,24},{9,... | collective-permute-start | bytes 196616 | tf_op jit(solution)/shard_map/ppermute | solution.py:302
  53.3 1.9 %collective-permute-start.9 = (bf16[1,4,2,1,8,512]{5,4,3,2,1,0:T(8,128)(2,1)S(1)}, bf16[1,4,2,1,8,512]{5,4,3,2,1,0:T(8,128)(2,1)S(1)}, u32[]{:S(2)}, u32[]{:S(2)}) collective-permute-start(bf16[1,4,2,1,8,512]{5,4,3,2,1,0:T(8,128)(2,1)S(1)} %bitcast.23), channel_id=1, source_target_pairs={{0,17},{1,16},{2,19},{3,18},{4,21},{5,20},{6,23},{7,22},{8,25},{9,... | collective-permute-start | bytes 196616 | tf_op jit(solution)/shard_map/ppermute | solution.py:302
  55.2 1.4 %collective-permute-done.8 = bf16[1,4,2,1,8,512]{5,4,3,2,1,0:T(8,128)(2,1)S(1)} collective-permute-done((bf16[1,4,2,1,8,512]{5,4,3,2,1,0:T(8,128)(2,1)S(1)}, bf16[1,4,2,1,8,512]{5,4,3,2,1,0:T(8,128)(2,1)S(1)}, u32[]{:S(2)}, u32[]{:S(2)}) %collective-permute-start.8) | collective-permute-done | bytes 65568 | tf_op jit(solution)/shard_map/ppermute | solution.py:302
  56.6 1.8 %collective-permute-done.9 = bf16[1,4,2,1,8,512]{5,4,3,2,1,0:T(8,128)(2,1)S(1)} collective-permute-done((bf16[1,4,2,1,8,512]{5,4,3,2,1,0:T(8,128)(2,1)S(1)}, bf16[1,4,2,1,8,512]{5,4,3,2,1,0:T(8,128)(2,1)S(1)}, u32[]{:S(2)}, u32[]{:S(2)}) %collective-permute-start.9) | collective-permute-done | bytes 65568 | tf_op jit(solution)/shard_map/ppermute | solution.py:302
  58.5 2.1 %collective-permute-start.12 = (bf16[4,1,2,1,8,512]{5,4,3,2,1,0:T(8,128)(2,1)S(1)}, bf16[4,1,2,1,8,512]{5,4,3,2,1,0:T(8,128)(2,1)S(1)}, u32[]{:S(2)}, u32[]{:S(2)}) collective-permute-start(bf16[4,1,2,1,8,512]{5,4,3,2,1,0:T(8,128)(2,1)S(1)} %get-tuple-element.42), channel_id=1, source_target_pairs={{0,6},{1,7},{2,4},{3,5},{4,2},{5,3},{6,0},{7,1},{8,14},{9,15},{10,... | collective-permute-start | bytes 196616 | tf_op jit(solution)/shard_map/ppermute | solution.py:302
  60.6 1.2 %collective-permute-start.11 = (bf16[4,1,2,1,8,512]{5,4,3,2,1,0:T(8,128)(2,1)S(1)}, bf16[4,1,2,1,8,512]{5,4,3,2,1,0:T(8,128)(2,1)S(1)}, u32[]{:S(2)}, u32[]{:S(2)}) collective-permute-start(bf16[4,1,2,1,8,512]{5,4,3,2,1,0:T(8,128)(2,1)S(1)} %get-tuple-element.43), channel_id=1, source_target_pairs={{0,4},{1,5},{2,6},{3,7},{4,0},{5,1},{6,2},{7,3},{8,12},{9,13},{10,... | collective-permute-start | bytes 196616 | tf_op jit(solution)/shard_map/ppermute | solution.py:302
  61.7 1.2 %collective-permute-start.10 = (bf16[4,1,2,1,8,512]{5,4,3,2,1,0:T(8,128)(2,1)S(1)}, bf16[4,1,2,1,8,512]{5,4,3,2,1,0:T(8,128)(2,1)S(1)}, u32[]{:S(2)}, u32[]{:S(2)}) collective-permute-start(bf16[4,1,2,1,8,512]{5,4,3,2,1,0:T(8,128)(2,1)S(1)} %get-tuple-element.44), channel_id=1, source_target_pairs={{0,2},{1,3},{2,0},{3,1},{4,6},{5,7},{6,4},{7,5},{8,10},{9,11},{10,... | collective-permute-start | bytes 196616 | tf_op jit(solution)/shard_map/ppermute | solution.py:302
  62.9 3.0 %all-to-all-done.rows_ref = bf16[32,3,8,1024]{3,2,1,0:T(8,128)(2,1)S(1)} async-done(((bf16[32,3,8,1024]{3,2,1,0:T(8,128)(2,1)}), bf16[32,3,8,1024]{3,2,1,0:T(8,128)(2,1)S(1)}, u32[]{:S(2)}, u32[]{:S(2)}) %all-to-all-start) | async-done | bytes 1572896 | tf_op jit(solution)/shard_map/all_to_all | solution.py:250
  66.0 7.1 %time.3.refs_0_ = bf16[32,3,8,512]{3,2,1,0:T(8,128)(2,1)} custom-call(bf16[32,3,8,1024]{3,2,1,0:T(8,128)(2,1)S(1)} %all-to-all-done.rows_ref, bf16[1024,1536]{1,0:T(8,128)(2,1)} %project_ref.3, bf16[8,1,8,512]{3,2,1,0:T(8,128)(2,1)} %copy-done.3), custom_call_target="tpu_custom_call" | custom-call | flops 4026531840 | bytes 6291456 | tf_op jit(solution)/shard_map/time/pallas_call | solution.py:407
  73.1 2.9 %all-to-all-start.1 = ((bf16[32,3,8,512]{3,2,1,0:T(8,128)(2,1)}), bf16[32,3,8,512]{3,2,1,0:T(8,128)(2,1)S(1)}, u32[]{:S(2)}, u32[]{:S(2)}) async-start(bf16[32,3,8,512]{3,2,1,0:T(8,128)(2,1)} %after.3), calls=%async_computation.1 | async-start | bytes 1572864 | tf_op jit(solution)/shard_map/all_to_all | solution.py:250
  76.1 0.3 collective-permute-start.13
  76.4 1.1 %collective-permute-done.13 = bf16[4,4,1,1,8,512]{5,4,3,2,1,0:T(8,128)(2,1)S(1)} collective-permute-done((bf16[4,4,1,1,8,512]{5,4,3,2,1,0:T(8,128)(2,1)S(1)}, bf16[4,4,1,1,8,512]{5,4,3,2,1,0:T(8,128)(2,1)S(1)}, u32[]{:S(2)}, u32[]{:S(2)}) %collective-permute-start.13) | collective-permute-done | bytes 131104 | tf_op jit(solution)/shard_map/ppermute | solution.py:302
  77.6 1.1 %copy-done.2 = bf16[1,256,1024]{2,1,0:T(8,128)(2,1)S(1)} copy-done((bf16[1,256,1024]{2,1,0:T(8,128)(2,1)S(1)}, bf16[1,256,1024]{2,1,0:T(8,128)(2,1)}, u32[]{:S(2)}) %copy-start.2) | copy-done | bytes 524312
  78.7 1.3 %final.2.before_ref = bf16[4,256,1024]{2,1,0:T(8,128)(2,1)} custom-call(bf16[1,256,1024]{2,1,0:T(8,128)(2,1)S(1)} %copy-done.2, bf16[32,1,8,512]{3,2,1,0:T(8,128)(2,1)S(1)} %bitcast.16, bf16[512,1024]{1,0:T(8,128)(2,1)S(1)} %copy-done), custom_call_target="tpu_custom_call" | custom-call | flops 268435456 | bytes 2621440 | tf_op jit(solution)/shard_map/final/pallas_call | solution.py:431
  80.0 18.0 %all-to-all-done.1.context_ref = bf16[32,3,8,512]{3,2,1,0:T(8,128)(2,1)S(1)} async-done(((bf16[32,3,8,512]{3,2,1,0:T(8,128)(2,1)}), bf16[32,3,8,512]{3,2,1,0:T(8,128)(2,1)S(1)}, u32[]{:S(2)}, u32[]{:S(2)}) %all-to-all-start.1) | async-done | bytes 786464 | tf_op jit(solution)/shard_map/all_to_all | solution.py:250
  98.0 1.8 %final.3 = bf16[4,256,1024]{2,1,0:T(8,128)(2,1)} custom-call(bf16[3,256,1024]{2,1,0:T(8,128)(2,1)S(1)} %copy-done.1, bf16[32,3,8,512]{3,2,1,0:T(8,128)(2,1)S(1)} %all-to-all-done.1.context_ref, bf16[512,1024]{1,0:T(8,128)(2,1)S(1)} %copy-done, bf16[4,256,1024]{2,1,0:T(8,128)(2,1)} %final.2.before_ref), custom_call_target="tpu_custom_call", output_to_operand_aliasing={{}: (3, {})} | custom-call | flops 805306368 | bytes 5767168 | tf_op jit(solution)/shard_map/final/pallas_call | solution.py:452
  (26 shorter events, 0.4 us)
Async XLA Ops:
  4.5 14.8 %collective-permute-start = (bf16[1,2,4,1,8,1024]{5,4,3,2,1,0:T(8,128)(2,1)S(1)}, bf16[1,2,4,1,8,1024]{5,4,3,2,1,0:T(8,128)(2,1)S(1)}, u32[]{:S(2)}, u32[]{:S(2)}) collective-permute-start(bf16[1,2,4,1,8,1024]{5,4,3,2,1,0:T(8,128)(2,1)S(1)} %bitcast.22), channel_id=1, source_target_pairs={{0,2},{1,3},{2,0},{3,1},{4,6},{5,7},{6,4},{7,5},{8,10},{9,11},{10,... | collective-permute-start | bytes 393224 | tf_op jit(solution)/shard_map/ppermute | solution.py:302
  7.6 12.9 %collective-permute-start.1 = (bf16[1,2,4,1,8,1024]{5,4,3,2,1,0:T(8,128)(2,1)S(1)}, bf16[1,2,4,1,8,1024]{5,4,3,2,1,0:T(8,128)(2,1)S(1)}, u32[]{:S(2)}, u32[]{:S(2)}) collective-permute-start(bf16[1,2,4,1,8,1024]{5,4,3,2,1,0:T(8,128)(2,1)S(1)} %bitcast.21), channel_id=1, source_target_pairs={{0,4},{1,5},{2,6},{3,7},{4,0},{5,1},{6,2},{7,3},{8,12},{9,13},{10,... | collective-permute-start | bytes 393224 | tf_op jit(solution)/shard_map/ppermute | solution.py:302
  10.2 10.3 %collective-permute-start.2 = (bf16[1,2,4,1,8,1024]{5,4,3,2,1,0:T(8,128)(2,1)S(1)}, bf16[1,2,4,1,8,1024]{5,4,3,2,1,0:T(8,128)(2,1)S(1)}, u32[]{:S(2)}, u32[]{:S(2)}) collective-permute-start(bf16[1,2,4,1,8,1024]{5,4,3,2,1,0:T(8,128)(2,1)S(1)} %bitcast.20), channel_id=1, source_target_pairs={{0,6},{1,7},{2,4},{3,5},{4,2},{5,3},{6,0},{7,1},{8,14},{9,15},{10,... | collective-permute-start | bytes 393224 | tf_op jit(solution)/shard_map/ppermute | solution.py:302
  20.5 45.5 %all-to-all-start = ((bf16[32,3,8,1024]{3,2,1,0:T(8,128)(2,1)}), bf16[32,3,8,1024]{3,2,1,0:T(8,128)(2,1)S(1)}, u32[]{:S(2)}, u32[]{:S(2)}) async-start(bf16[32,3,8,1024]{3,2,1,0:T(8,128)(2,1)} %after.2), calls=%async_computation | async-start | bytes 3145728 | tf_op jit(solution)/shard_map/all_to_all | solution.py:250
  25.9 1.6 %collective-permute-start.3 = (bf16[4,1,4,1,8,1024]{5,4,3,2,1,0:T(8,128)(2,1)S(1)}, bf16[4,1,4,1,8,1024]{5,4,3,2,1,0:T(8,128)(2,1)S(1)}, u32[]{:S(2)}, u32[]{:S(2)}) collective-permute-start(bf16[4,1,4,1,8,1024]{5,4,3,2,1,0:T(8,128)(2,1)S(1)} %get-tuple-element.38), channel_id=1, source_target_pairs={{0,8},{1,9},{2,10},{3,11},{4,12},{5,13},{6,14},{7,15},{8,0},{9,1},... | collective-permute-start | bytes 786440 | tf_op jit(solution)/shard_map/ppermute | solution.py:302
  27.5 22.1 %collective-permute-start.4 = (bf16[4,2,1,1,8,1024]{5,4,3,2,1,0:T(8,128)(2,1)S(1)}, bf16[4,2,1,1,8,1024]{5,4,3,2,1,0:T(8,128)(2,1)S(1)}, u32[]{:S(2)}, u32[]{:S(2)}) collective-permute-start(bf16[4,2,1,1,8,1024]{5,4,3,2,1,0:T(8,128)(2,1)S(1)} %get-tuple-element.34), channel_id=1, source_target_pairs={{0,16},{1,17},{2,18},{3,19},{4,20},{5,21},{6,22},{7,23},{8,24},{9,... | collective-permute-start | bytes 393224 | tf_op jit(solution)/shard_map/ppermute | solution.py:302
  29.4 20.2 %collective-permute-start.6 = (bf16[4,2,1,1,8,1024]{5,4,3,2,1,0:T(8,128)(2,1)S(1)}, bf16[4,2,1,1,8,1024]{5,4,3,2,1,0:T(8,128)(2,1)S(1)}, u32[]{:S(2)}, u32[]{:S(2)}) collective-permute-start(bf16[4,2,1,1,8,1024]{5,4,3,2,1,0:T(8,128)(2,1)S(1)} %get-tuple-element.35), channel_id=1, source_target_pairs={{0,17},{1,16},{2,19},{3,18},{4,21},{5,20},{6,23},{7,22},{8,25},{9,... | collective-permute-start | bytes 393224 | tf_op jit(solution)/shard_map/ppermute | solution.py:302
  30.8 18.9 %collective-permute-start.5 = (bf16[4,2,1,1,8,1024]{5,4,3,2,1,0:T(8,128)(2,1)S(1)}, bf16[4,2,1,1,8,1024]{5,4,3,2,1,0:T(8,128)(2,1)S(1)}, u32[]{:S(2)}, u32[]{:S(2)}) collective-permute-start(bf16[4,2,1,1,8,1024]{5,4,3,2,1,0:T(8,128)(2,1)S(1)} %get-tuple-element.36), channel_id=1, source_target_pairs={{0,1},{1,0},{2,3},{3,2},{4,5},{5,4},{6,7},{7,6},{8,9},{9,8},{10,11... | collective-permute-start | bytes 393224 | tf_op jit(solution)/shard_map/ppermute | solution.py:302
  51.6 14.4 %copy-start.3 = (bf16[8,1,8,512]{3,2,1,0:T(8,128)(2,1)}, bf16[8,1,8,512]{3,2,1,0:T(8,128)(2,1)S(1)}, u32[]{:S(2)}) copy-start(bf16[8,1,8,512]{3,2,1,0:T(8,128)(2,1)S(1)} %get-tuple-element.28.before_ref) | copy-start | bytes 196612
  51.6 5.0 %collective-permute-start.8 = (bf16[1,4,2,1,8,512]{5,4,3,2,1,0:T(8,128)(2,1)S(1)}, bf16[1,4,2,1,8,512]{5,4,3,2,1,0:T(8,128)(2,1)S(1)}, u32[]{:S(2)}, u32[]{:S(2)}) collective-permute-start(bf16[1,4,2,1,8,512]{5,4,3,2,1,0:T(8,128)(2,1)S(1)} %bitcast.25), channel_id=1, source_target_pairs={{0,1},{1,0},{2,3},{3,2},{4,5},{5,4},{6,7},{7,6},{8,9},{9,8},{10,11... | collective-permute-start | bytes 196616 | tf_op jit(solution)/shard_map/ppermute | solution.py:302
  51.7 4.9 %collective-permute-start.7 = (bf16[1,4,2,1,8,512]{5,4,3,2,1,0:T(8,128)(2,1)S(1)}, bf16[1,4,2,1,8,512]{5,4,3,2,1,0:T(8,128)(2,1)S(1)}, u32[]{:S(2)}, u32[]{:S(2)}) collective-permute-start(bf16[1,4,2,1,8,512]{5,4,3,2,1,0:T(8,128)(2,1)S(1)} %bitcast.24), channel_id=1, source_target_pairs={{0,16},{1,17},{2,18},{3,19},{4,20},{5,21},{6,22},{7,23},{8,24},{9,... | collective-permute-start | bytes 196616 | tf_op jit(solution)/shard_map/ppermute | solution.py:302
  53.3 5.2 %collective-permute-start.9 = (bf16[1,4,2,1,8,512]{5,4,3,2,1,0:T(8,128)(2,1)S(1)}, bf16[1,4,2,1,8,512]{5,4,3,2,1,0:T(8,128)(2,1)S(1)}, u32[]{:S(2)}, u32[]{:S(2)}) collective-permute-start(bf16[1,4,2,1,8,512]{5,4,3,2,1,0:T(8,128)(2,1)S(1)} %bitcast.23), channel_id=1, source_target_pairs={{0,17},{1,16},{2,19},{3,18},{4,21},{5,20},{6,23},{7,22},{8,25},{9,... | collective-permute-start | bytes 196616 | tf_op jit(solution)/shard_map/ppermute | solution.py:302
  58.5 14.6 %collective-permute-start.12 = (bf16[4,1,2,1,8,512]{5,4,3,2,1,0:T(8,128)(2,1)S(1)}, bf16[4,1,2,1,8,512]{5,4,3,2,1,0:T(8,128)(2,1)S(1)}, u32[]{:S(2)}, u32[]{:S(2)}) collective-permute-start(bf16[4,1,2,1,8,512]{5,4,3,2,1,0:T(8,128)(2,1)S(1)} %get-tuple-element.42), channel_id=1, source_target_pairs={{0,6},{1,7},{2,4},{3,5},{4,2},{5,3},{6,0},{7,1},{8,14},{9,15},{10,... | collective-permute-start | bytes 196616 | tf_op jit(solution)/shard_map/ppermute | solution.py:302
  60.6 12.5 %collective-permute-start.11 = (bf16[4,1,2,1,8,512]{5,4,3,2,1,0:T(8,128)(2,1)S(1)}, bf16[4,1,2,1,8,512]{5,4,3,2,1,0:T(8,128)(2,1)S(1)}, u32[]{:S(2)}, u32[]{:S(2)}) collective-permute-start(bf16[4,1,2,1,8,512]{5,4,3,2,1,0:T(8,128)(2,1)S(1)} %get-tuple-element.43), channel_id=1, source_target_pairs={{0,4},{1,5},{2,6},{3,7},{4,0},{5,1},{6,2},{7,3},{8,12},{9,13},{10,... | collective-permute-start | bytes 196616 | tf_op jit(solution)/shard_map/ppermute | solution.py:302
  61.7 11.4 %collective-permute-start.10 = (bf16[4,1,2,1,8,512]{5,4,3,2,1,0:T(8,128)(2,1)S(1)}, bf16[4,1,2,1,8,512]{5,4,3,2,1,0:T(8,128)(2,1)S(1)}, u32[]{:S(2)}, u32[]{:S(2)}) collective-permute-start(bf16[4,1,2,1,8,512]{5,4,3,2,1,0:T(8,128)(2,1)S(1)} %get-tuple-element.44), channel_id=1, source_target_pairs={{0,2},{1,3},{2,0},{3,1},{4,6},{5,7},{6,4},{7,5},{8,10},{9,11},{10,... | collective-permute-start | bytes 196616 | tf_op jit(solution)/shard_map/ppermute | solution.py:302
  73.1 4.5 %copy-start = (bf16[512,1024]{1,0:T(8,128)(2,1)S(1)}, bf16[512,1024]{1,0:T(8,128)(2,1)}, u32[]{:S(2)}) copy-start(bf16[512,1024]{1,0:T(8,128)(2,1)} %output_ref.5) | copy-start | bytes 3145732
  73.1 24.9 %all-to-all-start.1 = ((bf16[32,3,8,512]{3,2,1,0:T(8,128)(2,1)}), bf16[32,3,8,512]{3,2,1,0:T(8,128)(2,1)S(1)}, u32[]{:S(2)}, u32[]{:S(2)}) async-start(bf16[32,3,8,512]{3,2,1,0:T(8,128)(2,1)} %after.3), calls=%async_computation.1 | async-start | bytes 1572864 | tf_op jit(solution)/shard_map/all_to_all | solution.py:250
  76.1 1.4 %collective-permute-start.13 = (bf16[4,4,1,1,8,512]{5,4,3,2,1,0:T(8,128)(2,1)S(1)}, bf16[4,4,1,1,8,512]{5,4,3,2,1,0:T(8,128)(2,1)S(1)}, u32[]{:S(2)}, u32[]{:S(2)}) collective-permute-start(bf16[4,4,1,1,8,512]{5,4,3,2,1,0:T(8,128)(2,1)S(1)} %get-tuple-element.40), channel_id=1, source_target_pairs={{0,8},{1,9},{2,10},{3,11},{4,12},{5,13},{6,14},{7,15},{8,0},{9,1},... | collective-permute-start | bytes 393224 | tf_op jit(solution)/shard_map/ppermute | solution.py:302
  77.5 20.5 %copy-start.1 = (bf16[3,256,1024]{2,1,0:T(8,128)(2,1)S(1)}, bf16[3,256,1024]{2,1,0:T(8,128)(2,1)}, u32[]{:S(2)}) copy-start(bf16[3,256,1024]{2,1,0:T(8,128)(2,1)} %get-tuple-element.22.mixed_ref) | copy-start | bytes 4718596
  77.6 1.2 %copy-start.2 = (bf16[1,256,1024]{2,1,0:T(8,128)(2,1)S(1)}, bf16[1,256,1024]{2,1,0:T(8,128)(2,1)}, u32[]{:S(2)}) copy-start(bf16[1,256,1024]{2,1,0:T(8,128)(2,1)} %get-tuple-element.32.mixed_ref) | copy-start | bytes 1572868

commit v8 on v7

--- a/solution.py
+++ b/solution.py
@@ -32,24 +32,31 @@
 def attend(heads, bias):
     rows = heads.shape[0]
     low = lax.broadcasted_iota(jnp.int32, (rows, LANES), 1) < HEAD_DIM
+    nothing = jnp.zeros((rows, LANES), jnp.bfloat16)
     ones = jnp.ones((rows, LANES), jnp.bfloat16)
+
+    def apart(tile):
+        return jnp.concatenate([jnp.where(low, tile, nothing), jnp.where(low, nothing, tile)], axis=0)
+
+    ones = apart(ones)
     contexts, pending = [], []
     for pair in range(WIDTH // LANES):
         at = pair * LANES
         queries = heads[:, at : at + LANES] * jnp.bfloat16(HEAD_DIM**-0.5)
-        keys = heads[:, WIDTH + at : WIDTH + at + LANES]
-        values = heads[:, 2 * WIDTH + at : 2 * WIDTH + at + LANES]
-        nothing = jnp.zeros_like(queries)
-        stacked = jnp.concatenate([jnp.where(low, queries, nothing), jnp.where(low, nothing, queries)], axis=0)
-        scores = lax.dot_general(stacked, keys, (((1,), (1,)), ((), ())), preferred_element_type=jnp.float32)
-        if bias is not None:
-            scores = scores + jnp.concatenate([bias, bias], axis=0)
-        weights = jnp.exp(scores - jnp.max(scores, axis=-1, keepdims=True)).astype(jnp.bfloat16)
+        keys = apart(heads[:, WIDTH + at : WIDTH + at + LANES])
+        values = apart(heads[:, 2 * WIDTH + at : 2 * WIDTH + at + LANES])
+        scores = lax.dot_general(queries, keys, (((1,), (1,)), ((), ())), preferred_element_type=jnp.float32)
+        weights = []
+        for one in (scores[:, :rows], scores[:, rows:]):
+            if bias is not None:
+                one = one + bias
+            weights.append(jnp.exp(one - jnp.max(one, axis=-1, keepdims=True)).astype(jnp.bfloat16))
         pending.append((weights, values))
     for weights, values in pending:
-        sums = jnp.dot(weights, jnp.concatenate([values, ones], axis=1), preferred_element_type=jnp.float32)
-        context = sums[:, :LANES] / sums[:, LANES:]
-        contexts.append(jnp.where(low, context[:rows], context[rows:]))
+        sums = jnp.dot(
+            jnp.concatenate(weights, axis=1), jnp.concatenate([values, ones], axis=1), preferred_element_type=jnp.float32
+        )
+        contexts.append(sums[:, :LANES] / sums[:, LANES:])
     return jnp.concatenate(contexts, axis=1).astype(jnp.bfloat16)
 
 

time: 100 us -> 100 us (level)
  no operation moved by 1% of the time
where the time goes in v8:
time: 100 us; the launch traced here: 99.7 us
  waiting for transfers between devices  44.6 us (45%)
  Pallas kernels  27.5 us (28%)
  starting transfers between devices  26 us (26%)
  local copies, waits for them, and re-layouts  1.25 us (1%)
    ppermute x14, waiting for transfers between devices, swap(): lax.ppermute(block, AXES, [(device, device ^ mask_of(index, group)) for d...  23.6 us
    all_to_all x2, waiting for transfers between devices, exchange(): lax.all_to_all(sent, AXES, split_axis=0, concat_axis=0, tiled=True)  21 us
    ppermute x14, starting transfers between devices, swap(): lax.ppermute(block, AXES, [(device, device ^ mask_of(index, group)) for d...  17.9 us
    pallas_call x1, Pallas kernels, space_call(): pl.pallas_call(partial(space_kernel, groups, len(before)), grid=(clips,),...  9.13 us
    all_to_all x2, starting transfers between devices, exchange(): lax.all_to_all(sent, AXES, split_axis=0, concat_axis=0, tiled=True)  8.1 us
    pallas_call x1, Pallas kernels, time_wide_call(): pl.pallas_call(partial(time_wide_kernel, patch_here), in_specs=[pl.BlockS...  7.07 us
    pallas_call x1, Pallas kernels, space_first_call(): pl.pallas_call(partial(space_first_kernel, groups), in_specs=[ANYWHERE] *...  4.5 us
  transfers between devices with their start and end apart: 16, of which 9 were waited for; matrix products, arithmetic and copies ran while one was open for 0% of the time, Pallas kernels for 21%

profile of v8, /device:TPU:0, one launch (start us, length us, event | category | flops | bytes accessed | tf_op | source)
XLA Modules:
  0.0 99.7 jit_solution(6181413209264475873)
XLA Ops:
  0.0 4.5 %space.2 = (bf16[1,256,1024]{2,1,0:T(8,128)(2,1)S(1)}, bf16[1024,1536]{1,0:T(8,128)(2,1)S(1)}, bf16[512,1024]{1,0:T(8,128)(2,1)S(1)}, bf16[8,1,8,1024]{3,2,1,0:T...) custom-call(bf16[4,256,1024]{2,1,0:T(8,128)(2,1)} %bitcast.26, ...), custom_call_target="tpu_custom_call" | custom-call | flops 1610612736 | bytes 5767168 | tf_op jit(solution)/shard_map/space/pallas_call | solution.py:368
  4.5 3.1 %collective-permute-start = (bf16[1,2,4,1,8,1024]{5,4,3,2,1,0:T(8,128)(2,1)S(1)}, bf16[1,2,4,1,8,1024]{5,4,3,2,1,0:T(8,128)(2,1)S(1)}, u32[]{:S(2)}, u32[]{:S(2)}) collective-permute-start(bf16[1,2,4,1,8,1024]{5,4,3,2,1,0:T(8,128)(2,1)S(1)} %bitcast.22), channel_id=1, source_target_pairs={{0,2},{1,3},{2,0},{3,1},{4,6},{5,7},{6,4},{7,5},{8,10},{9,11},{10,... | collective-permute-start | bytes 393224 | tf_op jit(solution)/shard_map/ppermute | solution.py:309
  7.6 2.6 %collective-permute-start.1 = (bf16[1,2,4,1,8,1024]{5,4,3,2,1,0:T(8,128)(2,1)S(1)}, bf16[1,2,4,1,8,1024]{5,4,3,2,1,0:T(8,128)(2,1)S(1)}, u32[]{:S(2)}, u32[]{:S(2)}) collective-permute-start(bf16[1,2,4,1,8,1024]{5,4,3,2,1,0:T(8,128)(2,1)S(1)} %bitcast.21), channel_id=1, source_target_pairs={{0,4},{1,5},{2,6},{3,7},{4,0},{5,1},{6,2},{7,3},{8,12},{9,13},{10,... | collective-permute-start | bytes 393224 | tf_op jit(solution)/shard_map/ppermute | solution.py:309
  10.2 9.1 %space.3 = (bf16[1,256,1024]{2,1,0:T(8,128)(2,1)}, bf16[3,256,1024]{2,1,0:T(8,128)(2,1)}, bf16[32,3,8,1024]{3,2,1,0:T(8,128)(2,1)}) custom-call(bf16[4,256,1024]{2,1,0:T(8,128)(2,1)} %bitcast.27, f32[1,1024]{1,0:T(1,128)} %bitcast.29, bf16[1024,1536]{1,0:T(8,128)(2,1)S(1)} %get-tuple-element.19.project_ref, ...), custom_call_target="tpu_custom_call" | custom-call | flops 4831838208 | bytes 8912896 | tf_op jit(solution)/shard_map/space/pallas_call | solution.py:337
  19.3 1.2 %collective-permute-done.1.refs_2_ = bf16[1,2,4,1,8,1024]{5,4,3,2,1,0:T(8,128)(2,1)S(1)} collective-permute-done((bf16[1,2,4,1,8,1024]{5,4,3,2,1,0:T(8,128)(2,1)S(1)}, bf16[1,2,4,1,8,1024]{5,4,3,2,1,0:T(8,128)(2,1)S(1)}, u32[]{:S(2)}, u32[]{:S(2)}) %collective-permute-start.1) | collective-permute-done | bytes 131104 | tf_op jit(solution)/shard_map/ppermute | solution.py:309
  20.5 5.2 %all-to-all-start = ((bf16[32,3,8,1024]{3,2,1,0:T(8,128)(2,1)}), bf16[32,3,8,1024]{3,2,1,0:T(8,128)(2,1)S(1)}, u32[]{:S(2)}, u32[]{:S(2)}) async-start(bf16[32,3,8,1024]{3,2,1,0:T(8,128)(2,1)} %after.2), calls=%async_computation | async-start | bytes 3145728 | tf_op jit(solution)/shard_map/all_to_all | solution.py:257
  25.9 0.3 collective-permute-start.3
  26.2 1.3 %collective-permute-done.3.awaited_ref = bf16[4,1,4,1,8,1024]{5,4,3,2,1,0:T(8,128)(2,1)S(1)} collective-permute-done((bf16[4,1,4,1,8,1024]{5,4,3,2,1,0:T(8,128)(2,1)S(1)}, bf16[4,1,4,1,8,1024]{5,4,3,2,1,0:T(8,128)(2,1)S(1)}, u32[]{:S(2)}, u32[]{:S(2)}) %collective-permute-start.3) | collective-permute-done | bytes 262176 | tf_op jit(solution)/shard_map/ppermute | solution.py:309
  27.5 1.8 %collective-permute-start.4 = (bf16[4,2,1,1,8,1024]{5,4,3,2,1,0:T(8,128)(2,1)S(1)}, bf16[4,2,1,1,8,1024]{5,4,3,2,1,0:T(8,128)(2,1)S(1)}, u32[]{:S(2)}, u32[]{:S(2)}) collective-permute-start(bf16[4,2,1,1,8,1024]{5,4,3,2,1,0:T(8,128)(2,1)S(1)} %get-tuple-element.34), channel_id=1, source_target_pairs={{0,16},{1,17},{2,18},{3,19},{4,20},{5,21},{6,22},{7,23},{8,24},{9,... | collective-permute-start | bytes 393224 | tf_op jit(solution)/shard_map/ppermute | solution.py:309
  29.4 1.5 %collective-permute-start.6 = (bf16[4,2,1,1,8,1024]{5,4,3,2,1,0:T(8,128)(2,1)S(1)}, bf16[4,2,1,1,8,1024]{5,4,3,2,1,0:T(8,128)(2,1)S(1)}, u32[]{:S(2)}, u32[]{:S(2)}) collective-permute-start(bf16[4,2,1,1,8,1024]{5,4,3,2,1,0:T(8,128)(2,1)S(1)} %get-tuple-element.35), channel_id=1, source_target_pairs={{0,17},{1,16},{2,19},{3,18},{4,21},{5,20},{6,23},{7,22},{8,25},{9,... | collective-permute-start | bytes 393224 | tf_op jit(solution)/shard_map/ppermute | solution.py:309
  30.8 0.3 collective-permute-start.5
  31.1 1.9 %load.1.project_ref = bf16[1024,1536]{1,0:T(8,128)(2,1)S(1)} custom-call(bf16[1024,1536]{1,0:T(8,128)(2,1)} %project_ref.3, bf16[4,1,4,1,8,1024]{5,4,3,2,1,0:T(8,128)(2,1)S(1)} %collective-permute-done.3.awaited_ref), custom_call_target="tpu_custom_call" | custom-call | bytes 6291456 | tf_op jit(solution)/shard_map/load/pallas_call | solution.py:278
  33.0 16.6 %collective-permute-done.4 = bf16[4,2,1,1,8,1024]{5,4,3,2,1,0:T(8,128)(2,1)S(1)} collective-permute-done((bf16[4,2,1,1,8,1024]{5,4,3,2,1,0:T(8,128)(2,1)S(1)}, bf16[4,2,1,1,8,1024]{5,4,3,2,1,0:T(8,128)(2,1)S(1)}, u32[]{:S(2)}, u32[]{:S(2)}) %collective-permute-start.4) | collective-permute-done | bytes 131104 | tf_op jit(solution)/shard_map/ppermute | solution.py:309
  49.6 0.2 collective-permute-done.5
  49.8 1.8 %time.2 = (bf16[8,1,8,512]{3,2,1,0:T(8,128)(2,1)S(1)}, bf16[8,1,8,512]{3,2,1,0:T(8,128)(2,1)S(1)}, bf16[8,1,8,512]{3,2,1,0:T(8,128)(2,1)S(1)}, bf16[8,1,8,512]{3,2,1,0:T(8,128)(2,1)S(1)}) custom-call(bf16[32,1,8,1024]{3,2,1,0:T(8,128)(2,1)S(1)} %bitcast.17, bf16[1024,1536]{1,0:T(8,128)(2,1)S(1)} %load.1.project_ref), custom_call_target="tpu_custom_call" | custom-call | flops 1342177280 | bytes 4194304 | tf_op jit(solution)/shard_map/time/pallas_call | solution.py:395
  51.7 0.1 collective-permute-start.8
  51.7 1.5 %collective-permute-start.7 = (bf16[1,4,2,1,8,512]{5,4,3,2,1,0:T(8,128)(2,1)S(1)}, bf16[1,4,2,1,8,512]{5,4,3,2,1,0:T(8,128)(2,1)S(1)}, u32[]{:S(2)}, u32[]{:S(2)}) collective-permute-start(bf16[1,4,2,1,8,512]{5,4,3,2,1,0:T(8,128)(2,1)S(1)} %bitcast.24), channel_id=1, source_target_pairs={{0,16},{1,17},{2,18},{3,19},{4,20},{5,21},{6,22},{7,23},{8,24},{9,... | collective-permute-start | bytes 196616 | tf_op jit(solution)/shard_map/ppermute | solution.py:309
  53.3 1.9 %collective-permute-start.9 = (bf16[1,4,2,1,8,512]{5,4,3,2,1,0:T(8,128)(2,1)S(1)}, bf16[1,4,2,1,8,512]{5,4,3,2,1,0:T(8,128)(2,1)S(1)}, u32[]{:S(2)}, u32[]{:S(2)}) collective-permute-start(bf16[1,4,2,1,8,512]{5,4,3,2,1,0:T(8,128)(2,1)S(1)} %bitcast.23), channel_id=1, source_target_pairs={{0,17},{1,16},{2,19},{3,18},{4,21},{5,20},{6,23},{7,22},{8,25},{9,... | collective-permute-start | bytes 196616 | tf_op jit(solution)/shard_map/ppermute | solution.py:309
  55.2 1.4 %collective-permute-done.8 = bf16[1,4,2,1,8,512]{5,4,3,2,1,0:T(8,128)(2,1)S(1)} collective-permute-done((bf16[1,4,2,1,8,512]{5,4,3,2,1,0:T(8,128)(2,1)S(1)}, bf16[1,4,2,1,8,512]{5,4,3,2,1,0:T(8,128)(2,1)S(1)}, u32[]{:S(2)}, u32[]{:S(2)}) %collective-permute-start.8) | collective-permute-done | bytes 65568 | tf_op jit(solution)/shard_map/ppermute | solution.py:309
  56.6 1.8 %collective-permute-done.9 = bf16[1,4,2,1,8,512]{5,4,3,2,1,0:T(8,128)(2,1)S(1)} collective-permute-done((bf16[1,4,2,1,8,512]{5,4,3,2,1,0:T(8,128)(2,1)S(1)}, bf16[1,4,2,1,8,512]{5,4,3,2,1,0:T(8,128)(2,1)S(1)}, u32[]{:S(2)}, u32[]{:S(2)}) %collective-permute-start.9) | collective-permute-done | bytes 65568 | tf_op jit(solution)/shard_map/ppermute | solution.py:309
  58.5 2.1 %collective-permute-start.12 = (bf16[4,1,2,1,8,512]{5,4,3,2,1,0:T(8,128)(2,1)S(1)}, bf16[4,1,2,1,8,512]{5,4,3,2,1,0:T(8,128)(2,1)S(1)}, u32[]{:S(2)}, u32[]{:S(2)}) collective-permute-start(bf16[4,1,2,1,8,512]{5,4,3,2,1,0:T(8,128)(2,1)S(1)} %get-tuple-element.42), channel_id=1, source_target_pairs={{0,6},{1,7},{2,4},{3,5},{4,2},{5,3},{6,0},{7,1},{8,14},{9,15},{10,... | collective-permute-start | bytes 196616 | tf_op jit(solution)/shard_map/ppermute | solution.py:309
  60.6 1.2 %collective-permute-start.11 = (bf16[4,1,2,1,8,512]{5,4,3,2,1,0:T(8,128)(2,1)S(1)}, bf16[4,1,2,1,8,512]{5,4,3,2,1,0:T(8,128)(2,1)S(1)}, u32[]{:S(2)}, u32[]{:S(2)}) collective-permute-start(bf16[4,1,2,1,8,512]{5,4,3,2,1,0:T(8,128)(2,1)S(1)} %get-tuple-element.43), channel_id=1, source_target_pairs={{0,4},{1,5},{2,6},{3,7},{4,0},{5,1},{6,2},{7,3},{8,12},{9,13},{10,... | collective-permute-start | bytes 196616 | tf_op jit(solution)/shard_map/ppermute | solution.py:309
  61.7 1.2 %collective-permute-start.10 = (bf16[4,1,2,1,8,512]{5,4,3,2,1,0:T(8,128)(2,1)S(1)}, bf16[4,1,2,1,8,512]{5,4,3,2,1,0:T(8,128)(2,1)S(1)}, u32[]{:S(2)}, u32[]{:S(2)}) collective-permute-start(bf16[4,1,2,1,8,512]{5,4,3,2,1,0:T(8,128)(2,1)S(1)} %get-tuple-element.44), channel_id=1, source_target_pairs={{0,2},{1,3},{2,0},{3,1},{4,6},{5,7},{6,4},{7,5},{8,10},{9,11},{10,... | collective-permute-start | bytes 196616 | tf_op jit(solution)/shard_map/ppermute | solution.py:309
  62.9 3.0 %all-to-all-done.rows_ref = bf16[32,3,8,1024]{3,2,1,0:T(8,128)(2,1)S(1)} async-done(((bf16[32,3,8,1024]{3,2,1,0:T(8,128)(2,1)}), bf16[32,3,8,1024]{3,2,1,0:T(8,128)(2,1)S(1)}, u32[]{:S(2)}, u32[]{:S(2)}) %all-to-all-start) | async-done | bytes 1572896 | tf_op jit(solution)/shard_map/all_to_all | solution.py:257
  66.0 7.1 %time.3.refs_0_ = bf16[32,3,8,512]{3,2,1,0:T(8,128)(2,1)} custom-call(bf16[32,3,8,1024]{3,2,1,0:T(8,128)(2,1)S(1)} %all-to-all-done.rows_ref, bf16[1024,1536]{1,0:T(8,128)(2,1)} %project_ref.3, bf16[8,1,8,512]{3,2,1,0:T(8,128)(2,1)} %copy-done.3), custom_call_target="tpu_custom_call" | custom-call | flops 4026531840 | bytes 6291456 | tf_op jit(solution)/shard_map/time/pallas_call | solution.py:414
  73.1 2.9 %all-to-all-start.1 = ((bf16[32,3,8,512]{3,2,1,0:T(8,128)(2,1)}), bf16[32,3,8,512]{3,2,1,0:T(8,128)(2,1)S(1)}, u32[]{:S(2)}, u32[]{:S(2)}) async-start(bf16[32,3,8,512]{3,2,1,0:T(8,128)(2,1)} %after.3), calls=%async_computation.1 | async-start | bytes 1572864 | tf_op jit(solution)/shard_map/all_to_all | solution.py:257
  76.1 0.3 collective-permute-start.13
  76.4 1.1 %collective-permute-done.13 = bf16[4,4,1,1,8,512]{5,4,3,2,1,0:T(8,128)(2,1)S(1)} collective-permute-done((bf16[4,4,1,1,8,512]{5,4,3,2,1,0:T(8,128)(2,1)S(1)}, bf16[4,4,1,1,8,512]{5,4,3,2,1,0:T(8,128)(2,1)S(1)}, u32[]{:S(2)}, u32[]{:S(2)}) %collective-permute-start.13) | collective-permute-done | bytes 131104 | tf_op jit(solution)/shard_map/ppermute | solution.py:309
  77.6 1.1 %copy-done.2 = bf16[1,256,1024]{2,1,0:T(8,128)(2,1)S(1)} copy-done((bf16[1,256,1024]{2,1,0:T(8,128)(2,1)S(1)}, bf16[1,256,1024]{2,1,0:T(8,128)(2,1)}, u32[]{:S(2)}) %copy-start.2) | copy-done | bytes 524312
  78.7 1.3 %final.2.before_ref = bf16[4,256,1024]{2,1,0:T(8,128)(2,1)} custom-call(bf16[1,256,1024]{2,1,0:T(8,128)(2,1)S(1)} %copy-done.2, bf16[32,1,8,512]{3,2,1,0:T(8,128)(2,1)S(1)} %bitcast.16, bf16[512,1024]{1,0:T(8,128)(2,1)S(1)} %copy-done), custom_call_target="tpu_custom_call" | custom-call | flops 268435456 | bytes 2621440 | tf_op jit(solution)/shard_map/final/pallas_call | solution.py:438
  80.0 18.0 %all-to-all-done.1.context_ref = bf16[32,3,8,512]{3,2,1,0:T(8,128)(2,1)S(1)} async-done(((bf16[32,3,8,512]{3,2,1,0:T(8,128)(2,1)}), bf16[32,3,8,512]{3,2,1,0:T(8,128)(2,1)S(1)}, u32[]{:S(2)}, u32[]{:S(2)}) %all-to-all-start.1) | async-done | bytes 786464 | tf_op jit(solution)/shard_map/all_to_all | solution.py:257
  98.0 1.8 %final.3 = bf16[4,256,1024]{2,1,0:T(8,128)(2,1)} custom-call(bf16[3,256,1024]{2,1,0:T(8,128)(2,1)S(1)} %copy-done.1, bf16[32,3,8,512]{3,2,1,0:T(8,128)(2,1)S(1)} %all-to-all-done.1.context_ref, bf16[512,1024]{1,0:T(8,128)(2,1)S(1)} %copy-done, bf16[4,256,1024]{2,1,0:T(8,128)(2,1)} %final.2.before_ref), custom_call_target="tpu_custom_call", output_to_operand_aliasing={{}: (3, {})} | custom-call | flops 805306368 | bytes 5767168 | tf_op jit(solution)/shard_map/final/pallas_call | solution.py:459
  (26 shorter events, 0.4 us)
Async XLA Ops:
  4.5 14.8 %collective-permute-start = (bf16[1,2,4,1,8,1024]{5,4,3,2,1,0:T(8,128)(2,1)S(1)}, bf16[1,2,4,1,8,1024]{5,4,3,2,1,0:T(8,128)(2,1)S(1)}, u32[]{:S(2)}, u32[]{:S(2)}) collective-permute-start(bf16[1,2,4,1,8,1024]{5,4,3,2,1,0:T(8,128)(2,1)S(1)} %bitcast.22), channel_id=1, source_target_pairs={{0,2},{1,3},{2,0},{3,1},{4,6},{5,7},{6,4},{7,5},{8,10},{9,11},{10,... | collective-permute-start | bytes 393224 | tf_op jit(solution)/shard_map/ppermute | solution.py:309
  7.6 12.9 %collective-permute-start.1 = (bf16[1,2,4,1,8,1024]{5,4,3,2,1,0:T(8,128)(2,1)S(1)}, bf16[1,2,4,1,8,1024]{5,4,3,2,1,0:T(8,128)(2,1)S(1)}, u32[]{:S(2)}, u32[]{:S(2)}) collective-permute-start(bf16[1,2,4,1,8,1024]{5,4,3,2,1,0:T(8,128)(2,1)S(1)} %bitcast.21), channel_id=1, source_target_pairs={{0,4},{1,5},{2,6},{3,7},{4,0},{5,1},{6,2},{7,3},{8,12},{9,13},{10,... | collective-permute-start | bytes 393224 | tf_op jit(solution)/shard_map/ppermute | solution.py:309
  10.2 10.3 %collective-permute-start.2 = (bf16[1,2,4,1,8,1024]{5,4,3,2,1,0:T(8,128)(2,1)S(1)}, bf16[1,2,4,1,8,1024]{5,4,3,2,1,0:T(8,128)(2,1)S(1)}, u32[]{:S(2)}, u32[]{:S(2)}) collective-permute-start(bf16[1,2,4,1,8,1024]{5,4,3,2,1,0:T(8,128)(2,1)S(1)} %bitcast.20), channel_id=1, source_target_pairs={{0,6},{1,7},{2,4},{3,5},{4,2},{5,3},{6,0},{7,1},{8,14},{9,15},{10,... | collective-permute-start | bytes 393224 | tf_op jit(solution)/shard_map/ppermute | solution.py:309
  20.5 45.5 %all-to-all-start = ((bf16[32,3,8,1024]{3,2,1,0:T(8,128)(2,1)}), bf16[32,3,8,1024]{3,2,1,0:T(8,128)(2,1)S(1)}, u32[]{:S(2)}, u32[]{:S(2)}) async-start(bf16[32,3,8,1024]{3,2,1,0:T(8,128)(2,1)} %after.2), calls=%async_computation | async-start | bytes 3145728 | tf_op jit(solution)/shard_map/all_to_all | solution.py:257
  25.9 1.6 %collective-permute-start.3 = (bf16[4,1,4,1,8,1024]{5,4,3,2,1,0:T(8,128)(2,1)S(1)}, bf16[4,1,4,1,8,1024]{5,4,3,2,1,0:T(8,128)(2,1)S(1)}, u32[]{:S(2)}, u32[]{:S(2)}) collective-permute-start(bf16[4,1,4,1,8,1024]{5,4,3,2,1,0:T(8,128)(2,1)S(1)} %get-tuple-element.38), channel_id=1, source_target_pairs={{0,8},{1,9},{2,10},{3,11},{4,12},{5,13},{6,14},{7,15},{8,0},{9,1},... | collective-permute-start | bytes 786440 | tf_op jit(solution)/shard_map/ppermute | solution.py:309
  27.5 22.1 %collective-permute-start.4 = (bf16[4,2,1,1,8,1024]{5,4,3,2,1,0:T(8,128)(2,1)S(1)}, bf16[4,2,1,1,8,1024]{5,4,3,2,1,0:T(8,128)(2,1)S(1)}, u32[]{:S(2)}, u32[]{:S(2)}) collective-permute-start(bf16[4,2,1,1,8,1024]{5,4,3,2,1,0:T(8,128)(2,1)S(1)} %get-tuple-element.34), channel_id=1, source_target_pairs={{0,16},{1,17},{2,18},{3,19},{4,20},{5,21},{6,22},{7,23},{8,24},{9,... | collective-permute-start | bytes 393224 | tf_op jit(solution)/shard_map/ppermute | solution.py:309
  29.4 20.2 %collective-permute-start.6 = (bf16[4,2,1,1,8,1024]{5,4,3,2,1,0:T(8,128)(2,1)S(1)}, bf16[4,2,1,1,8,1024]{5,4,3,2,1,0:T(8,128)(2,1)S(1)}, u32[]{:S(2)}, u32[]{:S(2)}) collective-permute-start(bf16[4,2,1,1,8,1024]{5,4,3,2,1,0:T(8,128)(2,1)S(1)} %get-tuple-element.35), channel_id=1, source_target_pairs={{0,17},{1,16},{2,19},{3,18},{4,21},{5,20},{6,23},{7,22},{8,25},{9,... | collective-permute-start | bytes 393224 | tf_op jit(solution)/shard_map/ppermute | solution.py:309
  30.8 18.9 %collective-permute-start.5 = (bf16[4,2,1,1,8,1024]{5,4,3,2,1,0:T(8,128)(2,1)S(1)}, bf16[4,2,1,1,8,1024]{5,4,3,2,1,0:T(8,128)(2,1)S(1)}, u32[]{:S(2)}, u32[]{:S(2)}) collective-permute-start(bf16[4,2,1,1,8,1024]{5,4,3,2,1,0:T(8,128)(2,1)S(1)} %get-tuple-element.36), channel_id=1, source_target_pairs={{0,1},{1,0},{2,3},{3,2},{4,5},{5,4},{6,7},{7,6},{8,9},{9,8},{10,11... | collective-permute-start | bytes 393224 | tf_op jit(solution)/shard_map/ppermute | solution.py:309
  51.6 14.3 %copy-start.3 = (bf16[8,1,8,512]{3,2,1,0:T(8,128)(2,1)}, bf16[8,1,8,512]{3,2,1,0:T(8,128)(2,1)S(1)}, u32[]{:S(2)}) copy-start(bf16[8,1,8,512]{3,2,1,0:T(8,128)(2,1)S(1)} %get-tuple-element.28.before_ref) | copy-start | bytes 196612
  51.7 5.0 %collective-permute-start.8 = (bf16[1,4,2,1,8,512]{5,4,3,2,1,0:T(8,128)(2,1)S(1)}, bf16[1,4,2,1,8,512]{5,4,3,2,1,0:T(8,128)(2,1)S(1)}, u32[]{:S(2)}, u32[]{:S(2)}) collective-permute-start(bf16[1,4,2,1,8,512]{5,4,3,2,1,0:T(8,128)(2,1)S(1)} %bitcast.25), channel_id=1, source_target_pairs={{0,1},{1,0},{2,3},{3,2},{4,5},{5,4},{6,7},{7,6},{8,9},{9,8},{10,11... | collective-permute-start | bytes 196616 | tf_op jit(solution)/shard_map/ppermute | solution.py:309
  51.7 4.9 %collective-permute-start.7 = (bf16[1,4,2,1,8,512]{5,4,3,2,1,0:T(8,128)(2,1)S(1)}, bf16[1,4,2,1,8,512]{5,4,3,2,1,0:T(8,128)(2,1)S(1)}, u32[]{:S(2)}, u32[]{:S(2)}) collective-permute-start(bf16[1,4,2,1,8,512]{5,4,3,2,1,0:T(8,128)(2,1)S(1)} %bitcast.24), channel_id=1, source_target_pairs={{0,16},{1,17},{2,18},{3,19},{4,20},{5,21},{6,22},{7,23},{8,24},{9,... | collective-permute-start | bytes 196616 | tf_op jit(solution)/shard_map/ppermute | solution.py:309
  53.3 5.2 %collective-permute-start.9 = (bf16[1,4,2,1,8,512]{5,4,3,2,1,0:T(8,128)(2,1)S(1)}, bf16[1,4,2,1,8,512]{5,4,3,2,1,0:T(8,128)(2,1)S(1)}, u32[]{:S(2)}, u32[]{:S(2)}) collective-permute-start(bf16[1,4,2,1,8,512]{5,4,3,2,1,0:T(8,128)(2,1)S(1)} %bitcast.23), channel_id=1, source_target_pairs={{0,17},{1,16},{2,19},{3,18},{4,21},{5,20},{6,23},{7,22},{8,25},{9,... | collective-permute-start | bytes 196616 | tf_op jit(solution)/shard_map/ppermute | solution.py:309
  58.5 14.6 %collective-permute-start.12 = (bf16[4,1,2,1,8,512]{5,4,3,2,1,0:T(8,128)(2,1)S(1)}, bf16[4,1,2,1,8,512]{5,4,3,2,1,0:T(8,128)(2,1)S(1)}, u32[]{:S(2)}, u32[]{:S(2)}) collective-permute-start(bf16[4,1,2,1,8,512]{5,4,3,2,1,0:T(8,128)(2,1)S(1)} %get-tuple-element.42), channel_id=1, source_target_pairs={{0,6},{1,7},{2,4},{3,5},{4,2},{5,3},{6,0},{7,1},{8,14},{9,15},{10,... | collective-permute-start | bytes 196616 | tf_op jit(solution)/shard_map/ppermute | solution.py:309
  60.6 12.5 %collective-permute-start.11 = (bf16[4,1,2,1,8,512]{5,4,3,2,1,0:T(8,128)(2,1)S(1)}, bf16[4,1,2,1,8,512]{5,4,3,2,1,0:T(8,128)(2,1)S(1)}, u32[]{:S(2)}, u32[]{:S(2)}) collective-permute-start(bf16[4,1,2,1,8,512]{5,4,3,2,1,0:T(8,128)(2,1)S(1)} %get-tuple-element.43), channel_id=1, source_target_pairs={{0,4},{1,5},{2,6},{3,7},{4,0},{5,1},{6,2},{7,3},{8,12},{9,13},{10,... | collective-permute-start | bytes 196616 | tf_op jit(solution)/shard_map/ppermute | solution.py:309
  61.7 11.4 %collective-permute-start.10 = (bf16[4,1,2,1,8,512]{5,4,3,2,1,0:T(8,128)(2,1)S(1)}, bf16[4,1,2,1,8,512]{5,4,3,2,1,0:T(8,128)(2,1)S(1)}, u32[]{:S(2)}, u32[]{:S(2)}) collective-permute-start(bf16[4,1,2,1,8,512]{5,4,3,2,1,0:T(8,128)(2,1)S(1)} %get-tuple-element.44), channel_id=1, source_target_pairs={{0,2},{1,3},{2,0},{3,1},{4,6},{5,7},{6,4},{7,5},{8,10},{9,11},{10,... | collective-permute-start | bytes 196616 | tf_op jit(solution)/shard_map/ppermute | solution.py:309
  73.1 4.5 %copy-start = (bf16[512,1024]{1,0:T(8,128)(2,1)S(1)}, bf16[512,1024]{1,0:T(8,128)(2,1)}, u32[]{:S(2)}) copy-start(bf16[512,1024]{1,0:T(8,128)(2,1)} %output_ref.5) | copy-start | bytes 3145732
  73.1 24.9 %all-to-all-start.1 = ((bf16[32,3,8,512]{3,2,1,0:T(8,128)(2,1)}), bf16[32,3,8,512]{3,2,1,0:T(8,128)(2,1)S(1)}, u32[]{:S(2)}, u32[]{:S(2)}) async-start(bf16[32,3,8,512]{3,2,1,0:T(8,128)(2,1)} %after.3), calls=%async_computation.1 | async-start | bytes 1572864 | tf_op jit(solution)/shard_map/all_to_all | solution.py:257
  76.1 1.4 %collective-permute-start.13 = (bf16[4,4,1,1,8,512]{5,4,3,2,1,0:T(8,128)(2,1)S(1)}, bf16[4,4,1,1,8,512]{5,4,3,2,1,0:T(8,128)(2,1)S(1)}, u32[]{:S(2)}, u32[]{:S(2)}) collective-permute-start(bf16[4,4,1,1,8,512]{5,4,3,2,1,0:T(8,128)(2,1)S(1)} %get-tuple-element.40), channel_id=1, source_target_pairs={{0,8},{1,9},{2,10},{3,11},{4,12},{5,13},{6,14},{7,15},{8,0},{9,1},... | collective-permute-start | bytes 393224 | tf_op jit(solution)/shard_map/ppermute | solution.py:309
  77.5 20.5 %copy-start.1 = (bf16[3,256,1024]{2,1,0:T(8,128)(2,1)S(1)}, bf16[3,256,1024]{2,1,0:T(8,128)(2,1)}, u32[]{:S(2)}) copy-start(bf16[3,256,1024]{2,1,0:T(8,128)(2,1)} %get-tuple-element.22.mixed_ref) | copy-start | bytes 4718596
  77.5 1.2 %copy-start.2 = (bf16[1,256,1024]{2,1,0:T(8,128)(2,1)S(1)}, bf16[1,256,1024]{2,1,0:T(8,128)(2,1)}, u32[]{:S(2)}) copy-start(bf16[1,256,1024]{2,1,0:T(8,128)(2,1)} %get-tuple-element.32.mixed_ref) | copy-start | bytes 1572868
